TPU v7x, 128 devices: a whole 4x4x4 slice. The times are simulated.
128 devices in a mesh: rows: 16 (over x, z_hi, core), cols: 8 (over z_lo, y).
Axes of the slice: x: 4, y: 4, z: 4 (z_hi: 2, z_lo: 2; z = z_hi * 2 + z_lo), core: 2. Of those that a mesh axis runs over, the one named last changes fastest.
Arguments:
- stem_strips: bfloat16 [768, 512, 256], P(('rows', 'cols')), may hold values from -6 to 6
- norm_scale: float32 [256], replicated, may hold values from 0.1 to 1.9
- norm_shift: float32 [256], replicated, may hold values from -3 to 3
- expand_weight: bfloat16 [256, 1024], replicated, may hold values from -0.375 to 0.375
- depth_weight: float32 [9, 1024], replicated, may hold values from -2 to 2
- project_weight: bfloat16 [1024, 256], replicated, may hold values from -0.1875 to 0.1875
- block_gain: float32 [256], replicated, may hold values from 0.1 to 1.9
- block_inputs: bfloat16 [256, 768], replicated, may hold values from -0.375 to 0.375
- block_output: bfloat16 [256, 256], replicated, may hold values from -0.375 to 0.375
- block_bias: float32 [8, 64, 64], replicated, may hold values from -4 to 300, as said below
- first_gain: float32 [256], replicated, may hold values from 0.1 to 1.9
- first_up: bfloat16 [256, 1024], replicated, may hold values from -0.375 to 0.375
- first_down: bfloat16 [1024, 256], replicated, may hold values from -0.1875 to 0.1875
- grid_gain: float32 [256], replicated, may hold values from 0.1 to 1.9
- grid_inputs: bfloat16 [256, 768], replicated, may hold values from -0.375 to 0.375
- grid_output: bfloat16 [256, 256], replicated, may hold values from -0.375 to 0.375
- grid_bias: float32 [8, 64, 64], replicated, may hold values from -4 to 300, as said below
- second_gain: float32 [256], replicated, may hold values from 0.1 to 1.9
- second_up: bfloat16 [256, 1024], replicated, may hold values from -0.375 to 0.375
- second_down: bfloat16 [1024, 256], replicated, may hold values from -0.1875 to 0.1875
Outputs:
- block_out: bfloat16 [768, 512, 256], P('rows', 'cols')
Inputs may be any that keep to these rules, and one draw needn't show every extreme that they name: `block_bias`: entries of the position bias table. `grid_bias`: entries of the position bias table.
All inputs are finite; a program needn't handle non-finite values.
Results may differ from a plain program's by a relative error of at most 0.018.
Values may be sent and summed in bfloat16 or wider, within the bound.
No kernel may reach another device: no remote copies, remote signals or barrier semaphores. Data moves between devices by JAX's collectives and lax.ppermute only.
A program may use at most 128 MiB of HBM per device.

v0:
```python
import jax
import jax.numpy as jnp
from jax import lax
from jax.sharding import PartitionSpec as P

EPSILON = 1e-05


def extended(cells, sides, width):
    for axis, dim in sides:
        count = lax.axis_size(axis)
        ends = count - 1
        head = lax.slice_in_dim(cells, 0, width, axis=dim)
        tail = lax.slice_in_dim(cells, cells.shape[dim] - width, cells.shape[dim], axis=dim)
        cells = jnp.concatenate(
            [
                lax.ppermute(tail, axis, [(i, (i + 1) % count) for i in range(ends)]),
                cells,
                lax.ppermute(head, axis, [((i + 1) % count, i) for i in range(ends)]),
            ],
            axis=dim,
        )
    return cells


def layer_norm(values, norm_gain):
    values = values.astype(jnp.float32)
    center = values - jnp.mean(values, axis=-1, keepdims=True)
    spread = jnp.mean(center * center, axis=-1, keepdims=True)
    return (center * jax.lax.rsqrt(spread + EPSILON) * norm_gain).astype(jnp.bfloat16)


def attend(windows, norm_gain, in_weight, out_weight, pos_bias):
    count_win, places, channels = windows.shape
    head_count = pos_bias.shape[0]
    head_width = channels // head_count
    flat_in = windows.reshape(-1, channels)
    normed = layer_norm(flat_in, norm_gain)
    packed = jnp.dot(normed, in_weight, preferred_element_type=jnp.float32).astype(jnp.bfloat16)
    packed = packed.reshape(count_win, places, 3, head_count, head_width)
    scores = (
        jnp.einsum(
            "wqhd,wkhd->whqk", packed[:, :, 0], packed[:, :, 1], preferred_element_type=jnp.float32
        )
        * head_width ** (-0.5)
        + pos_bias
    )
    scores = scores - jnp.max(scores, axis=-1, keepdims=True)
    attention = jnp.exp(scores)
    attention = (attention / jnp.sum(attention, axis=-1, keepdims=True)).astype(jnp.bfloat16)
    combined = jnp.einsum(
        "whqk,wkhd->wqhd", attention, packed[:, :, 2], preferred_element_type=jnp.float32
    ).astype(jnp.bfloat16)
    update = jnp.dot(combined.reshape(-1, channels), out_weight, preferred_element_type=jnp.float32)
    return (flat_in.astype(jnp.float32) + update).astype(jnp.bfloat16)


def feed_forward(tokens, norm_gain, up_weight, down_weight):
    normed = layer_norm(tokens, norm_gain)
    hidden = jax.nn.gelu(jnp.dot(normed, up_weight, preferred_element_type=jnp.float32)).astype(
        jnp.bfloat16
    )
    result = tokens.astype(jnp.float32) + jnp.dot(
        hidden, down_weight, preferred_element_type=jnp.float32
    )
    return result.astype(jnp.bfloat16)


def expand_pixels(normed, expand_weight):
    rows_here, cols_here, channels = normed.shape
    flat = jnp.dot(normed.reshape(-1, channels), expand_weight, preferred_element_type=jnp.float32)
    return jax.nn.gelu(flat).astype(jnp.bfloat16).reshape(rows_here, cols_here, -1)


def body(
    stem_strips,
    norm_scale,
    norm_shift,
    expand_weight,
    depth_weight,
    project_weight,
    block_gain,
    block_inputs,
    block_output,
    block_bias,
    first_gain,
    first_up,
    first_down,
    grid_gain,
    grid_inputs,
    grid_output,
    grid_bias,
    second_gain,
    second_up,
    second_down,
):
    tile_data = lax.all_to_all(stem_strips, "cols", split_axis=1, concat_axis=0, tiled=True)
    rows_here, cols_here, channels = tile_data.shape
    wide = expand_weight.shape[1]
    normed = (tile_data.astype(jnp.float32) * norm_scale + norm_shift).astype(jnp.bfloat16)
    expanded = expand_pixels(normed, expand_weight)
    padded = extended(expanded, (("rows", 0), ("cols", 1)), 1)
    running = jnp.zeros((rows_here, cols_here, wide), jnp.float32)
    for offset in range(9):
        shifted = padded[offset // 3 : offset // 3 + rows_here, offset % 3 : offset % 3 + cols_here]
        running = running + shifted.astype(jnp.float32) * depth_weight[offset]
    activated = jax.nn.gelu(running).astype(jnp.bfloat16)
    update = jnp.dot(
        activated.reshape(-1, wide), project_weight, preferred_element_type=jnp.float32
    )
    section1 = (tile_data.reshape(-1, channels).astype(jnp.float32) + update).astype(jnp.bfloat16)
    blocks = section1.reshape(rows_here // 8, 8, cols_here // 8, 8, channels).transpose(
        0, 2, 1, 3, 4
    )
    blocks = blocks.reshape(-1, 64, channels)
    section2 = attend(blocks, block_gain, block_inputs, block_output, block_bias)
    section3 = feed_forward(section2, first_gain, first_up, first_down)
    section3 = section3.reshape(rows_here // 8, cols_here // 8, 8, 8, channels).transpose(
        0, 2, 1, 3, 4
    )
    grid_rows = lax.axis_size("rows")
    grid_cols = lax.axis_size("cols")
    outgoing = section3.reshape(
        rows_here // grid_rows, grid_rows, cols_here // grid_cols, grid_cols, channels
    )
    outgoing = outgoing.transpose(1, 3, 0, 2, 4)
    flat_send = outgoing.reshape(
        grid_rows * grid_cols, rows_here // grid_rows, cols_here // grid_cols, channels
    )
    arrived = lax.all_to_all(
        flat_send, ("rows", "cols"), split_axis=0, concat_axis=0, tiled=True
    ).reshape(outgoing.shape)
    grids = arrived.transpose(0, 2, 1, 3, 4).reshape(8, rows_here // 8, 8, cols_here // 8, channels)
    grids = grids.transpose(1, 3, 0, 2, 4).reshape(-1, 64, channels)
    section4 = attend(grids, grid_gain, grid_inputs, grid_output, grid_bias)
    section5 = feed_forward(section4, second_gain, second_up, second_down)
    returning = section5.reshape(rows_here // 8, cols_here // 8, 8, 8, channels).transpose(
        2, 0, 3, 1, 4
    )
    returning = returning.reshape(
        grid_rows, rows_here // grid_rows, grid_cols, cols_here // grid_cols, channels
    )
    returning = returning.transpose(0, 2, 1, 3, 4)
    flat_back = returning.reshape(
        grid_rows * grid_cols, rows_here // grid_rows, cols_here // grid_cols, channels
    )
    landed = lax.all_to_all(
        flat_back, ("rows", "cols"), split_axis=0, concat_axis=0, tiled=True
    ).reshape(returning.shape)
    return landed.transpose(2, 0, 3, 1, 4).reshape(rows_here, cols_here, channels)


def solution(mesh):
    return jax.shard_map(
        body,
        mesh=mesh,
        in_specs=(
            P(("rows", "cols"), None, None),
            P(),
            P(),
            P(),
            P(),
            P(),
            P(),
            P(),
            P(),
            P(),
            P(),
            P(),
            P(),
            P(),
            P(),
            P(),
            P(),
            P(),
            P(),
            P(),
        ),
        out_specs=P("rows", "cols", None),
        check_vma=False,
    )
```

profile of v0, /device:TPU:0, one launch (start us, length us, event | category | flops | bytes accessed | tf_op | source)
XLA Modules:
  0.0 329.9 jit_solution(12011305476684857373)
XLA Ops:
  0.0 2.4 copy.83
  2.4 32.6 %all_to_all.19 = bf16[6,512,256]{2,0,1:T(8,128)(2,1)S(1)} all-to-all(bf16[6,512,256]{2,0,1:T(8,128)(2,1)S(1)} %copy.83), channel_id=1, replica_groups=mesh['rows'=16,'cols'=8] {'cols'}, dimensions={1} | all-to-all | bytes 3145728 | tf_op jit(solution)/shard_map/all_to_all | solution.py:97
  35.5 1.6 copy-done.4
  37.5 4.3 %fusion.9 = bf16[3072,1024]{1,0:T(8,128)(2,1)S(1)} fusion(bf16[3072,256]{1,0:T(8,128)(2,1)S(1)} %fusion.82, bf16[256,1024]{1,0:T(8,128)(2,1)S(1)} %copy-done), kind=kOutput, calls=%fused_computation.13 | convolution fusion | flops 1638924288 | bytes 8388608 | tf_op jit(solution)/shard_map/dot_general | solution.py:71
  44.6 5.7 %collective-permute-done.1 = bf16[1,64,1024]{2,1,0:T(8,128)(2,1)S(1)} collective-permute-done((bf16[1,64,1024]{2,1,0:T(8,128)(2,1)S(1)}, bf16[1,64,1024]{2,1,0:T(8,128)(2,1)S(1)}, u32[]{:S(2)}, u32[]{:S(2)}) %collective-permute-start.1) | collective-permute-done | bytes 131104 | tf_op jit(solution)/shard_map/ppermute | solution.py:19
  50.7 3.0 collective-permute-start.2
  55.4 1.6 collective-permute-done.2
  57.0 4.4 %collective-permute-done.3 = bf16[50,1,1024]{2,1,0:T(2,128)(2,1)S(1)} collective-permute-done((bf16[50,1,1024]{2,1,0:T(2,128)(2,1)S(1)}, bf16[50,1,1024]{2,1,0:T(2,128)(2,1)S(1)}, u32[]{:S(2)}, u32[]{:S(2)}) %collective-permute-start.3) | collective-permute-done | bytes 102432 | tf_op jit(solution)/shard_map/ppermute | solution.py:19
  61.4 7.6 %maximum_maximum_fusion = (bf16[50,65,1024]{2,1,0:T(8,128)(2,1)S(1)}, bf16[50,65,1024]{2,1,0:T(8,128)(2,1)S(1)}) fusion(bf16[1,64,1024]{2,1,0:T(8,128)(2,1)S(1)} %collective-permute-done.1, bf16[48,64,1024]{2,1,0:T(8,128)(2,1)} %bitcast.137, bf16[1,64,1024]{2,1,0:T(8,128)(2,1)S(1)} %collective-permute-done, ...), kind=kLoop, calls=%fused_computation.46 | loop fusion | flops 53248000 | bytes 20070400 | tf_op jit(solution)/shard_map/concatenate | solution.py:15
  69.0 24.4 %fusion.17 = bf16[48,64,1024]{2,1,0:T(8,128)(2,1)} fusion(bf16[48,64,1024]{2,1,0:T(8,128)(2,1)} %bitcast.138, bf16[50,65,1024]{2,1,0:T(8,128)(2,1)S(1)} %get-tuple-element.12, bf16[1,64,1024]{2,1,0:T(8,128)(2,1)S(1)} %collective-permute-done.1, bf16[50,65,1024]{2,1,0:T(8,128)(2,1)S(1)} %get-tuple-element.11, ...), kind=kLoop, calls=%fused_computation.21 | loop fusion | flops 116391936 | bytes 50630656 | tf_op jit(solution)/shard_map/convert_element_type | solution.py:107
  93.5 4.7 %fusion.54 = bf16[3072,256]{1,0:T(8,128)(2,1)S(1)} fusion(f32[3072,256]{1,0:T(8,128)S(1)} %bitcast.147, bf16[3072,1024]{1,0:T(8,128)(2,1)} %bitcast.154, bf16[1024,256]{1,0:T(8,128)(2,1)S(1)} %copy-done.19), kind=kOutput, calls=%fused_computation.71 | convolution fusion | flops 1612185600 | bytes 11534336 | tf_op jit(solution)/shard_map/dot_general | solution.py:108
  98.7 2.0 convert_bitcast_fusion
  101.9 4.0 %copy.85 = f32[6,8,8,8,256]{4,3,2,1,0:T(8,128)} copy(f32[6,8,8,8,256]{4,3,1,2,0:T(8,128)} %convert_bitcast_fusion) | data formatting | bytes 6291456 | tf_op jit(solution)/shard_map/convert_element_type | solution.py:55
  106.0 3.1 fusion.80
  109.1 3.5 %convolution_convert_fusion.1 = bf16[3072,768]{1,0:T(8,128)(2,1)} fusion(bf16[3072,256]{1,0:T(8,128)(2,1)S(1)} %fusion.80, bf16[256,768]{1,0:T(8,128)(2,1)S(1)} %copy-done.8), kind=kOutput, calls=%fused_computation.59 | convolution fusion | flops 1210318848 | bytes 6684672 | tf_op jit(solution)/shard_map/dot_general | solution.py:39
  112.7 6.6 %copy.88 = bf16[3072,768]{0,1:T(8,128)(2,1)} copy(bf16[3072,768]{1,0:T(8,128)(2,1)} %convolution_convert_fusion.1) | data formatting | bytes 9437184 | tf_op jit(solution)/shard_map/convert_element_type | solution.py:39
  119.3 12.3 %reshape.180 = bf16[48,64,3,8,32]{1,0,4,3,2:T(8,128)(2,1)} reshape(bf16[3072,768]{0,1:T(8,128)(2,1)} %copy.88) | data formatting | bytes 9437184 | tf_op jit(solution)/shard_map/reshape | solution.py:40
  131.6 6.1 %fusion.111 = (bf16[48,64,1,8,32]{1,0,4,3,2:T(8,128)(2,1)}, bf16[48,64,1,8,32]{1,0,4,3,2:T(8,128)(2,1)S(1)}, bf16[48,64,1,8,32]{1,0,4,3,2:T(8,128)(2,1)S(1)}) fusion(bf16[48,64,3,8,32]{1,0,4,3,2:T(8,128)(2,1)} %reshape.180), kind=kLoop, calls=%fused_computation.141 | loop fusion | bytes 9437184 | tf_op jit(solution)/shard_map/slice | solution.py:52
  137.7 2.3 fusion.74
  140.0 8.2 %fusion.113 = (f32[48,8,64]{2,1,0:T(8,128)S(1)}, f32[48,8,64,64]{2,3,1,0:T(8,128)}) fusion(f32[48,8,64,64]{2,3,1,0:T(8,128)S(1)} %fusion.74, f32[8,64,64]{1,2,0:T(8,128)S(1)} %copy.92), kind=kOutput, calls=%fused_computation.143 | output fusion | flops 9437247 | bytes 12812288 | tf_op jit(solution)/shard_map/sub | solution.py:48
  148.2 6.4 %convert_bitcast_fusion.2 = bf16[48,64,8,32]{1,3,2,0:T(8,128)(2,1)S(1)} fusion(f32[48,8,64,64]{2,3,1,0:T(8,128)} %get-tuple-element.27, f32[48,8,64]{2,1,0:T(8,128)S(1)} %get-tuple-element.26, bf16[48,64,1,8,32]{1,0,4,3,2:T(8,128)(2,1)S(1)} %copy-done.6), kind=kOutput, calls=%fused_computation.108 | convolution fusion | flops 104595456 | bytes 9535488 | tf_op jit(solution)/shard_map/whqk,wkhd->wqhd/dot_general | solution.py:51
  154.7 3.7 %copy.94 = bf16[48,64,8,32]{1,0,3,2:T(8,128)(2,1)} copy(bf16[48,64,8,32]{1,3,2,0:T(8,128)(2,1)S(1)} %convert_bitcast_fusion.2) | data formatting | bytes 3145728 | tf_op jit(solution)/shard_map/convert_element_type | solution.py:53
  158.4 5.0 %reshape.181 = bf16[3072,256]{0,1:T(8,128)(2,1)} reshape(bf16[48,64,8,32]{1,0,3,2:T(8,128)(2,1)} %copy.94) | data formatting | bytes 3145728 | tf_op jit(solution)/shard_map/reshape | solution.py:54
  163.4 3.4 %convert_reduce_fusion.1 = (f32[3072]{0:T(1024)S(1)}, bf16[3072,256]{1,0:T(8,128)(2,1)S(1)}) fusion(f32[3072,256]{1,0:T(8,128)} %bitcast.143, bf16[3072,256]{0,1:T(8,128)(2,1)} %reshape.181, bf16[256,256]{1,0:T(8,128)(2,1)S(1)} %copy-done.12), kind=kOutput, calls=%fused_computation.65 | convolution fusion | flops 405795840 | bytes 6434816 | tf_op jit(solution)/shard_map/dot_general | solution.py:54
  167.8 6.5 %fusion.57 = bf16[3072,256]{1,0:T(8,128)(2,1)} fusion(bf16[1024,256]{1,0:T(8,128)(2,1)S(1)} %copy-done.20, bf16[256,1024]{1,0:T(8,128)(2,1)S(1)} %copy-done.21, bf16[3072,256]{1,0:T(8,128)(2,1)S(1)} %get-tuple-element.29, f32[256]{0:T(256)S(1)} %copy-done.24, f32[3072]{0:T(1024)S(1)} %add_rsqrt_fusion.3, f32[3072]{0:T(1024)S(1)} %broadcast_multiply_fusion.3), kind=kOutput, calls=%fused_computation.74 | convolution fusion | flops 3255828480 | bytes 4219904 | tf_op jit(solution)/shard_map/dot_general | solution.py:63
  174.3 1.6 copy.95
  175.9 1.6 copy.96
  177.5 14.5 %all-to-all-start.1 = ((bf16[128,3,8,256]{3,2,1,0:T(8,128)(2,1)}), bf16[128,3,8,256]{3,2,1,0:T(8,128)(2,1)S(1)}, u32[]{:S(2)}, u32[]{:S(2)}) async-start(bf16[128,3,8,256]{3,2,1,0:T(8,128)(2,1)} %bitcast.29), calls=%async_computation.1 | async-start | bytes 3145728 | tf_op jit(solution)/shard_map/all_to_all | solution.py:130
  192.1 24.8 %all-to-all-done.1 = bf16[128,3,8,256]{3,2,1,0:T(8,128)(2,1)S(1)} async-done(((bf16[128,3,8,256]{3,2,1,0:T(8,128)(2,1)}), bf16[128,3,8,256]{3,2,1,0:T(8,128)(2,1)S(1)}, u32[]{:S(2)}, u32[]{:S(2)}) %all-to-all-start.1) | async-done | bytes 1572896 | tf_op jit(solution)/shard_map/all_to_all | solution.py:130
  217.4 1.6 copy-done.3
  219.0 2.6 copy.98
  221.6 2.4 reduce_sum.95
  224.3 2.8 multiply_reduce_fusion
  227.6 3.1 fusion.77
  230.7 3.5 %convolution_convert_fusion = bf16[3072,768]{1,0:T(8,128)(2,1)} fusion(bf16[3072,256]{1,0:T(8,128)(2,1)S(1)} %fusion.77, bf16[256,768]{1,0:T(8,128)(2,1)S(1)} %copy-done.9), kind=kOutput, calls=%fused_computation.58 | convolution fusion | flops 1210318848 | bytes 6684672 | tf_op jit(solution)/shard_map/dot_general | solution.py:39
  234.2 6.6 %copy.104 = bf16[3072,768]{0,1:T(8,128)(2,1)} copy(bf16[3072,768]{1,0:T(8,128)(2,1)} %convolution_convert_fusion) | data formatting | bytes 9437184 | tf_op jit(solution)/shard_map/convert_element_type | solution.py:39
  240.8 12.3 %reshape.186 = bf16[48,64,3,8,32]{1,0,4,3,2:T(8,128)(2,1)} reshape(bf16[3072,768]{0,1:T(8,128)(2,1)} %copy.104) | data formatting | bytes 9437184 | tf_op jit(solution)/shard_map/reshape | solution.py:40
  253.2 5.7 %fusion.110 = (bf16[48,64,1,8,32]{1,0,4,3,2:T(8,128)(2,1)}, bf16[48,64,1,8,32]{1,0,4,3,2:T(8,128)(2,1)S(1)}, bf16[48,64,1,8,32]{1,0,4,3,2:T(8,128)(2,1)S(1)}) fusion(bf16[48,64,3,8,32]{1,0,4,3,2:T(8,128)(2,1)} %reshape.186), kind=kLoop, calls=%fused_computation.140 | loop fusion | bytes 9437184 | tf_op jit(solution)/shard_map/slice | solution.py:52
  258.9 2.3 fusion.73
  261.2 8.4 %fusion.114 = (f32[48,8,64]{2,1,0:T(8,128)S(1)}, f32[48,8,64,64]{2,3,1,0:T(8,128)}) fusion(f32[48,8,64,64]{2,3,1,0:T(8,128)S(1)} %fusion.73, f32[8,64,64]{1,2,0:T(8,128)S(1)} %copy.108), kind=kOutput, calls=%fused_computation.144 | output fusion | flops 9437247 | bytes 12812288 | tf_op jit(solution)/shard_map/sub | solution.py:48
  269.6 6.4 %convert_bitcast_fusion.1 = bf16[48,64,8,32]{1,3,2,0:T(8,128)(2,1)S(1)} fusion(f32[48,8,64,64]{2,3,1,0:T(8,128)} %get-tuple-element.31, f32[48,8,64]{2,1,0:T(8,128)S(1)} %get-tuple-element.30, bf16[48,64,1,8,32]{1,0,4,3,2:T(8,128)(2,1)S(1)} %copy-done.7), kind=kOutput, calls=%fused_computation.106 | convolution fusion | flops 104595456 | bytes 9535488 | tf_op jit(solution)/shard_map/whqk,wkhd->wqhd/dot_general | solution.py:51
  276.1 3.7 %copy.110 = bf16[48,64,8,32]{1,0,3,2:T(8,128)(2,1)} copy(bf16[48,64,8,32]{1,3,2,0:T(8,128)(2,1)S(1)} %convert_bitcast_fusion.1) | data formatting | bytes 3145728 | tf_op jit(solution)/shard_map/convert_element_type | solution.py:53
  279.7 5.0 %reshape.187 = bf16[3072,256]{0,1:T(8,128)(2,1)} reshape(bf16[48,64,8,32]{1,0,3,2:T(8,128)(2,1)} %copy.110) | data formatting | bytes 3145728 | tf_op jit(solution)/shard_map/reshape | solution.py:54
  284.8 3.4 %convert_reduce_fusion = (f32[3072]{0:T(1024)S(1)}, bf16[3072,256]{1,0:T(8,128)(2,1)S(1)}) fusion(f32[3072,256]{1,0:T(8,128)} %bitcast.142, bf16[3072,256]{0,1:T(8,128)(2,1)} %reshape.187, bf16[256,256]{1,0:T(8,128)(2,1)S(1)} %copy-done.13), kind=kOutput, calls=%fused_computation.62 | convolution fusion | flops 405795840 | bytes 6434816 | tf_op jit(solution)/shard_map/dot_general | solution.py:54
  289.2 6.6 %fusion.60 = bf16[3072,256]{1,0:T(8,128)(2,1)} fusion(bf16[1024,256]{1,0:T(8,128)(2,1)S(1)} %copy-done.22, bf16[256,1024]{1,0:T(8,128)(2,1)S(1)} %copy-done.23, bf16[3072,256]{1,0:T(8,128)(2,1)S(1)} %get-tuple-element.33, f32[256]{0:T(256)S(1)} %copy-done.25, f32[3072]{0:T(1024)S(1)} %add_rsqrt_fusion.2, f32[3072]{0:T(1024)S(1)} %broadcast_multiply_fusion.2), kind=kOutput, calls=%fused_computation.75 | convolution fusion | flops 3255828480 | bytes 4219904 | tf_op jit(solution)/shard_map/dot_general | solution.py:63
  295.7 3.1 copy.111
  299.0 29.0 %all_to_all.20 = bf16[128,3,8,256]{3,2,1,0:T(8,128)(2,1)S(1)} all-to-all(bf16[128,3,8,256]{3,2,1,0:T(8,128)(2,1)S(1)} %bitcast.151), channel_id=1, replica_groups=mesh['rows'=16,'cols'=8] {'rows','cols'}, dimensions={0} | all-to-all | bytes 3145728 | tf_op jit(solution)/shard_map/all_to_all | solution.py:147
  328.0 1.6 copy.113
  (86 shorter events, 10.6 us)
Async XLA Ops:
  0.0 37.5 %copy-start = (bf16[256,1024]{1,0:T(8,128)(2,1)S(1)}, bf16[256,1024]{1,0:T(8,128)(2,1)}, u32[]{:S(2)}) copy-start(bf16[256,1024]{1,0:T(8,128)(2,1)} %param.23) | copy-start | bytes 1572868
  0.0 37.1 %copy-start.16 = (f32[256]{0:T(256)S(1)}, f32[256]{0:T(256)}, u32[]{:S(2)}) copy-start(f32[256]{0:T(256)} %param.21) | copy-start | bytes 3076
  0.0 37.1 %copy-start.15 = (f32[256]{0:T(256)S(1)}, f32[256]{0:T(256)}, u32[]{:S(2)}) copy-start(f32[256]{0:T(256)} %param.22) | copy-start | bytes 3076
  35.5 1.6 copy-start.4
  41.8 8.6 %copy-start.2 = (bf16[3072,1024]{1,0:T(8,128)(2,1)}, bf16[3072,1024]{1,0:T(8,128)(2,1)S(1)}, u32[]{:S(2)}) copy-start(bf16[3072,1024]{1,0:T(8,128)(2,1)S(1)} %fusion.9) | copy-start | bytes 18874372
  41.8 13.4 %copy-start.14 = (f32[9,1024]{1,0:T(8,128)S(1)}, f32[9,1024]{1,0:T(8,128)}, u32[]{:S(2)}) copy-start(f32[9,1024]{1,0:T(8,128)} %param.24) | copy-start | bytes 110596
  41.8 13.4 %copy-start.10 = (f32[8,64,64]{2,1,0:T(8,128)S(1)}, f32[8,64,64]{2,1,0:T(8,128)}, u32[]{:S(2)}) copy-start(f32[8,64,64]{2,1,0:T(8,128)} %param.29) | copy-start | bytes 393220
  41.8 2.7 collective-permute-start
  43.3 7.1 %collective-permute-start.1 = (bf16[1,64,1024]{2,1,0:T(8,128)(2,1)S(1)}, bf16[1,64,1024]{2,1,0:T(8,128)(2,1)S(1)}, u32[]{:S(2)}, u32[]{:S(2)}) collective-permute-start(bf16[1,64,1024]{2,1,0:T(8,128)(2,1)S(1)} %get-tuple-element.16), channel_id=1, source_target_pairs={{8,0},{16,8},{24,16},{32,24},{40,32},{48,40},{56,48},{64,56},{72,6... | collective-permute-start | bytes 393224 | tf_op jit(solution)/shard_map/ppermute | solution.py:19
  50.7 6.3 %collective-permute-start.2 = (bf16[50,1,1024]{2,1,0:T(2,128)(2,1)S(1)}, bf16[50,1,1024]{2,1,0:T(2,128)(2,1)S(1)}, u32[]{:S(2)}, u32[]{:S(2)}) collective-permute-start(bf16[50,1,1024]{2,1,0:T(2,128)(2,1)S(1)} %get-tuple-element.13), channel_id=1, source_target_pairs={{0,1},{1,2},{2,3},{3,4},{4,5},{5,6},{6,7},{8,9},{9,10},{10,11},{11... | collective-permute-start | bytes 307208 | tf_op jit(solution)/shard_map/ppermute | solution.py:17
  53.7 7.7 %collective-permute-start.3 = (bf16[50,1,1024]{2,1,0:T(2,128)(2,1)S(1)}, bf16[50,1,1024]{2,1,0:T(2,128)(2,1)S(1)}, u32[]{:S(2)}, u32[]{:S(2)}) collective-permute-start(bf16[50,1,1024]{2,1,0:T(2,128)(2,1)S(1)} %get-tuple-element.14), channel_id=1, source_target_pairs={{1,0},{2,1},{3,2},{4,3},{5,4},{6,5},{7,6},{9,8},{10,9},{11,10},{12... | collective-permute-start | bytes 307208 | tf_op jit(solution)/shard_map/ppermute | solution.py:19
  69.0 24.5 %copy-start.5 = (f32[6,8,64,256]{3,2,0,1:T(8,128)S(1)}, f32[6,8,64,256]{3,2,0,1:T(8,128)}, u32[]{:S(2)}) copy-start(f32[6,8,64,256]{3,2,0,1:T(8,128)} %copy-done.4) | copy-start | bytes 9437188
  69.0 24.5 %copy-start.19 = (bf16[1024,256]{1,0:T(8,128)(2,1)S(1)}, bf16[1024,256]{1,0:T(8,128)(2,1)}, u32[]{:S(2)}) copy-start(bf16[1024,256]{1,0:T(8,128)(2,1)} %param.25) | copy-start | bytes 1572868
  100.7 5.3 %copy-start.17 = (f32[256]{0:T(256)S(1)}, f32[256]{0:T(256)}, u32[]{:S(2)}) copy-start(f32[256]{0:T(256)} %param.26) | copy-start | bytes 3076
  101.7 7.5 %copy-start.8 = (bf16[256,768]{1,0:T(8,128)(2,1)S(1)}, bf16[256,768]{1,0:T(8,128)(2,1)}, u32[]{:S(2)}) copy-start(bf16[256,768]{1,0:T(8,128)(2,1)} %param.27) | copy-start | bytes 1179652
  140.0 8.2 %copy-start.6 = (bf16[48,64,1,8,32]{1,0,4,3,2:T(8,128)(2,1)S(1)}, bf16[48,64,1,8,32]{1,0,4,3,2:T(8,128)(2,1)}, u32[]{:S(2)}) copy-start(bf16[48,64,1,8,32]{1,0,4,3,2:T(8,128)(2,1)} %get-tuple-element.8) | copy-start | bytes 4718596
  154.7 8.7 %copy-start.12 = (bf16[256,256]{1,0:T(8,128)(2,1)S(1)}, bf16[256,256]{1,0:T(8,128)(2,1)}, u32[]{:S(2)}) copy-start(bf16[256,256]{1,0:T(8,128)(2,1)} %param.28) | copy-start | bytes 393220
  158.3 9.4 %copy-start.20 = (bf16[1024,256]{1,0:T(8,128)(2,1)S(1)}, bf16[1024,256]{1,0:T(8,128)(2,1)}, u32[]{:S(2)}) copy-start(bf16[1024,256]{1,0:T(8,128)(2,1)} %param.32) | copy-start | bytes 1572868
  158.4 9.4 %copy-start.21 = (bf16[256,1024]{1,0:T(8,128)(2,1)S(1)}, bf16[256,1024]{1,0:T(8,128)(2,1)}, u32[]{:S(2)}) copy-start(bf16[256,1024]{1,0:T(8,128)(2,1)} %param.31) | copy-start | bytes 1572868
  158.4 9.4 %copy-start.24 = (f32[256]{0:T(256)S(1)}, f32[256]{0:T(256)}, u32[]{:S(2)}) copy-start(f32[256]{0:T(256)} %param.30) | copy-start | bytes 3076
  174.3 17.7 %copy-start.11 = (f32[8,64,64]{2,1,0:T(8,128)S(1)}, f32[8,64,64]{2,1,0:T(8,128)}, u32[]{:S(2)}) copy-start(f32[8,64,64]{2,1,0:T(8,128)} %param.36) | copy-start | bytes 393220
  177.5 39.5 %all-to-all-start.1 = ((bf16[128,3,8,256]{3,2,1,0:T(8,128)(2,1)}), bf16[128,3,8,256]{3,2,1,0:T(8,128)(2,1)S(1)}, u32[]{:S(2)}, u32[]{:S(2)}) async-start(bf16[128,3,8,256]{3,2,1,0:T(8,128)(2,1)} %bitcast.29), calls=%async_computation.1 | async-start | bytes 3145728 | tf_op jit(solution)/shard_map/all_to_all | solution.py:130
  217.4 1.7 copy-start.3
  221.6 6.0 %copy-start.18 = (f32[256]{0:T(256)S(1)}, f32[256]{0:T(256)}, u32[]{:S(2)}) copy-start(f32[256]{0:T(256)} %param.33) | copy-start | bytes 3076
  224.0 6.7 %copy-start.9 = (bf16[256,768]{1,0:T(8,128)(2,1)S(1)}, bf16[256,768]{1,0:T(8,128)(2,1)}, u32[]{:S(2)}) copy-start(bf16[256,768]{1,0:T(8,128)(2,1)} %param.34) | copy-start | bytes 1179652
  261.2 8.4 %copy-start.7 = (bf16[48,64,1,8,32]{1,0,4,3,2:T(8,128)(2,1)S(1)}, bf16[48,64,1,8,32]{1,0,4,3,2:T(8,128)(2,1)}, u32[]{:S(2)}) copy-start(bf16[48,64,1,8,32]{1,0,4,3,2:T(8,128)(2,1)} %get-tuple-element.5) | copy-start | bytes 4718596
  276.1 8.7 %copy-start.13 = (bf16[256,256]{1,0:T(8,128)(2,1)S(1)}, bf16[256,256]{1,0:T(8,128)(2,1)}, u32[]{:S(2)}) copy-start(bf16[256,256]{1,0:T(8,128)(2,1)} %param.35) | copy-start | bytes 393220
  279.7 9.4 %copy-start.22 = (bf16[1024,256]{1,0:T(8,128)(2,1)S(1)}, bf16[1024,256]{1,0:T(8,128)(2,1)}, u32[]{:S(2)}) copy-start(bf16[1024,256]{1,0:T(8,128)(2,1)} %param.39) | copy-start | bytes 1572868
  279.7 9.4 %copy-start.23 = (bf16[256,1024]{1,0:T(8,128)(2,1)S(1)}, bf16[256,1024]{1,0:T(8,128)(2,1)}, u32[]{:S(2)}) copy-start(bf16[256,1024]{1,0:T(8,128)(2,1)} %param.38) | copy-start | bytes 1572868
  279.7 9.4 %copy-start.25 = (f32[256]{0:T(256)S(1)}, f32[256]{0:T(256)}, u32[]{:S(2)}) copy-start(f32[256]{0:T(256)} %param.37) | copy-start | bytes 3076
  295.7 33.9 %copy-start.1 = (bf16[256,1024]{1,0:T(8,128)(2,1)S(1)}, bf16[256,1024]{1,0:T(8,128)(2,1)}, u32[]{:S(2)}) copy-start(bf16[256,1024]{1,0:T(8,128)(2,1)} %param.23) | copy-start | bytes 1572868
where the time goes:
time: 335 us; the launch traced here: 330 us
  local copies, waits for them, and re-layouts  89.6 us (27%)
  other arithmetic  66 us (20%)
  blocking collectives  61.6 us (18%)
  matrix products  53.5 us (16%)
  waiting for transfers between devices  36.6 us (11%)
  starting transfers between devices  21.7 us (6%)
    all_to_all x1, blocking collectives, body(): lax.all_to_all(stem_strips, 'cols', split_axis=1, concat_axis=0, tiled=True)  32.6 us
    all_to_all x1, blocking collectives, body(): lax.all_to_all(flat_back, ('rows', 'cols'), split_axis=0, concat_axis=0,...  29 us
    all_to_all x1, waiting for transfers between devices, body(): lax.all_to_all(flat_send, ('rows', 'cols'), split_axis=0, concat_axis=0,...  24.8 us
    reshape x2, local copies, waits for them, and re-layouts, attend(): packed = packed.reshape(count_win, places, 3, head_count, head_width)  24.7 us
    convert_element_type x1, other arithmetic, body(): activated = jax.nn.gelu(running).astype(jnp.bfloat16)  24.4 us
    sub x2, other arithmetic, attend(): scores = scores - jnp.max(scores, axis=-1, keepdims=True)  16.6 us
    all_to_all x1, starting transfers between devices, body(): lax.all_to_all(flat_send, ('rows', 'cols'), split_axis=0, concat_axis=0,...  14.5 us
    convert_element_type x2, local copies, waits for them, and re-layouts, attend(): jnp.dot(normed, in_weight, preferred_element_type=jnp.float32)  13.2 us
  transfers between devices with their start and end apart: 5, of which 4 were waited for; matrix products, arithmetic and copies ran while one was open for 0% of the time, Pallas kernels for 0%

commit v1 on v0

v1 whole, which is shorter than its diff:
```python
import functools

import jax
import jax.numpy as jnp
from jax import lax
from jax.experimental import pallas as pl
from jax.experimental.pallas import tpu as pltpu
from jax.sharding import PartitionSpec as P

EPSILON = 1e-05
LOG2E = 1.4426950408889634
GELU_A = 0.7978845608028654
GELU_B = GELU_A * 0.044715
VMEM_LIMIT = 56 * 1024 * 1024
F32 = jnp.float32
BF16 = jnp.bfloat16

CORE_ROWS = [[core + 2 * i for i in range(8)] for core in range(2)]
CORE_ALL = [[(core + 2 * i) * 8 + c for i in range(8) for c in range(8)] for core in range(2)]
Y_UP = [(c, c + 1) for c in range(7) if c % 4 != 3]
Y_DOWN = [(c + 1, c) for c in range(7) if c % 4 != 3]


def twice_gelu(x):
    inner = x * (GELU_B * (x * x) + GELU_A)
    return x * (1.0 + jnp.tanh(inner))


def own_y():
    return lax.rem(lax.axis_index("cols"), 4)


def bottleneck_kernel(
    x_ref, top_ref, bot_ref, scale_ref, shift_ref, we_ref, dw_ref, wp_ref,
    own_ref, up_ref, down_ref, e_ref,
):
    device = lax.axis_index("rows") * 8 + lax.axis_index("cols")
    has_top = (device > 0).astype(F32)
    has_bot = (device < 127).astype(F32)
    scale = scale_ref[...]
    shift = shift_ref[...]
    pad = 8

    edge = jnp.zeros((pad, 128), F32)

    def clear(index, carry):
        for lb in range(8):
            e_ref[index, lb, 0:pad, :] = edge
            e_ref[index, lb, 512 + pad : 512 + 2 * pad, :] = edge
        return carry

    lax.fori_loop(0, 8, clear, 0)

    def expand(values, row, ct, factor):
        normed = (values.astype(F32) * scale + shift).astype(BF16)
        start = pl.multiple_of(ct * 128, 128) + pad
        for nb in range(4):
            flat = jnp.dot(
                normed, we_ref[:, nb * 256 : (nb + 1) * 256], preferred_element_type=F32
            )
            wide = twice_gelu(flat)
            if factor is not None:
                wide = wide * factor
            for half in range(2):
                e_ref[row, nb * 2 + half, pl.ds(start, 128), :] = wide[
                    :, half * 128 : (half + 1) * 128
                ]

    def expand_own(step, carry):
        row = step // 4
        ct = lax.rem(step, 4)
        expand(x_ref[row, pl.ds(pl.multiple_of(ct * 128, 128), 128), :], row + 1, ct, None)
        return carry

    def expand_edge(ct, carry):
        cols = pl.ds(pl.multiple_of(ct * 128, 128), 128)
        expand(top_ref[0, cols, :], 0, ct, has_top)
        expand(bot_ref[0, cols, :], 7, ct, has_bot)
        return carry

    lax.fori_loop(0, 24, expand_own, 0)
    lax.fori_loop(0, 4, expand_edge, 0)

    def depth(step, carry):
        row = step // 4
        ct = lax.rem(step, 4)
        base = pl.multiple_of(ct * 128, 128)
        total = jnp.zeros((128, 256), F32)
        for pair in range(4):
            parts = []
            for lb in (2 * pair, 2 * pair + 1):
                acc = None
                for tap in range(9):
                    term = (
                        e_ref[row + tap // 3, lb, pl.ds(base + (pad - 1 + tap % 3), 128), :]
                        * dw_ref[tap : tap + 1, lb * 128 : (lb + 1) * 128]
                    )
                    acc = term if acc is None else acc + term
                parts.append(twice_gelu(acc).astype(BF16))
            wide = jnp.concatenate(parts, axis=1)
            total = total + jnp.dot(
                wide, wp_ref[pair * 256 : (pair + 1) * 256, :], preferred_element_type=F32
            )
        result = x_ref[row, pl.ds(base, 128), :].astype(F32) + 0.5 * total
        result = result.astype(BF16)
        for jj in range(2):
            for tp in range(4):
                at = jj * 64 + tp * 16
                own_ref[row * 4 + tp, ct * 2 + jj] = result[at : at + 16]
        return carry

    lax.fori_loop(0, 24, depth, 0)

    y = own_y()

    def pick(m, carry):
        n_up = y + 1
        row = jnp.minimum(2 * y + m // n_up, 5)
        up_ref[m] = own_ref[row * 4 + 3 - y + lax.rem(m, n_up)]
        n_down = 4 - y
        row = jnp.minimum(m // n_down, 5)
        down_ref[m] = own_ref[row * 4 + lax.rem(m, n_down)]
        return carry

    lax.fori_loop(0, 8, pick, 0)


def bottleneck(strips, top, bot, scale, shift, we, dw, wp):
    return pl.pallas_call(
        bottleneck_kernel,
        out_shape=[
            jax.ShapeDtypeStruct((24, 8, 16, 256), BF16),
            jax.ShapeDtypeStruct((8, 8, 16, 256), BF16),
            jax.ShapeDtypeStruct((8, 8, 16, 256), BF16),
        ],
        scratch_shapes=[pltpu.VMEM((8, 8, 528, 128), F32)],
        compiler_params=pltpu.CompilerParams(vmem_limit_bytes=VMEM_LIMIT),
        name="bottleneck",
    )(strips, top, bot, scale, shift, we, dw, wp)


def normed_of(x, gain):
    center = x - jnp.mean(x, axis=-1, keepdims=True)
    spread = jnp.mean(center * center, axis=-1, keepdims=True)
    return (center * lax.rsqrt(spread + EPSILON) * gain).astype(BF16)


def head_masks(dtype):
    lane = lax.broadcasted_iota(jnp.int32, (1, 128), 1)
    return [(lane // 32 == h).astype(F32).astype(dtype) for h in range(4)]


def attend_and_mix(x, w):
    tokens = x.shape[0]
    masks = head_masks(BF16)
    masks_f = head_masks(F32)
    normed = normed_of(x, w["gain_a"][...])
    q, k, v = [
        jnp.dot(normed, w["inputs"][:, c * 256 : (c + 1) * 256], preferred_element_type=F32).astype(
            BF16
        )
        for c in range(3)
    ]
    rows = []
    for win in range(tokens // 64):
        at = slice(win * 64, (win + 1) * 64)
        groups = []
        for g in range(2):
            lanes = slice(g * 128, (g + 1) * 128)
            qg, kg, vg = q[at, lanes], k[at, lanes], v[at, lanes]
            spread_q = jnp.concatenate([qg * masks[h] for h in range(4)], axis=0)
            scores = lax.dot_general(
                kg, spread_q, (((1,), (1,)), ((), ())), preferred_element_type=F32
            )
            scores = scores * (LOG2E * 32**-0.5) + w["bias"][g]
            scores = scores - jnp.max(scores, axis=0, keepdims=True)
            weights = jnp.exp2(scores)
            weights = weights * (1.0 / jnp.sum(weights, axis=0, keepdims=True))
            mixed = lax.dot_general(
                weights.astype(BF16), vg, (((0,), (0,)), ((), ())), preferred_element_type=F32
            )
            out = mixed[0:64] * masks_f[0]
            for h in range(1, 4):
                out = out + mixed[h * 64 : (h + 1) * 64] * masks_f[h]
            groups.append(out.astype(BF16))
        rows.append(jnp.concatenate(groups, axis=1))
    combined = jnp.concatenate(rows, axis=0)
    x = x + jnp.dot(combined, w["output"][...], preferred_element_type=F32)
    x = x.astype(BF16).astype(F32)
    normed = normed_of(x, w["gain_m"][...])
    total = jnp.zeros((tokens, 256), F32)
    for c in range(4):
        cols = slice(c * 256, (c + 1) * 256)
        hidden = jnp.dot(normed, w["up"][:, cols], preferred_element_type=F32)
        hidden = twice_gelu(hidden).astype(BF16)
        total = total + jnp.dot(hidden, w["down"][cols, :], preferred_element_type=F32)
    return x + 0.5 * total


NAMES = ("gain_a", "inputs", "output", "bias", "gain_m", "up", "down")


def block_kernel(k, own_ref, up_ref, down_ref, *refs):
    w = dict(zip(NAMES, refs))
    out_ref = refs[len(NAMES)]
    y = own_y()
    n = 3 * y + k
    p = n // 4
    tp = lax.rem(n, 4)
    places = []
    for s in range(8):
        row = 8 * p + s
        owner = row // 6
        local = row - 6 * owner
        v = jnp.maximum(y - 1, 0)
        m_up = jnp.clip((local - 2 * v) * (v + 1) + tp - (3 - v), 0, 7)
        v = jnp.minimum(y + 1, 3)
        m_down = jnp.clip(local * (4 - v) + tp, 0, 7)
        places.append((owner, local * 4 + tp, m_up, m_down))

    def step(g, carry):
        units = []
        for owner, at, m_up, m_down in places:
            js = pl.ds(g * 2, 2)
            mine = own_ref[at, js].astype(F32)
            above = up_ref[m_up, js].astype(F32)
            below = down_ref[m_down, js].astype(F32)
            units.append(jnp.where(owner == y, mine, jnp.where(owner < y, above, below)))
        x = jnp.concatenate(
            [
                units[s][jj, t * 8 : (t + 1) * 8, :]
                for jj in range(2)
                for t in range(2)
                for s in range(8)
            ],
            axis=0,
        )
        out = attend_and_mix(x, w)
        for s in range(8):
            for jj in range(2):
                both = [out[(jj * 2 + t) * 64 + s * 8 :][:8] for t in range(2)]
                out_ref[s, g * 2 + jj] = jnp.concatenate(both, axis=0).astype(BF16)
        return carry

    lax.fori_loop(0, 4, step, 0)


def grid_kernel(x_ref, *refs):
    w = dict(zip(NAMES, refs))
    out_ref, flat_ref = refs[len(NAMES) :]

    def load(i, carry):
        values = x_ref[i].astype(F32).reshape(128, 256)
        for half in range(2):
            flat_ref[half, pl.ds(pl.multiple_of(i * 128, 128), 128), :] = values[
                :, half * 128 : (half + 1) * 128
            ]
        return carry

    lax.fori_loop(0, 8, load, 0)

    def step(g, carry):
        windows = []
        for b in range(4):
            at = pl.ds(g * 4 + b, 64, stride=16)
            windows.append(
                jnp.concatenate([flat_ref[half, at, :] for half in range(2)], axis=1)
            )
        out = attend_and_mix(jnp.concatenate(windows, axis=0), w)
        for b in range(4):
            at = pl.ds(g * 4 + b, 64, stride=16)
            for half in range(2):
                flat_ref[half, at, :] = out[
                    b * 64 : (b + 1) * 64, half * 128 : (half + 1) * 128
                ]
        return carry

    lax.fori_loop(0, 4, step, 0)

    def store(i, carry):
        at = pl.ds(pl.multiple_of(i * 128, 128), 128)
        values = jnp.concatenate([flat_ref[half, at, :] for half in range(2)], axis=1)
        out_ref[pl.ds(i * 8, 8)] = values.astype(BF16).reshape(8, 16, 256)
        return carry

    lax.fori_loop(0, 8, store, 0)


def block_section(k, own, up, down, weights):
    return pl.pallas_call(
        functools.partial(block_kernel, k),
        out_shape=jax.ShapeDtypeStruct((8, 8, 16, 256), BF16),
        compiler_params=pltpu.CompilerParams(vmem_limit_bytes=VMEM_LIMIT),
        name="block_section",
    )(own, up, down, *weights)


def grid_section(x, weights):
    return pl.pallas_call(
        grid_kernel,
        out_shape=jax.ShapeDtypeStruct((64, 16, 256), BF16),
        scratch_shapes=[pltpu.VMEM((2, 1024, 128), F32)],
        compiler_params=pltpu.CompilerParams(vmem_limit_bytes=VMEM_LIMIT),
        name="grid_section",
    )(x, *weights)


def turned_bias(bias):
    return (bias * LOG2E).reshape(2, 4, 64, 64).transpose(0, 3, 1, 2).reshape(2, 64, 256)


def body(
    stem_strips, norm_scale, norm_shift, expand_weight, depth_weight, project_weight,
    block_gain, block_inputs, block_output, block_bias, first_gain, first_up, first_down,
    grid_gain, grid_inputs, grid_output, grid_bias, second_gain, second_up, second_down,
):
    row = lambda a: a.reshape(1, -1)
    both = ("rows", "cols")
    top = lax.ppermute(stem_strips[5:6], both, [(d, d + 1) for d in range(127)])
    bot = lax.ppermute(stem_strips[0:1], both, [(d + 1, d) for d in range(127)])
    own, up, down = bottleneck(
        stem_strips, top, bot, row(norm_scale), row(norm_shift), expand_weight,
        depth_weight * 0.5, project_weight,
    )
    up = lax.ppermute(up, "cols", Y_UP)
    down = lax.ppermute(down, "cols", Y_DOWN)
    block_weights = (
        row(block_gain), block_inputs, block_output, turned_bias(block_bias),
        row(first_gain), first_up, first_down,
    )
    grid_weights = (
        row(grid_gain), grid_inputs, grid_output, turned_bias(grid_bias),
        row(second_gain), second_up, second_down,
    )
    done = [block_section(k, own, up, down, block_weights) for k in range(3)]
    sent = jnp.stack(done, axis=1)
    arrived = lax.all_to_all(sent, "rows", 0, 0, axis_index_groups=CORE_ROWS, tiled=True)
    grids = [grid_section(arrived[:, k], grid_weights) for k in range(3)]
    back = jnp.stack(grids, axis=1)
    landed = lax.all_to_all(back, both, 0, 0, axis_index_groups=CORE_ALL, tiled=True)
    landed = landed.reshape(8, 2, 3, 4, 16, 256).transpose(1, 2, 0, 3, 4, 5)
    return landed.reshape(48, 64, 256)


def solution(mesh):
    return jax.shard_map(
        body,
        mesh=mesh,
        in_specs=(P(("rows", "cols"), None, None),) + (P(),) * 19,
        out_specs=P("rows", "cols", None),
        check_vma=False,
    )
```

time: 335 us -> 196 us (0.59); the launches traced: 330 us -> 196 us
  Pallas kernels: 0 us -> 95 us
  local copies, waits for them, and re-layouts: 89.6 us -> 8.4 us
  other arithmetic: 66 us -> 3.95 us
  matrix products: 53.5 us -> 0 us
  blocking collectives: 61.6 us -> 32.8 us
  starting transfers between devices: 21.7 us -> 17.5 us
    pallas_call x0 -> x7, Pallas kernels: none -> 95 us  [the longest x3 34.5 us: block_section(): pl.pallas_call(functools.partial(block_kernel, k), out_shape=jax.ShapeDty...]
    dot_general x12 -> x0, matrix products: 53.5 us -> none  [the longest x2 13.1 us: feed_forward(): jnp.dot(hidden, down_weight, preferred_element_type=jnp.float32)]
    reshape x6 -> x4, local copies, waits for them, and re-layouts: 39.4 us -> 2.01 us  [turned_bias(): (bias * LOG2E).reshape(2, 4, 64, 64).transpose(0, 3, 1, 2)]
    convert_element_type x5 -> x0, other arithmetic: 33 us -> none  [the longest x1 24.4 us: body(): activated = jax.nn.gelu(running).astype(jnp.bfloat16)]
    all_to_all x2 -> x1, blocking collectives: 61.6 us -> 32.8 us  [body(): lax.all_to_all(back, both, 0, 0, axis_index_groups=CORE_ALL, tiled=True)]
    convert_element_type x8 -> x0, local copies, waits for them, and re-layouts: 27.9 us -> none  [the longest x2 13.2 us: attend(): jnp.dot(normed, in_weight, preferred_element_type=jnp.float32)]
    sub x2 -> x0, other arithmetic: 16.6 us -> none  [attend(): scores = scores - jnp.max(scores, axis=-1, keepdims=True)]
    slice x4 -> x1, local copies, waits for them, and re-layouts: 11.8 us -> 1.06 us  [body(): bot = lax.ppermute(stem_strips[0:1], both, [(d + 1, d) for d in range(127)])]
  transfers between devices with their start and end apart: 5 -> 5, of which waited for: 4 -> 5; matrix products, arithmetic and copies ran while one was open for 0% -> 2% of each run, Pallas kernels for 0% -> 0%
where the time goes in v1:
time: 196 us
  Pallas kernels  95 us (48%)
  waiting for transfers between devices  37.8 us (19%)
  blocking collectives  32.8 us (17%)
  starting transfers between devices  17.5 us (9%)
  local copies, waits for them, and re-layouts  8.4 us (4%)
  other arithmetic  3.95 us (2%)
    pallas_call x3, Pallas kernels, block_section(): pl.pallas_call(functools.partial(block_kernel, k), out_shape=jax.ShapeDty...  34.5 us
    pallas_call x3, Pallas kernels, grid_section(): pl.pallas_call(grid_kernel, out_shape=jax.ShapeDtypeStruct((64, 16, 256),...  34.2 us
    all_to_all x1, blocking collectives, body(): lax.all_to_all(back, both, 0, 0, axis_index_groups=CORE_ALL, tiled=True)  32.8 us
    pallas_call x1, Pallas kernels, bottleneck(): pl.pallas_call(bottleneck_kernel, out_shape=[jax.ShapeDtypeStruct((24, 8,...  26.3 us
    all_to_all x1, waiting for transfers between devices, body(): lax.all_to_all(sent, 'rows', 0, 0, axis_index_groups=CORE_ROWS, tiled=True)  19 us
    ppermute x1, waiting for transfers between devices, body(): up = lax.ppermute(up, 'cols', Y_UP)  7.91 us
    all_to_all x1, starting transfers between devices, body(): lax.all_to_all(sent, 'rows', 0, 0, axis_index_groups=CORE_ROWS, tiled=True)  7.82 us
    ppermute x1, waiting for transfers between devices, body(): bot = lax.ppermute(stem_strips[0:1], both, [(d + 1, d) for d in range(127)])  4.11 us
  transfers between devices with their start and end apart: 5, of which 5 were waited for; matrix products, arithmetic and copies ran while one was open for 2% of the time, Pallas kernels for 0%

profile of v1, /device:TPU:0, one launch (start us, length us, event | category | flops | bytes accessed | tf_op | source)
XLA Modules:
  0.0 195.5 jit_solution(847464542009310590)
XLA Ops:
  0.0 1.1 fusion
  1.1 3.6 %collective-permute-start = (bf16[1,512,256]{2,1,0:T(8,128)(2,1)S(1)}, bf16[1,512,256]{2,1,0:T(8,128)(2,1)S(1)}, u32[]{:S(2)}, u32[]{:S(2)}) collective-permute-start(bf16[1,512,256]{2,1,0:T(8,128)(2,1)S(1)} %get-tuple-element.15), channel_id=1, source_target_pairs={{0,1},{1,2},{2,3},{3,4},{4,5},{5,6},{6,7},{7,8},{8,9},{9,10},{10,1... | collective-permute-start | bytes 786440 | tf_op jit(solution)/shard_map/ppermute | solution.py:319
  4.7 1.3 collective-permute-start.1
  6.0 1.5 broadcast_multiply_fusion.2.dw_ref
  7.4 2.8 %collective-permute-done.top_ref = bf16[1,512,256]{2,1,0:T(8,128)(2,1)S(1)} collective-permute-done((bf16[1,512,256]{2,1,0:T(8,128)(2,1)S(1)}, bf16[1,512,256]{2,1,0:T(8,128)(2,1)S(1)}, u32[]{:S(2)}, u32[]{:S(2)}) %collective-permute-start) | collective-permute-done | bytes 262176 | tf_op jit(solution)/shard_map/ppermute | solution.py:319
  10.2 0.0 copy-start.8
  10.2 4.1 %collective-permute-done.1.bot_ref = bf16[1,512,256]{2,1,0:T(8,128)(2,1)S(1)} collective-permute-done((bf16[1,512,256]{2,1,0:T(8,128)(2,1)S(1)}, bf16[1,512,256]{2,1,0:T(8,128)(2,1)S(1)}, u32[]{:S(2)}, u32[]{:S(2)}) %collective-permute-start.1) | collective-permute-done | bytes 262176 | tf_op jit(solution)/shard_map/ppermute | solution.py:320
  14.3 0.0 copy-start.9
  14.3 0.0 copy-done.8
  14.3 0.7 copy-done.9
  15.0 0.0 copy-start.6
  15.0 26.3 %bottleneck.1 = (bf16[24,8,16,256]{3,2,1,0:T(8,128)(2,1)}, bf16[8,8,16,256]{3,2,1,0:T(8,128)(2,1)}, bf16[8,8,16,256]{3,2,1,0:T(8,128)(2,1)}) custom-call(bf16[6,512,256]{2,1,0:T(8,128)(2,1)} %x_ref.1, bf16[1,512,256]{2,1,0:T(8,128)(2,1)} %copy-done.8, bf16[1,512,256]{2,1,0:T(8,128)(2,1)} %copy-done.9, f32[1,256]{1,0:T(1,128)} %bitcast.55, ...), custom_call_target="tpu_custom_call" | custom-call | tf_op jit(solution)/shard_map/bottleneck/pallas_call | solution.py:129
  41.3 3.5 %collective-permute-start.2 = (bf16[8,8,16,256]{3,2,1,0:T(8,128)(2,1)}, bf16[8,8,16,256]{3,2,1,0:T(8,128)(2,1)S(1)}, u32[]{:S(2)}, u32[]{:S(2)}) collective-permute-start(bf16[8,8,16,256]{3,2,1,0:T(8,128)(2,1)} %get-tuple-element.9), channel_id=1, source_target_pairs={{0,1},{1,2},{2,3},{4,5},{5,6},{6,7},{8,9},{9,10},{10,11},{12,13},{... | collective-permute-start | bytes 1572872 | tf_op jit(solution)/shard_map/ppermute | solution.py:325
  44.8 1.3 collective-permute-start.3
  46.1 0.0 copy-done.6
  46.2 0.1 copy.30
  46.3 0.9 reshape.40.refs_3_
  47.2 7.9 %collective-permute-done.2.up_ref = bf16[8,8,16,256]{3,2,1,0:T(8,128)(2,1)S(1)} collective-permute-done((bf16[8,8,16,256]{3,2,1,0:T(8,128)(2,1)}, bf16[8,8,16,256]{3,2,1,0:T(8,128)(2,1)S(1)}, u32[]{:S(2)}, u32[]{:S(2)}) %collective-permute-start.2) | collective-permute-done | bytes 524320 | tf_op jit(solution)/shard_map/ppermute | solution.py:325
  55.1 0.0 copy-start
  55.1 4.0 %collective-permute-done.3.down_ref = bf16[8,8,16,256]{3,2,1,0:T(8,128)(2,1)S(1)} collective-permute-done((bf16[8,8,16,256]{3,2,1,0:T(8,128)(2,1)}, bf16[8,8,16,256]{3,2,1,0:T(8,128)(2,1)S(1)}, u32[]{:S(2)}, u32[]{:S(2)}) %collective-permute-start.3) | collective-permute-done | bytes 524320 | tf_op jit(solution)/shard_map/ppermute | solution.py:326
  59.1 0.0 copy-start.1
  59.1 0.0 copy-done
  59.1 0.8 copy-done.1
  60.0 11.5 %block_section.3 = bf16[8,8,16,256]{3,2,1,0:T(8,128)(2,1)} custom-call(bf16[24,8,16,256]{3,2,1,0:T(8,128)(2,1)} %get-tuple-element.8.own_ref, bf16[8,8,16,256]{3,2,1,0:T(8,128)(2,1)} %copy-done, bf16[8,8,16,256]{3,2,1,0:T(8,128)(2,1)} %copy-done.1, f32[1,256]{1,0:T(1,128)} %bitcast.43, bf16[256,768]{1,0:T(8,128)(2,1)} %refs_1_.8, bf16[256,256]{1,0:T(8,128)(2,1)} %refs_2_.8, ...), custom_call_target="tpu_custom_call" | custom-call | tf_op jit(solution)/shard_map/block_section/pallas_call | solution.py:290
  71.4 11.5 %block_section.4 = bf16[8,8,16,256]{3,2,1,0:T(8,128)(2,1)} custom-call(bf16[24,8,16,256]{3,2,1,0:T(8,128)(2,1)} %get-tuple-element.8.own_ref, bf16[8,8,16,256]{3,2,1,0:T(8,128)(2,1)} %copy-done, bf16[8,8,16,256]{3,2,1,0:T(8,128)(2,1)} %copy-done.1, f32[1,256]{1,0:T(1,128)} %bitcast.44, bf16[256,768]{1,0:T(8,128)(2,1)} %refs_1_.8, bf16[256,256]{1,0:T(8,128)(2,1)} %refs_2_.8, ...), custom_call_target="tpu_custom_call" | custom-call | tf_op jit(solution)/shard_map/block_section/pallas_call | solution.py:290
  82.9 0.0 copy-start.3
  82.9 11.6 %block_section.5 = bf16[8,8,16,256]{3,2,1,0:T(8,128)(2,1)} custom-call(bf16[24,8,16,256]{3,2,1,0:T(8,128)(2,1)} %get-tuple-element.8.own_ref, bf16[8,8,16,256]{3,2,1,0:T(8,128)(2,1)} %copy-done, bf16[8,8,16,256]{3,2,1,0:T(8,128)(2,1)} %copy-done.1, f32[1,256]{1,0:T(1,128)} %bitcast.45, bf16[256,768]{1,0:T(8,128)(2,1)} %refs_1_.8, bf16[256,256]{1,0:T(8,128)(2,1)} %refs_2_.8, ...), custom_call_target="tpu_custom_call" | custom-call | tf_op jit(solution)/shard_map/block_section/pallas_call | solution.py:290
  94.5 0.0 copy-done.2
  94.5 0.0 copy-done.3
  94.5 1.2 pad_maximum_fusion
  95.7 1.2 copy.31
  97.0 0.0 copy-start.7
  97.0 7.8 %all-to-all-start = ((bf16[8,3,8,16,256]{4,3,2,1,0:T(8,128)(2,1)}), bf16[8,3,8,16,256]{4,3,2,1,0:T(8,128)(2,1)S(1)}, u32[]{:S(2)}, u32[]{:S(2)}) async-start(bf16[8,3,8,16,256]{4,3,2,1,0:T(8,128)(2,1)} %copy.31), calls=%async_computation | async-start | bytes 3145728 | tf_op jit(solution)/shard_map/all_to_all | solution.py:337
  104.8 0.0 copy-done.7
  104.8 0.1 copy.33
  105.0 0.9 reshape.44.refs_3_
  105.8 19.0 %all-to-all-done = bf16[8,3,8,16,256]{4,3,2,1,0:T(8,128)(2,1)S(1)} async-done(((bf16[8,3,8,16,256]{4,3,2,1,0:T(8,128)(2,1)}), bf16[8,3,8,16,256]{4,3,2,1,0:T(8,128)(2,1)S(1)}, u32[]{:S(2)}, u32[]{:S(2)}) %all-to-all-start) | async-done | bytes 1572896 | tf_op jit(solution)/shard_map/all_to_all | solution.py:337
  124.8 1.2 slice_bitcast_fusion.2
  126.0 11.4 %grid_section.3 = bf16[64,16,256]{2,1,0:T(8,128)(2,1)} custom-call(bf16[8,8,16,256]{3,2,1,0:T(8,128)(2,1)} %get-tuple-element.11.x_ref, f32[1,256]{1,0:T(1,128)} %bitcast.49, bf16[256,768]{1,0:T(8,128)(2,1)} %refs_1_.11, bf16[256,256]{1,0:T(8,128)(2,1)} %refs_2_.11, f32[2,64,256]{2,1,0:T(8,128)} %reshape.44.refs_3_, f32[1,256]{1,0:T(1,128)} %bitcast.52, ...), custom_call_target="tpu_custom_call" | custom-call | tf_op jit(solution)/shard_map/grid_section/pallas_call | solution.py:299
  137.4 11.4 %grid_section.4 = bf16[64,16,256]{2,1,0:T(8,128)(2,1)} custom-call(bf16[8,8,16,256]{3,2,1,0:T(8,128)(2,1)} %get-tuple-element.12.x_ref, f32[1,256]{1,0:T(1,128)} %bitcast.50, bf16[256,768]{1,0:T(8,128)(2,1)} %refs_1_.11, bf16[256,256]{1,0:T(8,128)(2,1)} %refs_2_.11, f32[2,64,256]{2,1,0:T(8,128)} %reshape.44.refs_3_, f32[1,256]{1,0:T(1,128)} %bitcast.53, ...), custom_call_target="tpu_custom_call" | custom-call | tf_op jit(solution)/shard_map/grid_section/pallas_call | solution.py:299
  148.8 0.0 copy-start.4
  148.8 11.4 %grid_section.5 = bf16[64,16,256]{2,1,0:T(8,128)(2,1)} custom-call(bf16[8,8,16,256]{3,2,1,0:T(8,128)(2,1)} %get-tuple-element.13.x_ref, f32[1,256]{1,0:T(1,128)} %bitcast.51, bf16[256,768]{1,0:T(8,128)(2,1)} %refs_1_.11, bf16[256,256]{1,0:T(8,128)(2,1)} %refs_2_.11, f32[2,64,256]{2,1,0:T(8,128)} %reshape.44.refs_3_, f32[1,256]{1,0:T(1,128)} %bitcast.54, ...), custom_call_target="tpu_custom_call" | custom-call | tf_op jit(solution)/shard_map/grid_section/pallas_call | solution.py:299
  160.2 0.0 copy-done.4
  160.2 0.0 copy-done.5
  160.2 1.2 pad_maximum_fusion.1
  161.4 0.1 copy.36
  161.5 32.8 %all_to_all.10 = bf16[64,3,16,256]{3,2,1,0:T(8,128)(2,1)S(1)} all-to-all(bf16[64,3,16,256]{3,2,1,0:T(8,128)(2,1)S(1)} %copy.36), channel_id=1, replica_groups={{0,1,2,3,4,5,6,7,16,17,18,19,20,21,22,23,32,33,34,35,36,37,38,39,48,49,..., dimensions={0} | all-to-all | bytes 3145728 | tf_op jit(solution)/shard_map/all_to_all | solution.py:340
  194.3 1.2 copy.37
  (4 shorter events, 0.1 us)
Async XLA Ops:
  1.1 9.1 %collective-permute-start = (bf16[1,512,256]{2,1,0:T(8,128)(2,1)S(1)}, bf16[1,512,256]{2,1,0:T(8,128)(2,1)S(1)}, u32[]{:S(2)}, u32[]{:S(2)}) collective-permute-start(bf16[1,512,256]{2,1,0:T(8,128)(2,1)S(1)} %get-tuple-element.15), channel_id=1, source_target_pairs={{0,1},{1,2},{2,3},{3,4},{4,5},{5,6},{6,7},{7,8},{8,9},{9,10},{10,1... | collective-permute-start | bytes 786440 | tf_op jit(solution)/shard_map/ppermute | solution.py:319
  4.7 9.6 %collective-permute-start.1 = (bf16[1,512,256]{2,1,0:T(8,128)(2,1)S(1)}, bf16[1,512,256]{2,1,0:T(8,128)(2,1)S(1)}, u32[]{:S(2)}, u32[]{:S(2)}) collective-permute-start(bf16[1,512,256]{2,1,0:T(8,128)(2,1)S(1)} %get-tuple-element.14), channel_id=1, source_target_pairs={{1,0},{2,1},{3,2},{4,3},{5,4},{6,5},{7,6},{8,7},{9,8},{10,9},{11,1... | collective-permute-start | bytes 786440 | tf_op jit(solution)/shard_map/ppermute | solution.py:320
  10.2 4.1 %copy-start.8 = (bf16[1,512,256]{2,1,0:T(8,128)(2,1)}, bf16[1,512,256]{2,1,0:T(8,128)(2,1)S(1)}, u32[]{:S(2)}) copy-start(bf16[1,512,256]{2,1,0:T(8,128)(2,1)S(1)} %collective-permute-done.top_ref) | copy-start | bytes 786436
  14.3 0.7 copy-start.9
  15.0 31.1 %copy-start.6 = (f32[8,64,64]{2,1,0:T(8,128)S(1)}, f32[8,64,64]{2,1,0:T(8,128)}, u32[]{:S(2)}) copy-start(f32[8,64,64]{2,1,0:T(8,128)} %param.29) | copy-start | bytes 393220
  41.3 13.8 %collective-permute-start.2 = (bf16[8,8,16,256]{3,2,1,0:T(8,128)(2,1)}, bf16[8,8,16,256]{3,2,1,0:T(8,128)(2,1)S(1)}, u32[]{:S(2)}, u32[]{:S(2)}) collective-permute-start(bf16[8,8,16,256]{3,2,1,0:T(8,128)(2,1)} %get-tuple-element.9), channel_id=1, source_target_pairs={{0,1},{1,2},{2,3},{4,5},{5,6},{6,7},{8,9},{9,10},{10,11},{12,13},{... | collective-permute-start | bytes 1572872 | tf_op jit(solution)/shard_map/ppermute | solution.py:325
  44.8 14.3 %collective-permute-start.3 = (bf16[8,8,16,256]{3,2,1,0:T(8,128)(2,1)}, bf16[8,8,16,256]{3,2,1,0:T(8,128)(2,1)S(1)}, u32[]{:S(2)}, u32[]{:S(2)}) collective-permute-start(bf16[8,8,16,256]{3,2,1,0:T(8,128)(2,1)} %get-tuple-element.10), channel_id=1, source_target_pairs={{1,0},{2,1},{3,2},{5,4},{6,5},{7,6},{9,8},{10,9},{11,10},{13,12},{... | collective-permute-start | bytes 1572872 | tf_op jit(solution)/shard_map/ppermute | solution.py:326
  55.1 4.0 %copy-start = (bf16[8,8,16,256]{3,2,1,0:T(8,128)(2,1)}, bf16[8,8,16,256]{3,2,1,0:T(8,128)(2,1)S(1)}, u32[]{:S(2)}) copy-start(bf16[8,8,16,256]{3,2,1,0:T(8,128)(2,1)S(1)} %collective-permute-done.2.up_ref) | copy-start | bytes 1572868
  59.1 0.8 copy-start.1
  82.9 11.6 %copy-start.2 = (bf16[8,8,16,256]{3,2,1,0:T(8,128)(2,1)S(1)}, bf16[8,8,16,256]{3,2,1,0:T(8,128)(2,1)}, u32[]{:S(2)}) copy-start(bf16[8,8,16,256]{3,2,1,0:T(8,128)(2,1)} %block_section.3) | copy-start | bytes 1572868
  82.9 11.6 %copy-start.3 = (bf16[8,8,16,256]{3,2,1,0:T(8,128)(2,1)S(1)}, bf16[8,8,16,256]{3,2,1,0:T(8,128)(2,1)}, u32[]{:S(2)}) copy-start(bf16[8,8,16,256]{3,2,1,0:T(8,128)(2,1)} %block_section.4) | copy-start | bytes 1572868
  97.0 7.8 %copy-start.7 = (f32[8,64,64]{2,1,0:T(8,128)S(1)}, f32[8,64,64]{2,1,0:T(8,128)}, u32[]{:S(2)}) copy-start(f32[8,64,64]{2,1,0:T(8,128)} %param.36) | copy-start | bytes 393220
  97.0 27.8 %all-to-all-start = ((bf16[8,3,8,16,256]{4,3,2,1,0:T(8,128)(2,1)}), bf16[8,3,8,16,256]{4,3,2,1,0:T(8,128)(2,1)S(1)}, u32[]{:S(2)}, u32[]{:S(2)}) async-start(bf16[8,3,8,16,256]{4,3,2,1,0:T(8,128)(2,1)} %copy.31), calls=%async_computation | async-start | bytes 3145728 | tf_op jit(solution)/shard_map/all_to_all | solution.py:337
  148.8 11.4 %copy-start.4 = (bf16[64,16,256]{2,1,0:T(8,128)(2,1)S(1)}, bf16[64,16,256]{2,1,0:T(8,128)(2,1)}, u32[]{:S(2)}) copy-start(bf16[64,16,256]{2,1,0:T(8,128)(2,1)} %grid_section.3) | copy-start | bytes 1572868
  148.8 11.4 %copy-start.5 = (bf16[64,16,256]{2,1,0:T(8,128)(2,1)S(1)}, bf16[64,16,256]{2,1,0:T(8,128)(2,1)}, u32[]{:S(2)}) copy-start(bf16[64,16,256]{2,1,0:T(8,128)(2,1)} %grid_section.4) | copy-start | bytes 1572868

commit v2 on v1

--- a/solution.py
+++ b/solution.py
@@ -11,7 +11,7 @@
 LOG2E = 1.4426950408889634
 GELU_A = 0.7978845608028654
 GELU_B = GELU_A * 0.044715
-VMEM_LIMIT = 56 * 1024 * 1024
+VMEM_LIMIT = 40 * 1024 * 1024
 F32 = jnp.float32
 BF16 = jnp.bfloat16
 
@@ -51,9 +51,8 @@
 
     lax.fori_loop(0, 8, clear, 0)
 
-    def expand(values, row, ct, factor):
+    def expand(values, row, factor):
         normed = (values.astype(F32) * scale + shift).astype(BF16)
-        start = pl.multiple_of(ct * 128, 128) + pad
         for nb in range(4):
             flat = jnp.dot(
                 normed, we_ref[:, nb * 256 : (nb + 1) * 256], preferred_element_type=F32
@@ -62,38 +61,29 @@
             if factor is not None:
                 wide = wide * factor
             for half in range(2):
-                e_ref[row, nb * 2 + half, pl.ds(start, 128), :] = wide[
+                e_ref[row, nb * 2 + half, pad : 512 + pad, :] = wide[
                     :, half * 128 : (half + 1) * 128
                 ]
 
-    def expand_own(step, carry):
-        row = step // 4
-        ct = lax.rem(step, 4)
-        expand(x_ref[row, pl.ds(pl.multiple_of(ct * 128, 128), 128), :], row + 1, ct, None)
-        return carry
-
-    def expand_edge(ct, carry):
-        cols = pl.ds(pl.multiple_of(ct * 128, 128), 128)
-        expand(top_ref[0, cols, :], 0, ct, has_top)
-        expand(bot_ref[0, cols, :], 7, ct, has_bot)
-        return carry
-
-    lax.fori_loop(0, 24, expand_own, 0)
-    lax.fori_loop(0, 4, expand_edge, 0)
-
-    def depth(step, carry):
-        row = step // 4
-        ct = lax.rem(step, 4)
-        base = pl.multiple_of(ct * 128, 128)
-        total = jnp.zeros((128, 256), F32)
+    def expand_own(row, carry):
+        expand(x_ref[row], row + 1, None)
+        return carry
+
+    lax.fori_loop(0, 6, expand_own, 0)
+    expand(top_ref[0], 0, has_top)
+    expand(bot_ref[0], 7, has_bot)
+    taps = dw_ref[...] * 0.5
+
+    def depth(row, carry):
+        total = jnp.zeros((512, 256), F32)
         for pair in range(4):
             parts = []
             for lb in (2 * pair, 2 * pair + 1):
                 acc = None
                 for tap in range(9):
                     term = (
-                        e_ref[row + tap // 3, lb, pl.ds(base + (pad - 1 + tap % 3), 128), :]
-                        * dw_ref[tap : tap + 1, lb * 128 : (lb + 1) * 128]
+                        e_ref[row + tap // 3, lb, pl.ds(pad - 1 + tap % 3, 512), :]
+                        * taps[tap : tap + 1, lb * 128 : (lb + 1) * 128]
                     )
                     acc = term if acc is None else acc + term
                 parts.append(twice_gelu(acc).astype(BF16))
@@ -101,15 +91,15 @@
             total = total + jnp.dot(
                 wide, wp_ref[pair * 256 : (pair + 1) * 256, :], preferred_element_type=F32
             )
-        result = x_ref[row, pl.ds(base, 128), :].astype(F32) + 0.5 * total
+        result = x_ref[row].astype(F32) + 0.5 * total
         result = result.astype(BF16)
-        for jj in range(2):
+        for jj in range(8):
             for tp in range(4):
                 at = jj * 64 + tp * 16
-                own_ref[row * 4 + tp, ct * 2 + jj] = result[at : at + 16]
-        return carry
-
-    lax.fori_loop(0, 24, depth, 0)
+                own_ref[row * 4 + tp, jj] = result[at : at + 16]
+        return carry
+
+    lax.fori_loop(0, 6, depth, 0)
 
     y = own_y()
 
@@ -153,7 +143,14 @@
 def attend_and_mix(x, w):
     tokens = x.shape[0]
     masks = head_masks(BF16)
-    masks_f = head_masks(F32)
+    key_head = lax.broadcasted_iota(jnp.int32, (256, 128), 0) // 64
+    lane_head = lax.broadcasted_iota(jnp.int32, (256, 128), 1) // 32
+    head_ones = (key_head == lane_head).astype(F32).astype(BF16)
+    score_lane = lax.broadcasted_iota(jnp.int32, (64, 256), 1)
+    bias = [
+        jnp.concatenate([w["bias"][4 * g + h] for h in range(4)], axis=1) * LOG2E
+        for g in range(2)
+    ]
     normed = normed_of(x, w["gain_a"][...])
     q, k, v = [
         jnp.dot(normed, w["inputs"][:, c * 256 : (c + 1) * 256], preferred_element_type=F32).astype(
@@ -168,21 +165,24 @@
         for g in range(2):
             lanes = slice(g * 128, (g + 1) * 128)
             qg, kg, vg = q[at, lanes], k[at, lanes], v[at, lanes]
-            spread_q = jnp.concatenate([qg * masks[h] for h in range(4)], axis=0)
+            keys = jnp.concatenate([kg * masks[h] for h in range(4)], axis=0)
+            values = jnp.concatenate([vg * masks[h] for h in range(4)], axis=0)
+            values = jnp.concatenate([values, head_ones], axis=1)
             scores = lax.dot_general(
-                kg, spread_q, (((1,), (1,)), ((), ())), preferred_element_type=F32
+                qg, keys, (((1,), (1,)), ((), ())), preferred_element_type=F32
             )
-            scores = scores * (LOG2E * 32**-0.5) + w["bias"][g]
-            scores = scores - jnp.max(scores, axis=0, keepdims=True)
-            weights = jnp.exp2(scores)
-            weights = weights * (1.0 / jnp.sum(weights, axis=0, keepdims=True))
-            mixed = lax.dot_general(
-                weights.astype(BF16), vg, (((0,), (0,)), ((), ())), preferred_element_type=F32
-            )
-            out = mixed[0:64] * masks_f[0]
-            for h in range(1, 4):
-                out = out + mixed[h * 64 : (h + 1) * 64] * masks_f[h]
-            groups.append(out.astype(BF16))
+            scores = scores * (LOG2E * 32**-0.5) + bias[g]
+            top = None
+            for h in range(4):
+                peak = jnp.max(scores[:, h * 64 : (h + 1) * 64], axis=1, keepdims=True)
+                top = (
+                    jnp.broadcast_to(peak, (64, 256))
+                    if top is None
+                    else jnp.where(score_lane >= h * 64, peak, top)
+                )
+            weights = jnp.exp2(scores - top).astype(BF16)
+            mixed = jnp.dot(weights, values, preferred_element_type=F32)
+            groups.append((mixed[:, :128] * (1.0 / mixed[:, 128:])).astype(BF16))
         rows.append(jnp.concatenate(groups, axis=1))
     combined = jnp.concatenate(rows, axis=0)
     x = x + jnp.dot(combined, w["output"][...], preferred_element_type=F32)
@@ -221,7 +221,7 @@
     def step(g, carry):
         units = []
         for owner, at, m_up, m_down in places:
-            js = pl.ds(g * 2, 2)
+            js = pl.ds(g * 8, 8)
             mine = own_ref[at, js].astype(F32)
             above = up_ref[m_up, js].astype(F32)
             below = down_ref[m_down, js].astype(F32)
@@ -229,7 +229,7 @@
         x = jnp.concatenate(
             [
                 units[s][jj, t * 8 : (t + 1) * 8, :]
-                for jj in range(2)
+                for jj in range(8)
                 for t in range(2)
                 for s in range(8)
             ],
@@ -237,12 +237,12 @@
         )
         out = attend_and_mix(x, w)
         for s in range(8):
-            for jj in range(2):
+            for jj in range(8):
                 both = [out[(jj * 2 + t) * 64 + s * 8 :][:8] for t in range(2)]
-                out_ref[s, g * 2 + jj] = jnp.concatenate(both, axis=0).astype(BF16)
-        return carry
-
-    lax.fori_loop(0, 4, step, 0)
+                out_ref[s, g * 8 + jj] = jnp.concatenate(both, axis=0).astype(BF16)
+        return carry
+
+    step(0, 0)
 
 
 def grid_kernel(x_ref, *refs):
@@ -261,21 +261,21 @@
 
     def step(g, carry):
         windows = []
-        for b in range(4):
-            at = pl.ds(g * 4 + b, 64, stride=16)
+        for b in range(16):
+            at = pl.ds(b, 64, stride=16)
             windows.append(
                 jnp.concatenate([flat_ref[half, at, :] for half in range(2)], axis=1)
             )
         out = attend_and_mix(jnp.concatenate(windows, axis=0), w)
-        for b in range(4):
-            at = pl.ds(g * 4 + b, 64, stride=16)
+        for b in range(16):
+            at = pl.ds(b, 64, stride=16)
             for half in range(2):
                 flat_ref[half, at, :] = out[
                     b * 64 : (b + 1) * 64, half * 128 : (half + 1) * 128
                 ]
         return carry
 
-    lax.fori_loop(0, 4, step, 0)
+    step(0, 0)
 
     def store(i, carry):
         at = pl.ds(pl.multiple_of(i * 128, 128), 128)
@@ -303,10 +303,6 @@
         compiler_params=pltpu.CompilerParams(vmem_limit_bytes=VMEM_LIMIT),
         name="grid_section",
     )(x, *weights)
-
-
-def turned_bias(bias):
-    return (bias * LOG2E).reshape(2, 4, 64, 64).transpose(0, 3, 1, 2).reshape(2, 64, 256)
 
 
 def body(
@@ -320,16 +316,16 @@
     bot = lax.ppermute(stem_strips[0:1], both, [(d + 1, d) for d in range(127)])
     own, up, down = bottleneck(
         stem_strips, top, bot, row(norm_scale), row(norm_shift), expand_weight,
-        depth_weight * 0.5, project_weight,
+        depth_weight, project_weight,
     )
     up = lax.ppermute(up, "cols", Y_UP)
     down = lax.ppermute(down, "cols", Y_DOWN)
     block_weights = (
-        row(block_gain), block_inputs, block_output, turned_bias(block_bias),
+        row(block_gain), block_inputs, block_output, block_bias,
         row(first_gain), first_up, first_down,
     )
     grid_weights = (
-        row(grid_gain), grid_inputs, grid_output, turned_bias(grid_bias),
+        row(grid_gain), grid_inputs, grid_output, grid_bias,
         row(second_gain), second_up, second_down,
     )
     done = [block_section(k, own, up, down, block_weights) for k in range(3)]

time: 196 us -> 152 us (0.78)
  Pallas kernels: 95 us -> 49.3 us
  blocking collectives: 32.8 us -> 63.7 us
  waiting for transfers between devices: 37.8 us -> 16.6 us
  starting transfers between devices: 17.5 us -> 11.8 us
  other arithmetic: 3.95 us -> 0.35 us
    all_to_all x0 -> x1, blocking collectives: none -> 35.1 us  [body(): lax.all_to_all(sent, 'rows', 0, 0, axis_index_groups=CORE_ROWS, tiled=True)]
    pallas_call x3, Pallas kernels: 34.5 us -> 15.5 us  [block_section(): pl.pallas_call(functools.partial(block_kernel, k), out_shape=jax.ShapeDty...]
    all_to_all x1 -> x0, waiting for transfers between devices: 19 us -> none  [body(): lax.all_to_all(sent, 'rows', 0, 0, axis_index_groups=CORE_ROWS, tiled=True)]
    pallas_call x3, Pallas kernels: 34.2 us -> 17 us  [grid_section(): pl.pallas_call(grid_kernel, out_shape=jax.ShapeDtypeStruct((64, 16, 256),...]
    pallas_call x1, Pallas kernels: 26.3 us -> 16.8 us  [bottleneck(): pl.pallas_call(bottleneck_kernel, out_shape=[jax.ShapeDtypeStruct((24, 8,...]
    all_to_all x1 -> x0, starting transfers between devices: 7.82 us -> none  [body(): lax.all_to_all(sent, 'rows', 0, 0, axis_index_groups=CORE_ROWS, tiled=True)]
    unnamed x20 -> x40, local copies, waits for them, and re-layouts: 1.53 us -> 7 us
    all_to_all x1, blocking collectives: 32.8 us -> 28.5 us  [body(): lax.all_to_all(back, both, 0, 0, axis_index_groups=CORE_ALL, tiled=True)]
  transfers between devices with their start and end apart: 5 -> 4, of which waited for: 5 -> 4; matrix products, arithmetic and copies ran while one was open for 2% -> 0% of each run, Pallas kernels for 0% -> 0%
where the time goes in v2:
time: 152 us; the launch traced here: 151 us
  blocking collectives  63.7 us (42%)
  Pallas kernels  49.3 us (32%)
  waiting for transfers between devices  16.6 us (11%)
  starting transfers between devices  11.8 us (8%)
  local copies, waits for them, and re-layouts  9.61 us (6%)
    all_to_all x1, blocking collectives, body(): lax.all_to_all(sent, 'rows', 0, 0, axis_index_groups=CORE_ROWS, tiled=True)  35.1 us
    all_to_all x1, blocking collectives, body(): lax.all_to_all(back, both, 0, 0, axis_index_groups=CORE_ALL, tiled=True)  28.5 us
    pallas_call x3, Pallas kernels, grid_section(): pl.pallas_call(grid_kernel, out_shape=jax.ShapeDtypeStruct((64, 16, 256),...  17 us
    pallas_call x1, Pallas kernels, bottleneck(): pl.pallas_call(bottleneck_kernel, out_shape=[jax.ShapeDtypeStruct((24, 8,...  16.8 us
    pallas_call x3, Pallas kernels, block_section(): pl.pallas_call(functools.partial(block_kernel, k), out_shape=jax.ShapeDty...  15.5 us
    unnamed x40, local copies, waits for them, and re-layouts  7 us
    ppermute x1, waiting for transfers between devices, body(): up = lax.ppermute(up, 'cols', Y_UP)  6.87 us
    ppermute x1, waiting for transfers between devices, body(): down = lax.ppermute(down, 'cols', Y_DOWN)  4.97 us
  transfers between devices with their start and end apart: 4, of which 4 were waited for; matrix products, arithmetic and copies ran while one was open for 0% of the time, Pallas kernels for 0%

profile of v2, /device:TPU:0, one launch (start us, length us, event | category | flops | bytes accessed | tf_op | source)
XLA Modules:
  0.0 151.5 jit_solution(18303086799709405117)
XLA Ops:
  0.0 1.1 fusion
  1.1 1.3 collective-permute-start.1
  2.4 4.6 %collective-permute-start = (bf16[1,512,256]{2,1,0:T(8,128)(2,1)S(1)}, bf16[1,512,256]{2,1,0:T(8,128)(2,1)S(1)}, u32[]{:S(2)}, u32[]{:S(2)}) collective-permute-start(bf16[1,512,256]{2,1,0:T(8,128)(2,1)S(1)} %get-tuple-element.15), channel_id=1, source_target_pairs={{0,1},{1,2},{2,3},{3,4},{4,5},{5,6},{6,7},{7,8},{8,9},{9,10},{10,1... | collective-permute-start | bytes 786440 | tf_op jit(solution)/shard_map/ppermute | solution.py:315
  6.9 4.0 %collective-permute-done.1.bot_ref = bf16[1,512,256]{2,1,0:T(8,128)(2,1)S(1)} collective-permute-done((bf16[1,512,256]{2,1,0:T(8,128)(2,1)S(1)}, bf16[1,512,256]{2,1,0:T(8,128)(2,1)S(1)}, u32[]{:S(2)}, u32[]{:S(2)}) %collective-permute-start.1) | collective-permute-done | bytes 262176 | tf_op jit(solution)/shard_map/ppermute | solution.py:316
  10.9 0.7 collective-permute-done.top_ref
  11.7 1.4 copy-done.6
  13.1 1.0 copy-done.11
  14.1 1.0 copy-done.12
  15.2 0.8 copy-done.13
  16.0 0.7 copy-done.18
  16.7 0.7 copy-done.19
  17.4 0.0 copy-start.9
  17.4 0.0 copy-start.16
  17.4 0.0 copy-start.17
  17.4 16.8 %bottleneck.1 = (bf16[24,8,16,256]{3,2,1,0:T(8,128)(2,1)S(1)}, bf16[8,8,16,256]{3,2,1,0:T(8,128)(2,1)S(1)}, bf16[8,8,16,256]{3,2,1,0:T(8,128)(2,1)S(1)}) custom-call(bf16[6,512,256]{2,1,0:T(8,128)(2,1)S(1)} %copy-done.6, bf16[1,512,256]{2,1,0:T(8,128)(2,1)S(1)} %collective-permute-done.top_ref, bf16[1,512,256]{2,1,0:T(8,128)(2,1)S(1)} %collective-permute-done.1.bot_ref, ...), custom_call_target="tpu_custom_call" | custom-call | tf_op jit(solution)/shard_map/bottleneck/pallas_call | solution.py:119
  34.2 4.4 %collective-permute-start.2 = (bf16[8,8,16,256]{3,2,1,0:T(8,128)(2,1)S(1)}, bf16[8,8,16,256]{3,2,1,0:T(8,128)(2,1)S(1)}, u32[]{:S(2)}, u32[]{:S(2)}) collective-permute-start(bf16[8,8,16,256]{3,2,1,0:T(8,128)(2,1)S(1)} %get-tuple-element.9), channel_id=1, source_target_pairs={{0,1},{1,2},{2,3},{4,5},{5,6},{6,7},{8,9},{9,10},{10,11},{12,13},{... | collective-permute-start | bytes 1572872 | tf_op jit(solution)/shard_map/ppermute | solution.py:321
  38.6 1.5 collective-permute-start.3
  40.1 6.9 %collective-permute-done.2.up_ref = bf16[8,8,16,256]{3,2,1,0:T(8,128)(2,1)S(1)} collective-permute-done((bf16[8,8,16,256]{3,2,1,0:T(8,128)(2,1)S(1)}, bf16[8,8,16,256]{3,2,1,0:T(8,128)(2,1)S(1)}, u32[]{:S(2)}, u32[]{:S(2)}) %collective-permute-start.2) | collective-permute-done | bytes 524320 | tf_op jit(solution)/shard_map/ppermute | solution.py:321
  47.0 5.0 %collective-permute-done.3.down_ref = bf16[8,8,16,256]{3,2,1,0:T(8,128)(2,1)S(1)} collective-permute-done((bf16[8,8,16,256]{3,2,1,0:T(8,128)(2,1)S(1)}, bf16[8,8,16,256]{3,2,1,0:T(8,128)(2,1)S(1)}, u32[]{:S(2)}, u32[]{:S(2)}) %collective-permute-start.3) | collective-permute-done | bytes 524320 | tf_op jit(solution)/shard_map/ppermute | solution.py:322
  52.0 0.0 copy-done
  52.0 0.0 copy-done.1
  52.0 0.0 copy-done.4
  52.0 0.0 copy-done.7
  52.0 0.0 copy-done.9
  52.0 0.0 copy-done.16
  52.0 0.0 copy-done.17
  52.0 5.1 %block_section.5 = bf16[8,8,16,256]{3,2,1,0:T(8,128)(2,1)S(1)} custom-call(bf16[24,8,16,256]{3,2,1,0:T(8,128)(2,1)S(1)} %get-tuple-element.8.own_ref, bf16[8,8,16,256]{3,2,1,0:T(8,128)(2,1)S(1)} %collective-permute-done.2.up_ref, bf16[8,8,16,256]{3,2,1,0:T(8,128)(2,1)S(1)} %collective-permute-done.3.down_ref, f32[1,256]{1,0:T(1,128)S(1)} %bitcast.40, ...), custom_call_target="tpu_custom_call" | custom-call | tf_op jit(solution)/shard_map/block_section/pallas_call | solution.py:290
  57.1 5.1 %block_section.4 = bf16[8,8,16,256]{3,2,1,0:T(8,128)(2,1)S(1)} custom-call(bf16[24,8,16,256]{3,2,1,0:T(8,128)(2,1)S(1)} %get-tuple-element.8.own_ref, bf16[8,8,16,256]{3,2,1,0:T(8,128)(2,1)S(1)} %collective-permute-done.2.up_ref, bf16[8,8,16,256]{3,2,1,0:T(8,128)(2,1)S(1)} %collective-permute-done.3.down_ref, f32[1,256]{1,0:T(1,128)S(1)} %bitcast.41, ...), custom_call_target="tpu_custom_call" | custom-call | tf_op jit(solution)/shard_map/block_section/pallas_call | solution.py:290
  62.2 5.3 %block_section.3 = bf16[8,8,16,256]{3,2,1,0:T(8,128)(2,1)S(1)} custom-call(bf16[24,8,16,256]{3,2,1,0:T(8,128)(2,1)S(1)} %get-tuple-element.8.own_ref, bf16[8,8,16,256]{3,2,1,0:T(8,128)(2,1)S(1)} %collective-permute-done.2.up_ref, bf16[8,8,16,256]{3,2,1,0:T(8,128)(2,1)S(1)} %collective-permute-done.3.down_ref, f32[1,256]{1,0:T(1,128)S(1)} %bitcast.42, ...), custom_call_target="tpu_custom_call" | custom-call | tf_op jit(solution)/shard_map/block_section/pallas_call | solution.py:290
  67.6 0.2 pad_maximum_fusion
  67.8 0.1 copy.24
  67.9 35.1 %all_to_all.10 = bf16[8,3,8,16,256]{4,3,2,1,0:T(8,128)(2,1)S(1)} all-to-all(bf16[8,3,8,16,256]{4,3,2,1,0:T(8,128)(2,1)S(1)} %copy.24), channel_id=1, replica_groups={{0,16,32,48,64,80,96,112},{8,24,40,56,72,88,104,120},{1,17,33,49,65,81,..., dimensions={0} | all-to-all | bytes 3145728 | tf_op jit(solution)/shard_map/all_to_all | solution.py:333
  103.0 0.0 copy-start.10
  103.0 0.0 copy-start.14
  103.0 0.0 copy-start.15
  103.1 0.1 slice_bitcast_fusion.2
  103.2 0.9 copy-done.2
  104.0 0.2 copy-done.3
  104.2 0.1 copy-done.5
  104.3 0.1 copy-done.8
  104.4 0.0 copy-done.10
  104.4 5.6 %grid_section.3 = bf16[64,16,256]{2,1,0:T(8,128)(2,1)S(1)} custom-call(bf16[8,8,16,256]{3,2,1,0:T(8,128)(2,1)S(1)} %get-tuple-element.11.x_ref, f32[1,256]{1,0:T(1,128)S(1)} %bitcast.34, bf16[256,768]{1,0:T(8,128)(2,1)S(1)} %copy-done.5, bf16[256,256]{1,0:T(8,128)(2,1)S(1)} %copy-done.10, f32[8,64,64]{2,1,0:T(8,128)S(1)} %copy-done.8, ...), custom_call_target="tpu_custom_call" | custom-call | tf_op jit(solution)/shard_map/grid_section/pallas_call | solution.py:299
  110.0 5.6 %grid_section.4 = bf16[64,16,256]{2,1,0:T(8,128)(2,1)S(1)} custom-call(bf16[8,8,16,256]{3,2,1,0:T(8,128)(2,1)S(1)} %get-tuple-element.12.x_ref, f32[1,256]{1,0:T(1,128)S(1)} %bitcast.35, bf16[256,768]{1,0:T(8,128)(2,1)S(1)} %copy-done.5, bf16[256,256]{1,0:T(8,128)(2,1)S(1)} %copy-done.10, f32[8,64,64]{2,1,0:T(8,128)S(1)} %copy-done.8, ...), custom_call_target="tpu_custom_call" | custom-call | tf_op jit(solution)/shard_map/grid_section/pallas_call | solution.py:299
  115.6 5.8 %grid_section.5 = bf16[64,16,256]{2,1,0:T(8,128)(2,1)S(1)} custom-call(bf16[8,8,16,256]{3,2,1,0:T(8,128)(2,1)S(1)} %get-tuple-element.13.x_ref, f32[1,256]{1,0:T(1,128)S(1)} %bitcast.36, bf16[256,768]{1,0:T(8,128)(2,1)S(1)} %copy-done.5, bf16[256,256]{1,0:T(8,128)(2,1)S(1)} %copy-done.10, f32[8,64,64]{2,1,0:T(8,128)S(1)} %copy-done.8, ...), custom_call_target="tpu_custom_call" | custom-call | tf_op jit(solution)/shard_map/grid_section/pallas_call | solution.py:299
  121.4 0.2 pad_maximum_fusion.1
  121.6 0.1 copy.28
  121.7 28.5 %all_to_all.11 = bf16[64,3,16,256]{3,2,1,0:T(8,128)(2,1)S(1)} all-to-all(bf16[64,3,16,256]{3,2,1,0:T(8,128)(2,1)S(1)} %copy.28), channel_id=1, replica_groups={{0,1,2,3,4,5,6,7,16,17,18,19,20,21,22,23,32,33,34,35,36,37,38,39,48,49,..., dimensions={0} | all-to-all | bytes 3145728 | tf_op jit(solution)/shard_map/all_to_all | solution.py:336
  150.2 1.2 copy.29
  (16 shorter events, 0.0 us)
Async XLA Ops:
  1.1 9.9 %collective-permute-start.1 = (bf16[1,512,256]{2,1,0:T(8,128)(2,1)S(1)}, bf16[1,512,256]{2,1,0:T(8,128)(2,1)S(1)}, u32[]{:S(2)}, u32[]{:S(2)}) collective-permute-start(bf16[1,512,256]{2,1,0:T(8,128)(2,1)S(1)} %get-tuple-element.14), channel_id=1, source_target_pairs={{1,0},{2,1},{3,2},{4,3},{5,4},{6,5},{7,6},{8,7},{9,8},{10,9},{11,1... | collective-permute-start | bytes 786440 | tf_op jit(solution)/shard_map/ppermute | solution.py:316
  2.4 9.3 %collective-permute-start = (bf16[1,512,256]{2,1,0:T(8,128)(2,1)S(1)}, bf16[1,512,256]{2,1,0:T(8,128)(2,1)S(1)}, u32[]{:S(2)}, u32[]{:S(2)}) collective-permute-start(bf16[1,512,256]{2,1,0:T(8,128)(2,1)S(1)} %get-tuple-element.15), channel_id=1, source_target_pairs={{0,1},{1,2},{2,3},{3,4},{4,5},{5,6},{6,7},{7,8},{8,9},{9,10},{10,1... | collective-permute-start | bytes 786440 | tf_op jit(solution)/shard_map/ppermute | solution.py:315
  11.7 1.4 copy-start.6
  13.1 1.0 copy-start.11
  14.1 1.0 copy-start.12
  15.2 0.8 copy-start.13
  16.0 0.7 copy-start.18
  16.7 0.7 copy-start.19
  17.4 34.6 %copy-start = (bf16[256,1024]{1,0:T(8,128)(2,1)S(1)}, bf16[256,1024]{1,0:T(8,128)(2,1)}, u32[]{:S(2)}) copy-start(bf16[256,1024]{1,0:T(8,128)(2,1)} %refs_5_.8) | copy-start | bytes 1572868
  17.4 34.6 %copy-start.1 = (bf16[1024,256]{1,0:T(8,128)(2,1)S(1)}, bf16[1024,256]{1,0:T(8,128)(2,1)}, u32[]{:S(2)}) copy-start(bf16[1024,256]{1,0:T(8,128)(2,1)} %refs_6_.8) | copy-start | bytes 1572868
  17.4 34.6 %copy-start.4 = (bf16[256,768]{1,0:T(8,128)(2,1)S(1)}, bf16[256,768]{1,0:T(8,128)(2,1)}, u32[]{:S(2)}) copy-start(bf16[256,768]{1,0:T(8,128)(2,1)} %refs_1_.8) | copy-start | bytes 1179652
  17.4 34.6 %copy-start.7 = (f32[8,64,64]{2,1,0:T(8,128)S(1)}, f32[8,64,64]{2,1,0:T(8,128)}, u32[]{:S(2)}) copy-start(f32[8,64,64]{2,1,0:T(8,128)} %refs_3_.8) | copy-start | bytes 393220
  17.4 34.6 %copy-start.9 = (bf16[256,256]{1,0:T(8,128)(2,1)S(1)}, bf16[256,256]{1,0:T(8,128)(2,1)}, u32[]{:S(2)}) copy-start(bf16[256,256]{1,0:T(8,128)(2,1)} %refs_2_.8) | copy-start | bytes 393220
  17.4 34.6 %copy-start.16 = (f32[256]{0:T(256)S(1)}, f32[256]{0:T(256)}, u32[]{:S(2)}) copy-start(f32[256]{0:T(256)} %param.26) | copy-start | bytes 3076
  17.4 34.6 %copy-start.17 = (f32[256]{0:T(256)S(1)}, f32[256]{0:T(256)}, u32[]{:S(2)}) copy-start(f32[256]{0:T(256)} %param.30) | copy-start | bytes 3076
  34.2 12.8 %collective-permute-start.2 = (bf16[8,8,16,256]{3,2,1,0:T(8,128)(2,1)S(1)}, bf16[8,8,16,256]{3,2,1,0:T(8,128)(2,1)S(1)}, u32[]{:S(2)}, u32[]{:S(2)}) collective-permute-start(bf16[8,8,16,256]{3,2,1,0:T(8,128)(2,1)S(1)} %get-tuple-element.9), channel_id=1, source_target_pairs={{0,1},{1,2},{2,3},{4,5},{5,6},{6,7},{8,9},{9,10},{10,11},{12,13},{... | collective-permute-start | bytes 1572872 | tf_op jit(solution)/shard_map/ppermute | solution.py:321
  38.6 13.3 %collective-permute-start.3 = (bf16[8,8,16,256]{3,2,1,0:T(8,128)(2,1)S(1)}, bf16[8,8,16,256]{3,2,1,0:T(8,128)(2,1)S(1)}, u32[]{:S(2)}, u32[]{:S(2)}) collective-permute-start(bf16[8,8,16,256]{3,2,1,0:T(8,128)(2,1)S(1)} %get-tuple-element.10), channel_id=1, source_target_pairs={{1,0},{2,1},{3,2},{5,4},{6,5},{7,6},{9,8},{10,9},{11,10},{13,12},{... | collective-permute-start | bytes 1572872 | tf_op jit(solution)/shard_map/ppermute | solution.py:322
  103.0 1.0 copy-start.2
  103.0 1.2 copy-start.3
  103.0 1.3 copy-start.5
  103.0 1.4 copy-start.8
  103.0 1.4 copy-start.10
  103.0 1.4 copy-start.14
  103.0 1.4 copy-start.15

commit v3 on v2

v3 whole, which is shorter than its diff:
```python
import functools

import jax
import jax.numpy as jnp
from jax import lax
from jax.experimental import pallas as pl
from jax.experimental.pallas import tpu as pltpu
from jax.sharding import PartitionSpec as P

EPSILON = 1e-05
LOG2E = 1.4426950408889634
GELU_A = 0.7978845608028654
GELU_B = GELU_A * 0.044715
F32 = jnp.float32
BF16 = jnp.bfloat16

CORE_ROWS = [[core + 2 * i for i in range(8)] for core in range(2)]
CORE_ALL = [[(core + 2 * i) * 8 + c for i in range(8) for c in range(8)] for core in range(2)]
Y_UP = [(c, c + 1) for c in range(7) if c % 4 != 3]
Y_DOWN = [(c + 1, c) for c in range(7) if c % 4 != 3]


def twice_gelu(x):
    inner = x * (GELU_B * (x * x) + GELU_A)
    return x * (1.0 + jnp.tanh(inner))


def own_y():
    return lax.rem(lax.axis_index("cols"), 4)


PAD = 8


def twice_gelu_short(x):
    x = x.astype(BF16)
    inner = x * (BF16(GELU_B) * (x * x) + BF16(GELU_A))
    return x * (BF16(1.0) + jnp.tanh(inner))


def clear_edges(e_ref):
    edge = jnp.zeros((PAD, 128), F32)

    def clear(index, carry):
        for lb in range(8):
            e_ref[index, lb, 0:PAD, :] = edge
            e_ref[index, lb, 512 + PAD : 512 + 2 * PAD, :] = edge
        return carry

    lax.fori_loop(0, e_ref.shape[0], clear, 0)


def expand_row(values, scale, shift, we_ref, e_ref, row, factor):
    normed = (values.astype(F32) * scale + shift).astype(BF16)
    for nb in range(4):
        flat = jnp.dot(normed, we_ref[:, nb * 256 : (nb + 1) * 256], preferred_element_type=F32)
        wide = twice_gelu(flat)
        if factor is not None:
            wide = wide * factor
        for half in range(2):
            e_ref[row, nb * 2 + half, PAD : 512 + PAD, :] = wide[:, half * 128 : (half + 1) * 128]


def depth_row(sources, x_ref, row, taps, wp_ref, out_ref, at_row):
    for side in range(2):
        base = side * 256
        total = jnp.zeros((256, 256), F32)
        for pair in range(4):
            parts = []
            for lb in (2 * pair, 2 * pair + 1):
                acc = None
                for tap in range(9):
                    e_ref, at = sources[tap // 3]
                    term = (
                        e_ref[at, lb, pl.ds(base + PAD - 1 + tap % 3, 256), :]
                        * taps[tap : tap + 1, lb * 128 : (lb + 1) * 128]
                    )
                    acc = term if acc is None else acc + term
                parts.append(twice_gelu_short(acc))
            wide = jnp.concatenate(parts, axis=1)
            total = total + jnp.dot(
                wide, wp_ref[pair * 256 : (pair + 1) * 256, :], preferred_element_type=F32
            )
        values = x_ref[row, base : base + 256, :].astype(F32)
        result = (values + 0.5 * total).astype(BF16)
        for jj in range(4):
            for tp in range(4):
                at = jj * 64 + tp * 16
                out_ref[at_row * 4 + tp, 4 * side + jj] = result[at : at + 16]


def middle_kernel(
    x_hbm, scale_hbm, shift_hbm, we_hbm, dw_hbm, wp_hbm, mid_ref, e_ref,
    x_ref, scale_ref, shift_ref, we_ref, dw_ref, wp_ref, sem,
):
    pairs = [(scale_hbm, scale_ref), (shift_hbm, shift_ref), (we_hbm, we_ref)]
    pairs += [(x_hbm.at[r], x_ref.at[r]) for r in range(6)]
    pairs += [(dw_hbm, dw_ref), (wp_hbm, wp_ref)]
    copies = [pltpu.make_async_copy(a, b, sem.at[n]) for n, (a, b) in enumerate(pairs)]
    for copy in copies:
        copy.start()
    clear_edges(e_ref)
    for copy in copies[:3]:
        copy.wait()
    scale, shift = scale_ref[...], shift_ref[...]
    for row in range(6):
        copies[3 + row].wait()
        expand_row(x_ref[row], scale, shift, we_ref, e_ref, row, None)
    for copy in copies[9:]:
        copy.wait()
    taps = dw_ref[...] * 0.5

    def depth(step, carry):
        for row in (2 * step + 1, 2 * step + 2):
            sources = [(e_ref, row - 1), (e_ref, row), (e_ref, row + 1)]
            depth_row(sources, x_ref, row, taps, wp_ref, mid_ref, row - 1)
        return carry

    lax.fori_loop(0, 2, depth, 0)


def edge_kernel(
    x_ref, top_ref, bot_ref, e_ref, mid_ref, scale_ref, shift_ref, we_ref, dw_ref, wp_ref,
    edge_ref, up_l_ref, down_l_ref, up_r_ref, down_r_ref, halo_ref,
):
    device = lax.axis_index("rows") * 8 + lax.axis_index("cols")
    scale, shift = scale_ref[...], shift_ref[...]
    clear_edges(halo_ref)
    expand_row(top_ref[0], scale, shift, we_ref, halo_ref, 0, (device > 0).astype(F32))
    expand_row(bot_ref[0], scale, shift, we_ref, halo_ref, 1, (device < 127).astype(F32))
    taps = dw_ref[...] * 0.5
    sources = [(halo_ref, 0), (e_ref, 0), (e_ref, 1)]
    depth_row(sources, x_ref, 0, taps, wp_ref, edge_ref, 0)
    sources = [(e_ref, 4), (e_ref, 5), (halo_ref, 1)]
    depth_row(sources, x_ref, 5, taps, wp_ref, edge_ref, 1)
    v = own_y()

    def send(row, tp, m, left_ref, right_ref):
        inside = jnp.logical_and(row >= 1, row <= 4)

        @pl.when(inside)
        def _():
            at = jnp.clip(row - 1, 0, 3) * 4 + tp
            left_ref[m] = mid_ref[at, 0:4]
            right_ref[m] = mid_ref[at, 4:8]

        @pl.when(jnp.logical_not(inside))
        def _():
            at = jnp.where(row == 5, 4, 0) + tp
            left_ref[m] = edge_ref[at, 0:4]
            right_ref[m] = edge_ref[at, 4:8]

    def pick(m, carry):
        n_up = v + 1
        tp = jnp.clip(3 - v + lax.rem(m, n_up), 0, 3)
        send(jnp.minimum(2 * v + m // n_up, 5), tp, m, up_l_ref, up_r_ref)
        n_down = 4 - v
        send(jnp.minimum(m // n_down, 5), lax.rem(m, n_down), m, down_l_ref, down_r_ref)
        return carry

    lax.fori_loop(0, 8, pick, 0)


def vmem(limit):
    return pltpu.CompilerParams(vmem_limit_bytes=limit * 1024 * 1024)


def pieces(count, columns):
    return jax.ShapeDtypeStruct((count, columns, 16, 256), BF16)


def bottleneck_middle(strips, scale, shift, we, dw, wp):
    return pl.pallas_call(
        middle_kernel,
        out_shape=[pieces(16, 8), jax.ShapeDtypeStruct((6, 8, 512 + 2 * PAD, 128), F32)],
        in_specs=[pl.BlockSpec(memory_space=pltpu.HBM)] * 6,
        scratch_shapes=[
            pltpu.VMEM((6, 512, 256), BF16),
            pltpu.VMEM((1, 256), F32),
            pltpu.VMEM((1, 256), F32),
            pltpu.VMEM((256, 1024), BF16),
            pltpu.VMEM((9, 1024), F32),
            pltpu.VMEM((1024, 256), BF16),
            pltpu.SemaphoreType.DMA((11,)),
        ],
        compiler_params=vmem(24),
        name="bottleneck_middle",
    )(strips, scale, shift, we, dw, wp)


def bottleneck_edge(strips, top, bot, expanded, middle, scale, shift, we, dw, wp):
    return pl.pallas_call(
        edge_kernel,
        out_shape=[pieces(8, 8)] + [pieces(8, 4)] * 4,
        scratch_shapes=[pltpu.VMEM((2, 8, 512 + 2 * PAD, 128), F32)],
        compiler_params=vmem(24),
        name="bottleneck_edge",
    )(strips, top, bot, expanded, middle, scale, shift, we, dw, wp)


def normed_of(x, gain):
    center = x - jnp.mean(x, axis=-1, keepdims=True)
    spread = jnp.mean(center * center, axis=-1, keepdims=True)
    return (center * lax.rsqrt(spread + EPSILON) * gain).astype(BF16)


def head_masks(dtype):
    lane = lax.broadcasted_iota(jnp.int32, (1, 128), 1)
    return [(lane // 32 == h).astype(F32).astype(dtype) for h in range(4)]


def attend_and_mix(x, w):
    tokens = x.shape[0]
    masks = head_masks(BF16)
    key_head = lax.broadcasted_iota(jnp.int32, (256, 128), 0) // 64
    lane_head = lax.broadcasted_iota(jnp.int32, (256, 128), 1) // 32
    head_ones = (key_head == lane_head).astype(F32).astype(BF16)
    score_lane = lax.broadcasted_iota(jnp.int32, (64, 256), 1)
    bias = [
        jnp.concatenate([w["bias"][4 * g + h] for h in range(4)], axis=1) * LOG2E
        for g in range(2)
    ]
    normed = normed_of(x, w["gain_a"][...])
    q, k, v = [
        jnp.dot(normed, w["inputs"][:, c * 256 : (c + 1) * 256], preferred_element_type=F32).astype(
            BF16
        )
        for c in range(3)
    ]
    rows = []
    for win in range(tokens // 64):
        at = slice(win * 64, (win + 1) * 64)
        groups = []
        for g in range(2):
            lanes = slice(g * 128, (g + 1) * 128)
            qg, kg, vg = q[at, lanes], k[at, lanes], v[at, lanes]
            keys = jnp.concatenate([kg * masks[h] for h in range(4)], axis=0)
            values = jnp.concatenate([vg * masks[h] for h in range(4)], axis=0)
            values = jnp.concatenate([values, head_ones], axis=1)
            scores = lax.dot_general(
                qg, keys, (((1,), (1,)), ((), ())), preferred_element_type=F32
            )
            scores = scores * (LOG2E * 32**-0.5) + bias[g]
            top = None
            for h in range(4):
                peak = jnp.max(scores[:, h * 64 : (h + 1) * 64], axis=1, keepdims=True)
                top = (
                    jnp.broadcast_to(peak, (64, 256))
                    if top is None
                    else jnp.where(score_lane >= h * 64, peak, top)
                )
            weights = jnp.exp2(scores - top).astype(BF16)
            mixed = jnp.dot(weights, values, preferred_element_type=F32)
            groups.append((mixed[:, :128] * (1.0 / mixed[:, 128:])).astype(BF16))
        rows.append(jnp.concatenate(groups, axis=1))
    combined = jnp.concatenate(rows, axis=0)
    x = x + jnp.dot(combined, w["output"][...], preferred_element_type=F32)
    x = x.astype(BF16).astype(F32)
    normed = normed_of(x, w["gain_m"][...])
    total = jnp.zeros((tokens, 256), F32)
    for c in range(4):
        cols = slice(c * 256, (c + 1) * 256)
        hidden = jnp.dot(normed, w["up"][:, cols], preferred_element_type=F32)
        hidden = twice_gelu(hidden).astype(BF16)
        total = total + jnp.dot(hidden, w["down"][cols, :], preferred_element_type=F32)
    return x + 0.5 * total


NAMES = ("gain_a", "inputs", "output", "bias", "gain_m", "up", "down")


def block_places():
    y = own_y()
    places = []
    for k in range(3):
        n = 3 * y + k
        p = n // 4
        tp = lax.rem(n, 4)
        for s in range(8):
            row = 8 * p + s
            owner = row // 6
            local = row - 6 * owner
            v = jnp.maximum(y - 1, 0)
            m_up = jnp.clip((local - 2 * v) * (v + 1) + tp - (3 - v), 0, 7)
            v = jnp.minimum(y + 1, 3)
            m_down = jnp.clip(local * (4 - v) + tp, 0, 7)
            inside = jnp.logical_and(local >= 1, local <= 4)
            at_mid = jnp.clip(local - 1, 0, 3) * 4 + tp
            at_edge = jnp.where(local == 5, 4, 0) + tp
            places.append((owner, inside, at_mid, at_edge, m_up, m_down))
    return y, places


def block_kernel(half, mid_ref, edge_ref, up_ref, down_ref, *refs):
    w = dict(zip(NAMES, refs))
    refs = refs[len(NAMES) :]
    if half == 1:
        done_ref, out_ref = refs
        out_ref[:, :, 0:4] = done_ref[...]
    else:
        (out_ref,) = refs
    y, places = block_places()
    units = []
    js = slice(4 * half, 4 * half + 4)
    for owner, inside, at_mid, at_edge, m_up, m_down in places:
        mine = jnp.where(inside, mid_ref[at_mid, js].astype(F32), edge_ref[at_edge, js].astype(F32))
        above = up_ref[m_up].astype(F32)
        below = down_ref[m_down].astype(F32)
        units.append(jnp.where(owner == y, mine, jnp.where(owner < y, above, below)))
    windows = [(k, jj, t) for k in range(3) for jj in range(4) for t in range(2)]
    x = jnp.concatenate(
        [units[k * 8 + s][jj, t * 8 : (t + 1) * 8, :] for k, jj, t in windows for s in range(8)],
        axis=0,
    )
    out = attend_and_mix(x, w)
    for k in range(3):
        for jj in range(4):
            first = (k * 4 + jj) * 128
            for s in range(8):
                both = [out[first + t * 64 + s * 8 :][:8] for t in range(2)]
                out_ref[s, k, jj + 4 * half] = jnp.concatenate(both, axis=0).astype(BF16)


def grid_kernel(x_ref, *refs):
    w = dict(zip(NAMES, refs))
    out_ref, flat_ref = refs[len(NAMES) :]

    def slot(k, carry):
        for i in range(8):
            values = x_ref[i, k].astype(F32).reshape(128, 256)
            for half in range(2):
                flat_ref[half, i * 128 : (i + 1) * 128, :] = values[
                    :, half * 128 : (half + 1) * 128
                ]
        windows = []
        for b in range(16):
            at = pl.ds(b, 64, stride=16)
            windows.append(
                jnp.concatenate([flat_ref[half, at, :] for half in range(2)], axis=1)
            )
        out = attend_and_mix(jnp.concatenate(windows, axis=0), w)
        for b in range(16):
            at = pl.ds(b, 64, stride=16)
            for half in range(2):
                flat_ref[half, at, :] = out[
                    b * 64 : (b + 1) * 64, half * 128 : (half + 1) * 128
                ]
        for i in range(8):
            values = jnp.concatenate(
                [flat_ref[half, i * 128 : (i + 1) * 128, :] for half in range(2)], axis=1
            )
            out_ref[pl.ds(i * 8, 8), k] = values.astype(BF16).reshape(8, 16, 256)
        return carry

    lax.fori_loop(0, 3, slot, 0)


def block_section(half, mid, edge, up, down, weights, *done):
    return pl.pallas_call(
        functools.partial(block_kernel, half),
        out_shape=jax.ShapeDtypeStruct((8, 3, 4 if half == 0 else 8, 16, 256), BF16),
        compiler_params=vmem(24),
        name="block_section",
    )(mid, edge, up, down, *weights, *done)


def grid_section(x, weights):
    return pl.pallas_call(
        grid_kernel,
        out_shape=jax.ShapeDtypeStruct((64, 3, 16, 256), BF16),
        scratch_shapes=[pltpu.VMEM((2, 1024, 128), F32)],
        compiler_params=vmem(24),
        name="grid_section",
    )(x, *weights)


def body(
    stem_strips, norm_scale, norm_shift, expand_weight, depth_weight, project_weight,
    block_gain, block_inputs, block_output, block_bias, first_gain, first_up, first_down,
    grid_gain, grid_inputs, grid_output, grid_bias, second_gain, second_up, second_down,
):
    row = lambda a: a.reshape(1, -1)
    both = ("rows", "cols")
    top = lax.ppermute(stem_strips[5:6], both, [(d, d + 1) for d in range(127)])
    bot = lax.ppermute(stem_strips[0:1], both, [(d + 1, d) for d in range(127)])
    weights = (row(norm_scale), row(norm_shift), expand_weight, depth_weight, project_weight)
    middle, expanded = bottleneck_middle(
        *[pltpu.with_memory_space_constraint(a, pltpu.HBM) for a in (stem_strips, *weights)]
    )
    edge, up_l, down_l, up_r, down_r = bottleneck_edge(
        stem_strips, top, bot, expanded, middle, *weights
    )
    up_l, up_r = [lax.ppermute(a, "cols", Y_UP) for a in (up_l, up_r)]
    down_l, down_r = [lax.ppermute(a, "cols", Y_DOWN) for a in (down_l, down_r)]
    block_weights = (
        row(block_gain), block_inputs, block_output, block_bias,
        row(first_gain), first_up, first_down,
    )
    grid_weights = (
        row(grid_gain), grid_inputs, grid_output, grid_bias,
        row(second_gain), second_up, second_down,
    )
    left = block_section(0, middle, edge, up_l, down_l, block_weights)
    sent = block_section(1, middle, edge, up_r, down_r, block_weights, left)
    arrived = lax.all_to_all(sent, "rows", 0, 0, axis_index_groups=CORE_ROWS, tiled=True)
    back = grid_section(arrived, grid_weights)
    landed = lax.all_to_all(back, both, 0, 0, axis_index_groups=CORE_ALL, tiled=True)
    landed = landed.reshape(8, 2, 3, 4, 16, 256).transpose(1, 2, 0, 3, 4, 5)
    return landed.reshape(48, 64, 256)


def solution(mesh):
    return jax.shard_map(
        body,
        mesh=mesh,
        in_specs=(P(("rows", "cols"), None, None),) + (P(),) * 19,
        out_specs=P("rows", "cols", None),
        check_vma=False,
    )
```

time: 152 us -> 135 us (0.89)
  waiting for transfers between devices: 16.6 us -> 3.08 us
  local copies, waits for them, and re-layouts: 9.61 us -> 2.43 us
  starting transfers between devices: 11.8 us -> 16.9 us
    ppermute x2 -> x4, waiting for transfers between devices: 11.8 us -> 3.08 us  [the longest x2 3.07 us: body(): down_l, down_r = [lax.ppermute(a, 'cols', Y_DOWN) for a in (down_l, down_r)]]
    unnamed x40, local copies, waits for them, and re-layouts: 7 us -> 0.13 us
    all_to_all x1, blocking collectives: 35.1 us -> 29 us  [body(): lax.all_to_all(sent, 'rows', 0, 0, axis_index_groups=CORE_ROWS, tiled=True)]
    all_to_all x1, blocking collectives: 28.5 us -> 34.2 us  [body(): lax.all_to_all(back, both, 0, 0, axis_index_groups=CORE_ALL, tiled=True)]
    ppermute x2 -> x4, starting transfers between devices: 5.9 us -> 10.9 us  [the longest x2 8.13 us: body(): up_l, up_r = [lax.ppermute(a, 'cols', Y_UP) for a in (up_l, up_r)]]
    ppermute x1, waiting for transfers between devices: 4 us -> 0.01 us  [body(): bot = lax.ppermute(stem_strips[0:1], both, [(d + 1, d) for d in range(127)])]
    pallas_call x7 -> x5, Pallas kernels: 49.3 us -> 48.9 us  [the longest x1 16.5 us: grid_section(): pl.pallas_call(grid_kernel, out_shape=jax.ShapeDtypeStruct((64, 3, 16, 25...]
  transfers between devices with their start and end apart: 4 -> 6, of which waited for: 4 -> 1; matrix products, arithmetic and copies ran while one was open for 0% -> 0% of each run, Pallas kernels for 0% -> 14%
where the time goes in v3:
time: 135 us
  blocking collectives  63.2 us (47%)
  Pallas kernels  48.9 us (36%)
  starting transfers between devices  16.9 us (13%)
  waiting for transfers between devices  3.08 us (2%)
  local copies, waits for them, and re-layouts  2.43 us (2%)
    all_to_all x1, blocking collectives, body(): lax.all_to_all(back, both, 0, 0, axis_index_groups=CORE_ALL, tiled=True)  34.2 us
    all_to_all x1, blocking collectives, body(): lax.all_to_all(sent, 'rows', 0, 0, axis_index_groups=CORE_ROWS, tiled=True)  29 us
    pallas_call x1, Pallas kernels, grid_section(): pl.pallas_call(grid_kernel, out_shape=jax.ShapeDtypeStruct((64, 3, 16, 25...  16.5 us
    pallas_call x2, Pallas kernels, block_section(): pl.pallas_call(functools.partial(block_kernel, half), out_shape=jax.Shape...  15.4 us
    pallas_call x1, Pallas kernels, bottleneck_middle(): pl.pallas_call(middle_kernel, out_shape=[pieces(16, 8), jax.ShapeDtypeStr...  11.4 us
    ppermute x2, starting transfers between devices, body(): up_l, up_r = [lax.ppermute(a, 'cols', Y_UP) for a in (up_l, up_r)]  8.13 us
    pallas_call x1, Pallas kernels, bottleneck_edge(): pl.pallas_call(edge_kernel, out_shape=[pieces(8, 8)] + [pieces(8, 4)] * 4...  5.53 us
    ppermute x1, starting transfers between devices, body(): top = lax.ppermute(stem_strips[5:6], both, [(d, d + 1) for d in range(127)])  4.56 us
  transfers between devices with their start and end apart: 6, of which 1 were waited for; matrix products, arithmetic and copies ran while one was open for 0% of the time, Pallas kernels for 14%

profile of v3, /device:TPU:0, one launch (start us, length us, event | category | flops | bytes accessed | tf_op | source)
XLA Modules:
  0.0 134.9 jit_solution(8527007393777892079)
XLA Ops:
  0.0 1.1 fusion
  1.1 0.0 copy-start
  1.1 0.0 copy-start.3
  1.1 0.0 copy-start.4
  1.1 0.0 copy-start.11
  1.1 0.0 copy-start.14
  1.1 0.0 copy-start.15
  1.1 1.4 %collective-permute-start.1 = (bf16[1,512,256]{2,1,0:T(8,128)(2,1)S(1)}, bf16[1,512,256]{2,1,0:T(8,128)(2,1)S(1)}, u32[]{:S(2)}, u32[]{:S(2)}) collective-permute-start(bf16[1,512,256]{2,1,0:T(8,128)(2,1)S(1)} %get-tuple-element.19), channel_id=1, source_target_pairs={{1,0},{2,1},{3,2},{4,3},{5,4},{6,5},{7,6},{8,7},{9,8},{10,9},{11,1... | collective-permute-start | bytes 786440 | tf_op jit(solution)/shard_map/ppermute | solution.py:385
  2.6 4.6 %collective-permute-start = (bf16[1,512,256]{2,1,0:T(8,128)(2,1)S(1)}, bf16[1,512,256]{2,1,0:T(8,128)(2,1)S(1)}, u32[]{:S(2)}, u32[]{:S(2)}) collective-permute-start(bf16[1,512,256]{2,1,0:T(8,128)(2,1)S(1)} %get-tuple-element.20), channel_id=1, source_target_pairs={{0,1},{1,2},{2,3},{3,4},{4,5},{5,6},{6,7},{7,8},{8,9},{9,10},{10,1... | collective-permute-start | bytes 786440 | tf_op jit(solution)/shard_map/ppermute | solution.py:384
  7.1 11.4 %bottleneck_middle.1 = (bf16[16,8,16,256]{3,2,1,0:T(8,128)(2,1)S(1)}, f32[6,8,528,128]{3,2,1,0:T(8,128)S(1)}) custom-call(bf16[6,512,256]{2,1,0:T(8,128)(2,1)} %x_ref.1, f32[1,256]{1,0:T(1,128)} %bitcast.10, f32[1,256]{1,0:T(1,128)} %bitcast.12, bf16[256,1024]{1,0:T(8,128)(2,1)} %we_ref.1, f32[9,1024]{1,0:T(8,128)} %dw_ref.1, bf16[1024,256]{1,0:T(8,128)(2,1)} %wp_ref.1), custom_call_target="tpu_custom_call" | custom-call | tf_op jit(solution)/shard_map/bottleneck_middle/pallas_call | solution.py:173
  18.6 0.0 collective-permute-done.1.bot_ref
  18.6 0.0 collective-permute-done.top_ref
  18.6 0.0 copy-done
  18.6 0.0 copy-done.3
  18.6 0.0 copy-done.4
  18.6 0.0 copy-done.11
  18.7 0.0 copy-done.14
  18.7 0.0 copy-done.15
  18.7 0.0 copy-start.1
  18.7 0.0 copy-start.2
  18.7 0.0 copy-start.5
  18.7 0.0 copy-start.6
  18.7 0.0 copy-start.9
  18.7 0.0 copy-start.16
  18.7 0.0 copy-start.17
  18.8 5.5 %bottleneck_edge.1 = (bf16[8,8,16,256]{3,2,1,0:T(8,128)(2,1)S(1)}, bf16[8,4,16,256]{3,2,1,0:T(8,128)(2,1)S(1)}, bf16[8,4,16,256]{3,2,1,0:T(8,128)(2,1)S(1)}, bf1...) custom-call(bf16[6,512,256]{2,1,0:T(8,128)(2,1)S(1)} %copy-done, ...), custom_call_target="tpu_custom_call" | custom-call | tf_op jit(solution)/shard_map/bottleneck_edge/pallas_call | solution.py:192
  24.3 3.6 %collective-permute-start.4 = (bf16[8,4,16,256]{3,2,1,0:T(8,128)(2,1)S(1)}, bf16[8,4,16,256]{3,2,1,0:T(8,128)(2,1)S(1)}, u32[]{:S(2)}, u32[]{:S(2)}) collective-permute-start(bf16[8,4,16,256]{3,2,1,0:T(8,128)(2,1)S(1)} %get-tuple-element.17), channel_id=1, source_target_pairs={{0,1},{1,2},{2,3},{4,5},{5,6},{6,7},{8,9},{9,10},{10,11},{12,13},{... | collective-permute-start | bytes 786440 | tf_op jit(solution)/shard_map/ppermute | solution.py:393
  27.9 1.3 collective-permute-start.5
  29.2 4.6 %collective-permute-start.2 = (bf16[8,4,16,256]{3,2,1,0:T(8,128)(2,1)S(1)}, bf16[8,4,16,256]{3,2,1,0:T(8,128)(2,1)S(1)}, u32[]{:S(2)}, u32[]{:S(2)}) collective-permute-start(bf16[8,4,16,256]{3,2,1,0:T(8,128)(2,1)S(1)} %get-tuple-element.15), channel_id=1, source_target_pairs={{0,1},{1,2},{2,3},{4,5},{5,6},{6,7},{8,9},{9,10},{10,11},{12,13},{... | collective-permute-start | bytes 786440 | tf_op jit(solution)/shard_map/ppermute | solution.py:393
  33.7 1.5 %collective-permute-start.3 = (bf16[8,4,16,256]{3,2,1,0:T(8,128)(2,1)S(1)}, bf16[8,4,16,256]{3,2,1,0:T(8,128)(2,1)S(1)}, u32[]{:S(2)}, u32[]{:S(2)}) collective-permute-start(bf16[8,4,16,256]{3,2,1,0:T(8,128)(2,1)S(1)} %get-tuple-element.16), channel_id=1, source_target_pairs={{1,0},{2,1},{3,2},{5,4},{6,5},{7,6},{9,8},{10,9},{11,10},{13,12},{... | collective-permute-start | bytes 786440 | tf_op jit(solution)/shard_map/ppermute | solution.py:394
  35.2 0.0 collective-permute-done.4.up_ref
  35.2 3.1 %collective-permute-done.5.down_ref = bf16[8,4,16,256]{3,2,1,0:T(8,128)(2,1)S(1)} collective-permute-done((bf16[8,4,16,256]{3,2,1,0:T(8,128)(2,1)S(1)}, bf16[8,4,16,256]{3,2,1,0:T(8,128)(2,1)S(1)}, u32[]{:S(2)}, u32[]{:S(2)}) %collective-permute-start.5) | collective-permute-done | bytes 262176 | tf_op jit(solution)/shard_map/ppermute | solution.py:394
  38.3 0.0 copy-done.1
  38.4 7.6 %block_section.2.refs_7_ = bf16[8,3,4,16,256]{4,3,2,1,0:T(8,128)(2,1)S(1)} custom-call(bf16[16,8,16,256]{3,2,1,0:T(8,128)(2,1)S(1)} %get-tuple-element.12.mid_ref, bf16[8,8,16,256]{3,2,1,0:T(8,128)(2,1)S(1)} %get-tuple-element.14.edge_ref, bf16[8,4,16,256]{3,2,1,0:T(8,128)(2,1)S(1)} %collective-permute-done.4.up_ref, ...), custom_call_target="tpu_custom_call" | custom-call | tf_op jit(solution)/shard_map/block_section/pallas_call | solution.py:359
  45.9 0.0 collective-permute-done.2.up_ref
  45.9 0.0 collective-permute-done.3.down_ref
  46.0 7.9 %block_section.3 = bf16[8,3,8,16,256]{4,3,2,1,0:T(8,128)(2,1)S(1)} custom-call(bf16[16,8,16,256]{3,2,1,0:T(8,128)(2,1)S(1)} %get-tuple-element.12.mid_ref, bf16[8,8,16,256]{3,2,1,0:T(8,128)(2,1)S(1)} %get-tuple-element.14.edge_ref, bf16[8,4,16,256]{3,2,1,0:T(8,128)(2,1)S(1)} %collective-permute-done.2.up_ref, ...), custom_call_target="tpu_custom_call" | custom-call | tf_op jit(solution)/shard_map/block_section/pallas_call | solution.py:359
  53.8 0.0 copy-start.7
  53.8 0.0 copy-start.8
  53.9 0.0 copy-start.10
  53.9 0.0 copy-start.12
  53.9 0.0 copy-start.13
  53.9 0.0 copy-start.18
  53.9 0.0 copy-start.19
  53.9 29.0 %all_to_all.10.x_ref = bf16[8,3,8,16,256]{4,3,2,1,0:T(8,128)(2,1)S(1)} all-to-all(bf16[8,3,8,16,256]{4,3,2,1,0:T(8,128)(2,1)S(1)} %block_section.3), channel_id=1, replica_groups={{0,16,32,48,64,80,96,112},{8,24,40,56,72,88,104,120},{1,17,33,49,65,81,..., dimensions={0} | all-to-all | bytes 3145728 | tf_op jit(solution)/shard_map/all_to_all | solution.py:405
  82.9 16.5 %grid_section.1 = bf16[64,3,16,256]{3,2,1,0:T(8,128)(2,1)S(1)} custom-call(bf16[8,3,8,16,256]{4,3,2,1,0:T(8,128)(2,1)S(1)} %all_to_all.10.x_ref, f32[1,256]{1,0:T(1,128)S(1)} %bitcast.18, bf16[256,768]{1,0:T(8,128)(2,1)S(1)} %copy-done.10, bf16[256,256]{1,0:T(8,128)(2,1)S(1)} %copy-done.13, f32[8,64,64]{2,1,0:T(8,128)S(1)} %copy-done.12, ...), custom_call_target="tpu_custom_call" | custom-call | tf_op jit(solution)/shard_map/grid_section/pallas_call | solution.py:368
  99.5 34.2 %all_to_all.11 = bf16[64,3,16,256]{3,2,1,0:T(8,128)(2,1)S(1)} all-to-all(bf16[64,3,16,256]{3,2,1,0:T(8,128)(2,1)S(1)} %grid_section.1), channel_id=1, replica_groups={{0,1,2,3,4,5,6,7,16,17,18,19,20,21,22,23,32,33,34,35,36,37,38,39,48,49,..., dimensions={0} | all-to-all | bytes 3145728 | tf_op jit(solution)/shard_map/all_to_all | solution.py:407
  133.7 1.2 copy.21
  (13 shorter events, 0.0 us)
Async XLA Ops:
  1.1 17.5 %copy-start = (bf16[6,512,256]{2,1,0:T(8,128)(2,1)S(1)}, bf16[6,512,256]{2,1,0:T(8,128)(2,1)}, u32[]{:S(2)}) copy-start(bf16[6,512,256]{2,1,0:T(8,128)(2,1)} %x_ref.1) | copy-start | bytes 4718596
  1.1 17.5 %copy-start.3 = (bf16[256,1024]{1,0:T(8,128)(2,1)S(1)}, bf16[256,1024]{1,0:T(8,128)(2,1)}, u32[]{:S(2)}) copy-start(bf16[256,1024]{1,0:T(8,128)(2,1)} %we_ref.1) | copy-start | bytes 1572868
  1.1 17.5 %copy-start.4 = (bf16[1024,256]{1,0:T(8,128)(2,1)S(1)}, bf16[1024,256]{1,0:T(8,128)(2,1)}, u32[]{:S(2)}) copy-start(bf16[1024,256]{1,0:T(8,128)(2,1)} %wp_ref.1) | copy-start | bytes 1572868
  1.1 17.5 %copy-start.11 = (f32[9,1024]{1,0:T(8,128)S(1)}, f32[9,1024]{1,0:T(8,128)}, u32[]{:S(2)}) copy-start(f32[9,1024]{1,0:T(8,128)} %dw_ref.1) | copy-start | bytes 110596
  1.1 17.5 %copy-start.14 = (f32[256]{0:T(256)S(1)}, f32[256]{0:T(256)}, u32[]{:S(2)}) copy-start(f32[256]{0:T(256)} %param.21) | copy-start | bytes 3076
  1.1 17.5 %copy-start.15 = (f32[256]{0:T(256)S(1)}, f32[256]{0:T(256)}, u32[]{:S(2)}) copy-start(f32[256]{0:T(256)} %param.22) | copy-start | bytes 3076
  1.1 17.5 %collective-permute-start.1 = (bf16[1,512,256]{2,1,0:T(8,128)(2,1)S(1)}, bf16[1,512,256]{2,1,0:T(8,128)(2,1)S(1)}, u32[]{:S(2)}, u32[]{:S(2)}) collective-permute-start(bf16[1,512,256]{2,1,0:T(8,128)(2,1)S(1)} %get-tuple-element.19), channel_id=1, source_target_pairs={{1,0},{2,1},{3,2},{4,3},{5,4},{6,5},{7,6},{8,7},{9,8},{10,9},{11,1... | collective-permute-start | bytes 786440 | tf_op jit(solution)/shard_map/ppermute | solution.py:385
  2.6 16.0 %collective-permute-start = (bf16[1,512,256]{2,1,0:T(8,128)(2,1)S(1)}, bf16[1,512,256]{2,1,0:T(8,128)(2,1)S(1)}, u32[]{:S(2)}, u32[]{:S(2)}) collective-permute-start(bf16[1,512,256]{2,1,0:T(8,128)(2,1)S(1)} %get-tuple-element.20), channel_id=1, source_target_pairs={{0,1},{1,2},{2,3},{3,4},{4,5},{5,6},{6,7},{7,8},{8,9},{9,10},{10,1... | collective-permute-start | bytes 786440 | tf_op jit(solution)/shard_map/ppermute | solution.py:384
  18.7 19.6 %copy-start.1 = (bf16[256,1024]{1,0:T(8,128)(2,1)S(1)}, bf16[256,1024]{1,0:T(8,128)(2,1)}, u32[]{:S(2)}) copy-start(bf16[256,1024]{1,0:T(8,128)(2,1)} %refs_5_.4) | copy-start | bytes 1572868
  18.7 19.6 %copy-start.2 = (bf16[1024,256]{1,0:T(8,128)(2,1)S(1)}, bf16[1024,256]{1,0:T(8,128)(2,1)}, u32[]{:S(2)}) copy-start(bf16[1024,256]{1,0:T(8,128)(2,1)} %refs_6_.4) | copy-start | bytes 1572868
  18.7 19.6 %copy-start.5 = (bf16[256,768]{1,0:T(8,128)(2,1)S(1)}, bf16[256,768]{1,0:T(8,128)(2,1)}, u32[]{:S(2)}) copy-start(bf16[256,768]{1,0:T(8,128)(2,1)} %refs_1_.4) | copy-start | bytes 1179652
  18.7 19.6 %copy-start.6 = (f32[8,64,64]{2,1,0:T(8,128)S(1)}, f32[8,64,64]{2,1,0:T(8,128)}, u32[]{:S(2)}) copy-start(f32[8,64,64]{2,1,0:T(8,128)} %refs_3_.4) | copy-start | bytes 393220
  18.7 19.6 %copy-start.9 = (bf16[256,256]{1,0:T(8,128)(2,1)S(1)}, bf16[256,256]{1,0:T(8,128)(2,1)}, u32[]{:S(2)}) copy-start(bf16[256,256]{1,0:T(8,128)(2,1)} %refs_2_.4) | copy-start | bytes 393220
  18.7 19.6 %copy-start.16 = (f32[256]{0:T(256)S(1)}, f32[256]{0:T(256)}, u32[]{:S(2)}) copy-start(f32[256]{0:T(256)} %param.26) | copy-start | bytes 3076
  18.7 19.6 %copy-start.17 = (f32[256]{0:T(256)S(1)}, f32[256]{0:T(256)}, u32[]{:S(2)}) copy-start(f32[256]{0:T(256)} %param.30) | copy-start | bytes 3076
  24.3 10.9 %collective-permute-start.4 = (bf16[8,4,16,256]{3,2,1,0:T(8,128)(2,1)S(1)}, bf16[8,4,16,256]{3,2,1,0:T(8,128)(2,1)S(1)}, u32[]{:S(2)}, u32[]{:S(2)}) collective-permute-start(bf16[8,4,16,256]{3,2,1,0:T(8,128)(2,1)S(1)} %get-tuple-element.17), channel_id=1, source_target_pairs={{0,1},{1,2},{2,3},{4,5},{5,6},{6,7},{8,9},{9,10},{10,11},{12,13},{... | collective-permute-start | bytes 786440 | tf_op jit(solution)/shard_map/ppermute | solution.py:393
  27.9 10.4 %collective-permute-start.5 = (bf16[8,4,16,256]{3,2,1,0:T(8,128)(2,1)S(1)}, bf16[8,4,16,256]{3,2,1,0:T(8,128)(2,1)S(1)}, u32[]{:S(2)}, u32[]{:S(2)}) collective-permute-start(bf16[8,4,16,256]{3,2,1,0:T(8,128)(2,1)S(1)} %get-tuple-element.18), channel_id=1, source_target_pairs={{1,0},{2,1},{3,2},{5,4},{6,5},{7,6},{9,8},{10,9},{11,10},{13,12},{... | collective-permute-start | bytes 786440 | tf_op jit(solution)/shard_map/ppermute | solution.py:394
  29.2 16.8 %collective-permute-start.2 = (bf16[8,4,16,256]{3,2,1,0:T(8,128)(2,1)S(1)}, bf16[8,4,16,256]{3,2,1,0:T(8,128)(2,1)S(1)}, u32[]{:S(2)}, u32[]{:S(2)}) collective-permute-start(bf16[8,4,16,256]{3,2,1,0:T(8,128)(2,1)S(1)} %get-tuple-element.15), channel_id=1, source_target_pairs={{0,1},{1,2},{2,3},{4,5},{5,6},{6,7},{8,9},{9,10},{10,11},{12,13},{... | collective-permute-start | bytes 786440 | tf_op jit(solution)/shard_map/ppermute | solution.py:393
  33.7 12.2 %collective-permute-start.3 = (bf16[8,4,16,256]{3,2,1,0:T(8,128)(2,1)S(1)}, bf16[8,4,16,256]{3,2,1,0:T(8,128)(2,1)S(1)}, u32[]{:S(2)}, u32[]{:S(2)}) collective-permute-start(bf16[8,4,16,256]{3,2,1,0:T(8,128)(2,1)S(1)} %get-tuple-element.16), channel_id=1, source_target_pairs={{1,0},{2,1},{3,2},{5,4},{6,5},{7,6},{9,8},{10,9},{11,10},{13,12},{... | collective-permute-start | bytes 786440 | tf_op jit(solution)/shard_map/ppermute | solution.py:394
  53.8 29.0 %copy-start.7 = (bf16[256,1024]{1,0:T(8,128)(2,1)S(1)}, bf16[256,1024]{1,0:T(8,128)(2,1)}, u32[]{:S(2)}) copy-start(bf16[256,1024]{1,0:T(8,128)(2,1)} %refs_5_.5) | copy-start | bytes 1572868
  53.8 29.0 %copy-start.8 = (bf16[1024,256]{1,0:T(8,128)(2,1)S(1)}, bf16[1024,256]{1,0:T(8,128)(2,1)}, u32[]{:S(2)}) copy-start(bf16[1024,256]{1,0:T(8,128)(2,1)} %refs_6_.5) | copy-start | bytes 1572868
  53.9 29.0 %copy-start.10 = (bf16[256,768]{1,0:T(8,128)(2,1)S(1)}, bf16[256,768]{1,0:T(8,128)(2,1)}, u32[]{:S(2)}) copy-start(bf16[256,768]{1,0:T(8,128)(2,1)} %refs_1_.5) | copy-start | bytes 1179652
  53.9 29.0 %copy-start.12 = (f32[8,64,64]{2,1,0:T(8,128)S(1)}, f32[8,64,64]{2,1,0:T(8,128)}, u32[]{:S(2)}) copy-start(f32[8,64,64]{2,1,0:T(8,128)} %refs_3_.5) | copy-start | bytes 393220
  53.9 29.0 %copy-start.13 = (bf16[256,256]{1,0:T(8,128)(2,1)S(1)}, bf16[256,256]{1,0:T(8,128)(2,1)}, u32[]{:S(2)}) copy-start(bf16[256,256]{1,0:T(8,128)(2,1)} %refs_2_.5) | copy-start | bytes 393220
  53.9 29.0 %copy-start.18 = (f32[256]{0:T(256)S(1)}, f32[256]{0:T(256)}, u32[]{:S(2)}) copy-start(f32[256]{0:T(256)} %param.33) | copy-start | bytes 3076
  53.9 29.0 %copy-start.19 = (f32[256]{0:T(256)S(1)}, f32[256]{0:T(256)}, u32[]{:S(2)}) copy-start(f32[256]{0:T(256)} %param.37) | copy-start | bytes 3076

commit v4 on v3

--- a/solution.py
+++ b/solution.py
@@ -16,8 +16,10 @@
 
 CORE_ROWS = [[core + 2 * i for i in range(8)] for core in range(2)]
 CORE_ALL = [[(core + 2 * i) * 8 + c for i in range(8) for c in range(8)] for core in range(2)]
-Y_UP = [(c, c + 1) for c in range(7) if c % 4 != 3]
-Y_DOWN = [(c + 1, c) for c in range(7) if c % 4 != 3]
+Y_UP = [(c, c // 4 * 4 + (c + 1) % 4) for c in range(8)]
+Y_DOWN = [(b, a) for a, b in Y_UP]
+STRIP_DOWN = [(d, (d + 1) % 128) for d in range(128)]
+STRIP_UP = [(b, a) for a, b in STRIP_DOWN]
 
 
 def twice_gelu(x):
@@ -381,8 +383,8 @@
 ):
     row = lambda a: a.reshape(1, -1)
     both = ("rows", "cols")
-    top = lax.ppermute(stem_strips[5:6], both, [(d, d + 1) for d in range(127)])
-    bot = lax.ppermute(stem_strips[0:1], both, [(d + 1, d) for d in range(127)])
+    top = lax.ppermute(stem_strips[5:6], both, STRIP_DOWN)
+    bot = lax.ppermute(stem_strips[0:1], both, STRIP_UP)
     weights = (row(norm_scale), row(norm_shift), expand_weight, depth_weight, project_weight)
     middle, expanded = bottleneck_middle(
         *[pltpu.with_memory_space_constraint(a, pltpu.HBM) for a in (stem_strips, *weights)]

time: 135 us -> 128 us (0.948)
  blocking collectives: 63.2 us -> 59.1 us
  starting transfers between devices: 16.9 us -> 15 us
    ppermute x2, starting transfers between devices: 8.13 us -> 0.26 us  [body(): up_l, up_r = [lax.ppermute(a, 'cols', Y_UP) for a in (up_l, up_r)]]
    ppermute x2, starting transfers between devices: 2.76 us -> 6.46 us  [body(): down_l, down_r = [lax.ppermute(a, 'cols', Y_DOWN) for a in (down_l, down_r)]]
    ppermute x2, waiting for transfers between devices: 3.07 us -> 0.01 us  [body(): down_l, down_r = [lax.ppermute(a, 'cols', Y_DOWN) for a in (down_l, down_r)]]
    all_to_all x1, blocking collectives: 29 us -> 26.6 us  [body(): lax.all_to_all(sent, 'rows', 0, 0, axis_index_groups=CORE_ROWS, tiled=True)]
    ppermute x2, starting transfers between devices: 5.99 us -> 8.28 us  [the longest x1 8.28 us: body(): bot = lax.ppermute(stem_strips[0:1], both, STRIP_UP)]
    ppermute x2, waiting for transfers between devices: 0.01 us -> 2.12 us  [body(): up_l, up_r = [lax.ppermute(a, 'cols', Y_UP) for a in (up_l, up_r)]]
    all_to_all x1, blocking collectives: 34.2 us -> 32.6 us  [body(): lax.all_to_all(back, both, 0, 0, axis_index_groups=CORE_ALL, tiled=True)]
  transfers between devices with their start and end apart: 6 -> 6, of which waited for: 1 -> 1; matrix products, arithmetic and copies ran while one was open for 0% -> 0% of each run, Pallas kernels for 14% -> 15%
where the time goes in v4:
time: 128 us
  blocking collectives  59.1 us (46%)
  Pallas kernels  48.9 us (38%)
  starting transfers between devices  15 us (12%)
  local copies, waits for them, and re-layouts  2.43 us (2%)
  waiting for transfers between devices  2.13 us (2%)
    all_to_all x1, blocking collectives, body(): lax.all_to_all(back, both, 0, 0, axis_index_groups=CORE_ALL, tiled=True)  32.6 us
    all_to_all x1, blocking collectives, body(): lax.all_to_all(sent, 'rows', 0, 0, axis_index_groups=CORE_ROWS, tiled=True)  26.6 us
    pallas_call x1, Pallas kernels, grid_section(): pl.pallas_call(grid_kernel, out_shape=jax.ShapeDtypeStruct((64, 3, 16, 25...  16.5 us
    pallas_call x2, Pallas kernels, block_section(): pl.pallas_call(functools.partial(block_kernel, half), out_shape=jax.Shape...  15.4 us
    pallas_call x1, Pallas kernels, bottleneck_middle(): pl.pallas_call(middle_kernel, out_shape=[pieces(16, 8), jax.ShapeDtypeStr...  11.4 us
    ppermute x1, starting transfers between devices, body(): bot = lax.ppermute(stem_strips[0:1], both, STRIP_UP)  8.28 us
    ppermute x2, starting transfers between devices, body(): down_l, down_r = [lax.ppermute(a, 'cols', Y_DOWN) for a in (down_l, down_r)]  6.46 us
    pallas_call x1, Pallas kernels, bottleneck_edge(): pl.pallas_call(edge_kernel, out_shape=[pieces(8, 8)] + [pieces(8, 4)] * 4...  5.53 us
  transfers between devices with their start and end apart: 6, of which 1 were waited for; matrix products, arithmetic and copies ran while one was open for 0% of the time, Pallas kernels for 15%

profile of v4, /device:TPU:0, one launch (start us, length us, event | category | flops | bytes accessed | tf_op | source)
XLA Modules:
  0.0 128.0 jit_solution(6276736151551461779)
XLA Ops:
  0.0 1.1 fusion
  1.1 0.0 copy-start
  1.1 0.0 copy-start.3
  1.1 0.0 copy-start.4
  1.1 0.0 copy-start.11
  1.1 0.0 copy-start.14
  1.1 0.0 copy-start.15
  1.1 8.3 %collective-permute-start.1 = (bf16[1,512,256]{2,1,0:T(8,128)(2,1)S(1)}, bf16[1,512,256]{2,1,0:T(8,128)(2,1)S(1)}, u32[]{:S(2)}, u32[]{:S(2)}) collective-permute-start(bf16[1,512,256]{2,1,0:T(8,128)(2,1)S(1)} %get-tuple-element.19), channel_id=1, source_target_pairs={{1,0},{2,1},{3,2},{4,3},{5,4},{6,5},{7,6},{8,7},{9,8},{10,9},{11,1... | collective-permute-start | bytes 786440 | tf_op jit(solution)/shard_map/ppermute | solution.py:387
  9.4 0.0 collective-permute-start
  9.4 11.4 %bottleneck_middle.1 = (bf16[16,8,16,256]{3,2,1,0:T(8,128)(2,1)S(1)}, f32[6,8,528,128]{3,2,1,0:T(8,128)S(1)}) custom-call(bf16[6,512,256]{2,1,0:T(8,128)(2,1)} %x_ref.1, f32[1,256]{1,0:T(1,128)} %bitcast.10, f32[1,256]{1,0:T(1,128)} %bitcast.12, bf16[256,1024]{1,0:T(8,128)(2,1)} %we_ref.1, f32[9,1024]{1,0:T(8,128)} %dw_ref.1, bf16[1024,256]{1,0:T(8,128)(2,1)} %wp_ref.1), custom_call_target="tpu_custom_call" | custom-call | tf_op jit(solution)/shard_map/bottleneck_middle/pallas_call | solution.py:175
  20.9 0.0 collective-permute-done.1.bot_ref
  20.9 0.0 collective-permute-done.top_ref
  20.9 0.0 copy-done
  20.9 0.0 copy-done.3
  20.9 0.0 copy-done.4
  20.9 0.0 copy-done.11
  20.9 0.0 copy-done.14
  20.9 0.0 copy-done.15
  20.9 0.0 copy-start.1
  21.0 0.0 copy-start.2
  21.0 0.0 copy-start.5
  21.0 0.0 copy-start.6
  21.0 0.0 copy-start.9
  21.0 0.0 copy-start.16
  21.0 0.0 copy-start.17
  21.0 5.5 %bottleneck_edge.1 = (bf16[8,8,16,256]{3,2,1,0:T(8,128)(2,1)S(1)}, bf16[8,4,16,256]{3,2,1,0:T(8,128)(2,1)S(1)}, bf16[8,4,16,256]{3,2,1,0:T(8,128)(2,1)S(1)}, bf1...) custom-call(bf16[6,512,256]{2,1,0:T(8,128)(2,1)S(1)} %copy-done, ...), custom_call_target="tpu_custom_call" | custom-call | tf_op jit(solution)/shard_map/bottleneck_edge/pallas_call | solution.py:194
  26.6 0.3 collective-permute-start.4
  26.8 3.2 %collective-permute-start.5 = (bf16[8,4,16,256]{3,2,1,0:T(8,128)(2,1)S(1)}, bf16[8,4,16,256]{3,2,1,0:T(8,128)(2,1)S(1)}, u32[]{:S(2)}, u32[]{:S(2)}) collective-permute-start(bf16[8,4,16,256]{3,2,1,0:T(8,128)(2,1)S(1)} %get-tuple-element.18), channel_id=1, source_target_pairs={{1,0},{2,1},{3,2},{0,3},{5,4},{6,5},{7,6},{4,7},{9,8},{10,9},{11,1... | collective-permute-start | bytes 786440 | tf_op jit(solution)/shard_map/ppermute | solution.py:396
  30.1 0.0 collective-permute-start.2
  30.1 3.2 %collective-permute-start.3 = (bf16[8,4,16,256]{3,2,1,0:T(8,128)(2,1)S(1)}, bf16[8,4,16,256]{3,2,1,0:T(8,128)(2,1)S(1)}, u32[]{:S(2)}, u32[]{:S(2)}) collective-permute-start(bf16[8,4,16,256]{3,2,1,0:T(8,128)(2,1)S(1)} %get-tuple-element.16), channel_id=1, source_target_pairs={{1,0},{2,1},{3,2},{0,3},{5,4},{6,5},{7,6},{4,7},{9,8},{10,9},{11,1... | collective-permute-start | bytes 786440 | tf_op jit(solution)/shard_map/ppermute | solution.py:396
  33.3 2.1 %collective-permute-done.4.up_ref = bf16[8,4,16,256]{3,2,1,0:T(8,128)(2,1)S(1)} collective-permute-done((bf16[8,4,16,256]{3,2,1,0:T(8,128)(2,1)S(1)}, bf16[8,4,16,256]{3,2,1,0:T(8,128)(2,1)S(1)}, u32[]{:S(2)}, u32[]{:S(2)}) %collective-permute-start.4) | collective-permute-done | bytes 262176 | tf_op jit(solution)/shard_map/ppermute | solution.py:395
  35.4 0.0 collective-permute-done.5.down_ref
  35.5 7.6 %block_section.2.refs_7_ = bf16[8,3,4,16,256]{4,3,2,1,0:T(8,128)(2,1)S(1)} custom-call(bf16[16,8,16,256]{3,2,1,0:T(8,128)(2,1)S(1)} %get-tuple-element.12.mid_ref, bf16[8,8,16,256]{3,2,1,0:T(8,128)(2,1)S(1)} %get-tuple-element.14.edge_ref, bf16[8,4,16,256]{3,2,1,0:T(8,128)(2,1)S(1)} %collective-permute-done.4.up_ref, ...), custom_call_target="tpu_custom_call" | custom-call | tf_op jit(solution)/shard_map/block_section/pallas_call | solution.py:361
  43.0 0.0 collective-permute-done.2.up_ref
  43.1 0.0 collective-permute-done.3.down_ref
  43.1 7.9 %block_section.3 = bf16[8,3,8,16,256]{4,3,2,1,0:T(8,128)(2,1)S(1)} custom-call(bf16[16,8,16,256]{3,2,1,0:T(8,128)(2,1)S(1)} %get-tuple-element.12.mid_ref, bf16[8,8,16,256]{3,2,1,0:T(8,128)(2,1)S(1)} %get-tuple-element.14.edge_ref, bf16[8,4,16,256]{3,2,1,0:T(8,128)(2,1)S(1)} %collective-permute-done.2.up_ref, ...), custom_call_target="tpu_custom_call" | custom-call | tf_op jit(solution)/shard_map/block_section/pallas_call | solution.py:361
  50.9 0.0 copy-start.7
  51.0 0.0 copy-start.8
  51.0 0.0 copy-start.10
  51.0 0.0 copy-start.12
  51.0 0.0 copy-start.13
  51.0 0.0 copy-start.18
  51.0 0.0 copy-start.19
  51.0 26.6 %all_to_all.10.x_ref = bf16[8,3,8,16,256]{4,3,2,1,0:T(8,128)(2,1)S(1)} all-to-all(bf16[8,3,8,16,256]{4,3,2,1,0:T(8,128)(2,1)S(1)} %block_section.3), channel_id=1, replica_groups={{0,16,32,48,64,80,96,112},{8,24,40,56,72,88,104,120},{1,17,33,49,65,81,..., dimensions={0} | all-to-all | bytes 3145728 | tf_op jit(solution)/shard_map/all_to_all | solution.py:407
  77.6 0.0 copy-done.7
  77.6 16.5 %grid_section.1 = bf16[64,3,16,256]{3,2,1,0:T(8,128)(2,1)S(1)} custom-call(bf16[8,3,8,16,256]{4,3,2,1,0:T(8,128)(2,1)S(1)} %all_to_all.10.x_ref, f32[1,256]{1,0:T(1,128)S(1)} %bitcast.18, bf16[256,768]{1,0:T(8,128)(2,1)S(1)} %copy-done.10, bf16[256,256]{1,0:T(8,128)(2,1)S(1)} %copy-done.13, f32[8,64,64]{2,1,0:T(8,128)S(1)} %copy-done.12, ...), custom_call_target="tpu_custom_call" | custom-call | tf_op jit(solution)/shard_map/grid_section/pallas_call | solution.py:370
  94.2 32.6 %all_to_all.11 = bf16[64,3,16,256]{3,2,1,0:T(8,128)(2,1)S(1)} all-to-all(bf16[64,3,16,256]{3,2,1,0:T(8,128)(2,1)S(1)} %grid_section.1), channel_id=1, replica_groups={{0,1,2,3,4,5,6,7,16,17,18,19,20,21,22,23,32,33,34,35,36,37,38,39,48,49,..., dimensions={0} | all-to-all | bytes 3145728 | tf_op jit(solution)/shard_map/all_to_all | solution.py:409
  126.7 1.2 copy.21
  (13 shorter events, 0.0 us)
Async XLA Ops:
  1.1 19.8 %copy-start = (bf16[6,512,256]{2,1,0:T(8,128)(2,1)S(1)}, bf16[6,512,256]{2,1,0:T(8,128)(2,1)}, u32[]{:S(2)}) copy-start(bf16[6,512,256]{2,1,0:T(8,128)(2,1)} %x_ref.1) | copy-start | bytes 4718596
  1.1 19.8 %copy-start.3 = (bf16[256,1024]{1,0:T(8,128)(2,1)S(1)}, bf16[256,1024]{1,0:T(8,128)(2,1)}, u32[]{:S(2)}) copy-start(bf16[256,1024]{1,0:T(8,128)(2,1)} %we_ref.1) | copy-start | bytes 1572868
  1.1 19.8 %copy-start.4 = (bf16[1024,256]{1,0:T(8,128)(2,1)S(1)}, bf16[1024,256]{1,0:T(8,128)(2,1)}, u32[]{:S(2)}) copy-start(bf16[1024,256]{1,0:T(8,128)(2,1)} %wp_ref.1) | copy-start | bytes 1572868
  1.1 19.8 %copy-start.11 = (f32[9,1024]{1,0:T(8,128)S(1)}, f32[9,1024]{1,0:T(8,128)}, u32[]{:S(2)}) copy-start(f32[9,1024]{1,0:T(8,128)} %dw_ref.1) | copy-start | bytes 110596
  1.1 19.8 %copy-start.14 = (f32[256]{0:T(256)S(1)}, f32[256]{0:T(256)}, u32[]{:S(2)}) copy-start(f32[256]{0:T(256)} %param.21) | copy-start | bytes 3076
  1.1 19.8 %copy-start.15 = (f32[256]{0:T(256)S(1)}, f32[256]{0:T(256)}, u32[]{:S(2)}) copy-start(f32[256]{0:T(256)} %param.22) | copy-start | bytes 3076
  1.1 19.7 %collective-permute-start.1 = (bf16[1,512,256]{2,1,0:T(8,128)(2,1)S(1)}, bf16[1,512,256]{2,1,0:T(8,128)(2,1)S(1)}, u32[]{:S(2)}, u32[]{:S(2)}) collective-permute-start(bf16[1,512,256]{2,1,0:T(8,128)(2,1)S(1)} %get-tuple-element.19), channel_id=1, source_target_pairs={{1,0},{2,1},{3,2},{4,3},{5,4},{6,5},{7,6},{8,7},{9,8},{10,9},{11,1... | collective-permute-start | bytes 786440 | tf_op jit(solution)/shard_map/ppermute | solution.py:387
  9.4 11.5 %collective-permute-start = (bf16[1,512,256]{2,1,0:T(8,128)(2,1)S(1)}, bf16[1,512,256]{2,1,0:T(8,128)(2,1)S(1)}, u32[]{:S(2)}, u32[]{:S(2)}) collective-permute-start(bf16[1,512,256]{2,1,0:T(8,128)(2,1)S(1)} %get-tuple-element.20), channel_id=1, source_target_pairs={{0,1},{1,2},{2,3},{3,4},{4,5},{5,6},{6,7},{7,8},{8,9},{9,10},{10,1... | collective-permute-start | bytes 786440 | tf_op jit(solution)/shard_map/ppermute | solution.py:386
  20.9 14.5 %copy-start.1 = (bf16[256,1024]{1,0:T(8,128)(2,1)S(1)}, bf16[256,1024]{1,0:T(8,128)(2,1)}, u32[]{:S(2)}) copy-start(bf16[256,1024]{1,0:T(8,128)(2,1)} %refs_5_.4) | copy-start | bytes 1572868
  21.0 14.5 %copy-start.2 = (bf16[1024,256]{1,0:T(8,128)(2,1)S(1)}, bf16[1024,256]{1,0:T(8,128)(2,1)}, u32[]{:S(2)}) copy-start(bf16[1024,256]{1,0:T(8,128)(2,1)} %refs_6_.4) | copy-start | bytes 1572868
  21.0 14.4 %copy-start.5 = (bf16[256,768]{1,0:T(8,128)(2,1)S(1)}, bf16[256,768]{1,0:T(8,128)(2,1)}, u32[]{:S(2)}) copy-start(bf16[256,768]{1,0:T(8,128)(2,1)} %refs_1_.4) | copy-start | bytes 1179652
  21.0 14.4 %copy-start.6 = (f32[8,64,64]{2,1,0:T(8,128)S(1)}, f32[8,64,64]{2,1,0:T(8,128)}, u32[]{:S(2)}) copy-start(f32[8,64,64]{2,1,0:T(8,128)} %refs_3_.4) | copy-start | bytes 393220
  21.0 14.4 %copy-start.9 = (bf16[256,256]{1,0:T(8,128)(2,1)S(1)}, bf16[256,256]{1,0:T(8,128)(2,1)}, u32[]{:S(2)}) copy-start(bf16[256,256]{1,0:T(8,128)(2,1)} %refs_2_.4) | copy-start | bytes 393220
  21.0 14.4 %copy-start.16 = (f32[256]{0:T(256)S(1)}, f32[256]{0:T(256)}, u32[]{:S(2)}) copy-start(f32[256]{0:T(256)} %param.26) | copy-start | bytes 3076
  21.0 14.4 %copy-start.17 = (f32[256]{0:T(256)S(1)}, f32[256]{0:T(256)}, u32[]{:S(2)}) copy-start(f32[256]{0:T(256)} %param.30) | copy-start | bytes 3076
  26.6 8.8 %collective-permute-start.4 = (bf16[8,4,16,256]{3,2,1,0:T(8,128)(2,1)S(1)}, bf16[8,4,16,256]{3,2,1,0:T(8,128)(2,1)S(1)}, u32[]{:S(2)}, u32[]{:S(2)}) collective-permute-start(bf16[8,4,16,256]{3,2,1,0:T(8,128)(2,1)S(1)} %get-tuple-element.17), channel_id=1, source_target_pairs={{0,1},{1,2},{2,3},{3,0},{4,5},{5,6},{6,7},{7,4},{8,9},{9,10},{10,1... | collective-permute-start | bytes 786440 | tf_op jit(solution)/shard_map/ppermute | solution.py:395
  26.8 8.6 %collective-permute-start.5 = (bf16[8,4,16,256]{3,2,1,0:T(8,128)(2,1)S(1)}, bf16[8,4,16,256]{3,2,1,0:T(8,128)(2,1)S(1)}, u32[]{:S(2)}, u32[]{:S(2)}) collective-permute-start(bf16[8,4,16,256]{3,2,1,0:T(8,128)(2,1)S(1)} %get-tuple-element.18), channel_id=1, source_target_pairs={{1,0},{2,1},{3,2},{0,3},{5,4},{6,5},{7,6},{4,7},{9,8},{10,9},{11,1... | collective-permute-start | bytes 786440 | tf_op jit(solution)/shard_map/ppermute | solution.py:396
  30.1 13.0 %collective-permute-start.2 = (bf16[8,4,16,256]{3,2,1,0:T(8,128)(2,1)S(1)}, bf16[8,4,16,256]{3,2,1,0:T(8,128)(2,1)S(1)}, u32[]{:S(2)}, u32[]{:S(2)}) collective-permute-start(bf16[8,4,16,256]{3,2,1,0:T(8,128)(2,1)S(1)} %get-tuple-element.15), channel_id=1, source_target_pairs={{0,1},{1,2},{2,3},{3,0},{4,5},{5,6},{6,7},{7,4},{8,9},{9,10},{10,1... | collective-permute-start | bytes 786440 | tf_op jit(solution)/shard_map/ppermute | solution.py:395
  30.1 13.0 %collective-permute-start.3 = (bf16[8,4,16,256]{3,2,1,0:T(8,128)(2,1)S(1)}, bf16[8,4,16,256]{3,2,1,0:T(8,128)(2,1)S(1)}, u32[]{:S(2)}, u32[]{:S(2)}) collective-permute-start(bf16[8,4,16,256]{3,2,1,0:T(8,128)(2,1)S(1)} %get-tuple-element.16), channel_id=1, source_target_pairs={{1,0},{2,1},{3,2},{0,3},{5,4},{6,5},{7,6},{4,7},{9,8},{10,9},{11,1... | collective-permute-start | bytes 786440 | tf_op jit(solution)/shard_map/ppermute | solution.py:396
  50.9 26.6 %copy-start.7 = (bf16[256,1024]{1,0:T(8,128)(2,1)S(1)}, bf16[256,1024]{1,0:T(8,128)(2,1)}, u32[]{:S(2)}) copy-start(bf16[256,1024]{1,0:T(8,128)(2,1)} %refs_5_.5) | copy-start | bytes 1572868
  51.0 26.6 %copy-start.8 = (bf16[1024,256]{1,0:T(8,128)(2,1)S(1)}, bf16[1024,256]{1,0:T(8,128)(2,1)}, u32[]{:S(2)}) copy-start(bf16[1024,256]{1,0:T(8,128)(2,1)} %refs_6_.5) | copy-start | bytes 1572868
  51.0 26.6 %copy-start.10 = (bf16[256,768]{1,0:T(8,128)(2,1)S(1)}, bf16[256,768]{1,0:T(8,128)(2,1)}, u32[]{:S(2)}) copy-start(bf16[256,768]{1,0:T(8,128)(2,1)} %refs_1_.5) | copy-start | bytes 1179652
  51.0 26.6 %copy-start.12 = (f32[8,64,64]{2,1,0:T(8,128)S(1)}, f32[8,64,64]{2,1,0:T(8,128)}, u32[]{:S(2)}) copy-start(f32[8,64,64]{2,1,0:T(8,128)} %refs_3_.5) | copy-start | bytes 393220
  51.0 26.6 %copy-start.13 = (bf16[256,256]{1,0:T(8,128)(2,1)S(1)}, bf16[256,256]{1,0:T(8,128)(2,1)}, u32[]{:S(2)}) copy-start(bf16[256,256]{1,0:T(8,128)(2,1)} %refs_2_.5) | copy-start | bytes 393220
  51.0 26.6 %copy-start.18 = (f32[256]{0:T(256)S(1)}, f32[256]{0:T(256)}, u32[]{:S(2)}) copy-start(f32[256]{0:T(256)} %param.33) | copy-start | bytes 3076
  51.0 26.6 %copy-start.19 = (f32[256]{0:T(256)S(1)}, f32[256]{0:T(256)}, u32[]{:S(2)}) copy-start(f32[256]{0:T(256)} %param.37) | copy-start | bytes 3076

commit v5 on v4

--- a/solution.py
+++ b/solution.py
@@ -32,6 +32,8 @@
 
 
 PAD = 8
+SPAN = 272
+FIRST = (0, 240)
 
 
 def twice_gelu_short(x):
@@ -46,7 +48,7 @@
     def clear(index, carry):
         for lb in range(8):
             e_ref[index, lb, 0:PAD, :] = edge
-            e_ref[index, lb, 512 + PAD : 512 + 2 * PAD, :] = edge
+            e_ref[index, lb, SPAN + PAD : SPAN + 2 * PAD, :] = edge
         return carry
 
     lax.fori_loop(0, e_ref.shape[0], clear, 0)
@@ -59,36 +61,34 @@
         wide = twice_gelu(flat)
         if factor is not None:
             wide = wide * factor
-        for half in range(2):
-            e_ref[row, nb * 2 + half, PAD : 512 + PAD, :] = wide[:, half * 128 : (half + 1) * 128]
-
-
-def depth_row(sources, x_ref, row, taps, wp_ref, out_ref, at_row):
-    for side in range(2):
-        base = side * 256
-        total = jnp.zeros((256, 256), F32)
-        for pair in range(4):
-            parts = []
-            for lb in (2 * pair, 2 * pair + 1):
-                acc = None
-                for tap in range(9):
-                    e_ref, at = sources[tap // 3]
-                    term = (
-                        e_ref[at, lb, pl.ds(base + PAD - 1 + tap % 3, 256), :]
-                        * taps[tap : tap + 1, lb * 128 : (lb + 1) * 128]
-                    )
-                    acc = term if acc is None else acc + term
-                parts.append(twice_gelu_short(acc))
-            wide = jnp.concatenate(parts, axis=1)
-            total = total + jnp.dot(
-                wide, wp_ref[pair * 256 : (pair + 1) * 256, :], preferred_element_type=F32
-            )
-        values = x_ref[row, base : base + 256, :].astype(F32)
-        result = (values + 0.5 * total).astype(BF16)
-        for jj in range(4):
-            for tp in range(4):
-                at = jj * 64 + tp * 16
-                out_ref[at_row * 4 + tp, 4 * side + jj] = result[at : at + 16]
+        for part in range(2):
+            e_ref[row, nb * 2 + part, PAD : SPAN + PAD, :] = wide[:, part * 128 : (part + 1) * 128]
+
+
+def depth_row(half, sources, values, taps, wp_ref, out_ref, at_row):
+    base = 256 * half - FIRST[half] + PAD
+    total = jnp.zeros((256, 256), F32)
+    for pair in range(4):
+        parts = []
+        for lb in (2 * pair, 2 * pair + 1):
+            acc = None
+            for tap in range(9):
+                e_ref, at = sources[tap // 3]
+                term = (
+                    e_ref[at, lb, pl.ds(base - 1 + tap % 3, 256), :]
+                    * taps[tap : tap + 1, lb * 128 : (lb + 1) * 128]
+                )
+                acc = term if acc is None else acc + term
+            parts.append(twice_gelu_short(acc))
+        wide = jnp.concatenate(parts, axis=1)
+        total = total + jnp.dot(
+            wide, wp_ref[pair * 256 : (pair + 1) * 256, :], preferred_element_type=F32
+        )
+    result = (values.astype(F32) + 0.5 * total).astype(BF16)
+    for jj in range(4):
+        for tp in range(4):
+            at = jj * 64 + tp * 16
+            out_ref[at_row * 4 + tp, jj] = result[at : at + 16]
 
 
 def middle_kernel(
@@ -96,7 +96,7 @@
     x_ref, scale_ref, shift_ref, we_ref, dw_ref, wp_ref, sem,
 ):
     pairs = [(scale_hbm, scale_ref), (shift_hbm, shift_ref), (we_hbm, we_ref)]
-    pairs += [(x_hbm.at[r], x_ref.at[r]) for r in range(6)]
+    pairs += [(x_hbm.at[r, pl.ds(0, SPAN)], x_ref.at[r]) for r in range(6)]
     pairs += [(dw_hbm, dw_ref), (wp_hbm, wp_ref)]
     copies = [pltpu.make_async_copy(a, b, sem.at[n]) for n, (a, b) in enumerate(pairs)]
     for copy in copies:
@@ -115,69 +115,96 @@
     def depth(step, carry):
         for row in (2 * step + 1, 2 * step + 2):
             sources = [(e_ref, row - 1), (e_ref, row), (e_ref, row + 1)]
-            depth_row(sources, x_ref, row, taps, wp_ref, mid_ref, row - 1)
+            depth_row(0, sources, x_ref[row, 0:256], taps, wp_ref, mid_ref, row - 1)
         return carry
 
     lax.fori_loop(0, 2, depth, 0)
+
+
+def pick_pieces(own_ref, up_ref, down_ref):
+    v = own_y()
+
+    def pick(m, carry):
+        n_up = v + 1
+        row = jnp.minimum(2 * v + m // n_up, 5)
+        up_ref[m] = own_ref[row * 4 + jnp.clip(3 - v + lax.rem(m, n_up), 0, 3)]
+        n_down = 4 - v
+        row = jnp.minimum(m // n_down, 5)
+        down_ref[m] = own_ref[row * 4 + lax.rem(m, n_down)]
+        return carry
+
+    lax.fori_loop(0, 8, pick, 0)
+
+
+def expand_halo(half, top_ref, bot_ref, scale, shift, we_ref, e_ref, rows):
+    device = lax.axis_index("rows") * 8 + lax.axis_index("cols")
+    cols = slice(FIRST[half], FIRST[half] + SPAN)
+    for ref, row, present in ((top_ref, rows[0], device > 0), (bot_ref, rows[1], device < 127)):
+        expand_row(ref[0, cols], scale, shift, we_ref, e_ref, row, present.astype(F32))
 
 
 def edge_kernel(
     x_ref, top_ref, bot_ref, e_ref, mid_ref, scale_ref, shift_ref, we_ref, dw_ref, wp_ref,
-    edge_ref, up_l_ref, down_l_ref, up_r_ref, down_r_ref, halo_ref,
+    own_ref, up_ref, down_ref, halo_ref,
 ):
-    device = lax.axis_index("rows") * 8 + lax.axis_index("cols")
-    scale, shift = scale_ref[...], shift_ref[...]
     clear_edges(halo_ref)
-    expand_row(top_ref[0], scale, shift, we_ref, halo_ref, 0, (device > 0).astype(F32))
-    expand_row(bot_ref[0], scale, shift, we_ref, halo_ref, 1, (device < 127).astype(F32))
+    expand_halo(0, top_ref, bot_ref, scale_ref[...], shift_ref[...], we_ref, halo_ref, (0, 1))
     taps = dw_ref[...] * 0.5
     sources = [(halo_ref, 0), (e_ref, 0), (e_ref, 1)]
-    depth_row(sources, x_ref, 0, taps, wp_ref, edge_ref, 0)
+    depth_row(0, sources, x_ref[0, 0:256], taps, wp_ref, own_ref, 0)
     sources = [(e_ref, 4), (e_ref, 5), (halo_ref, 1)]
-    depth_row(sources, x_ref, 5, taps, wp_ref, edge_ref, 1)
-    v = own_y()
-
-    def send(row, tp, m, left_ref, right_ref):
-        inside = jnp.logical_and(row >= 1, row <= 4)
-
-        @pl.when(inside)
-        def _():
-            at = jnp.clip(row - 1, 0, 3) * 4 + tp
-            left_ref[m] = mid_ref[at, 0:4]
-            right_ref[m] = mid_ref[at, 4:8]
-
-        @pl.when(jnp.logical_not(inside))
-        def _():
-            at = jnp.where(row == 5, 4, 0) + tp
-            left_ref[m] = edge_ref[at, 0:4]
-            right_ref[m] = edge_ref[at, 4:8]
-
-    def pick(m, carry):
-        n_up = v + 1
-        tp = jnp.clip(3 - v + lax.rem(m, n_up), 0, 3)
-        send(jnp.minimum(2 * v + m // n_up, 5), tp, m, up_l_ref, up_r_ref)
-        n_down = 4 - v
-        send(jnp.minimum(m // n_down, 5), lax.rem(m, n_down), m, down_l_ref, down_r_ref)
-        return carry
-
-    lax.fori_loop(0, 8, pick, 0)
+    depth_row(0, sources, x_ref[5, 0:256], taps, wp_ref, own_ref, 5)
+
+    def keep(m, carry):
+        own_ref[4 + m] = mid_ref[m]
+        return carry
+
+    lax.fori_loop(0, 16, keep, 0)
+    pick_pieces(own_ref, up_ref, down_ref)
+
+
+def right_kernel(
+    x_ref, top_ref, bot_ref, scale_ref, shift_ref, we_ref, dw_ref, wp_ref,
+    own_ref, up_ref, down_ref, e_ref,
+):
+    clear_edges(e_ref)
+    scale, shift = scale_ref[...], shift_ref[...]
+    expand_halo(1, top_ref, bot_ref, scale, shift, we_ref, e_ref, (0, 7))
+    cols = slice(FIRST[1], FIRST[1] + SPAN)
+
+    def expand(step, carry):
+        for row in (3 * step, 3 * step + 1, 3 * step + 2):
+            expand_row(x_ref[row, cols], scale, shift, we_ref, e_ref, row + 1, None)
+        return carry
+
+    lax.fori_loop(0, 2, expand, 0)
+    taps = dw_ref[...] * 0.5
+
+    def depth(step, carry):
+        for row in (2 * step, 2 * step + 1):
+            sources = [(e_ref, row), (e_ref, row + 1), (e_ref, row + 2)]
+            depth_row(1, sources, x_ref[row, 256:512], taps, wp_ref, own_ref, row)
+        return carry
+
+    lax.fori_loop(0, 3, depth, 0)
+    pick_pieces(own_ref, up_ref, down_ref)
 
 
 def vmem(limit):
     return pltpu.CompilerParams(vmem_limit_bytes=limit * 1024 * 1024)
 
 
-def pieces(count, columns):
-    return jax.ShapeDtypeStruct((count, columns, 16, 256), BF16)
+def pieces(count):
+    return jax.ShapeDtypeStruct((count, 4, 16, 256), BF16)
 
 
 def bottleneck_middle(strips, scale, shift, we, dw, wp):
     return pl.pallas_call(
         middle_kernel,
-        out_shape=[pieces(16, 8), jax.ShapeDtypeStruct((6, 8, 512 + 2 * PAD, 128), F32)],
+        out_shape=[pieces(16), jax.ShapeDtypeStruct((6, 8, SPAN + 2 * PAD, 128), F32)],
         in_specs=[pl.BlockSpec(memory_space=pltpu.HBM)] * 6,
         scratch_shapes=[
-            pltpu.VMEM((6, 512, 256), BF16),
+            pltpu.VMEM((6, SPAN, 256), BF16),
             pltpu.VMEM((1, 256), F32),
             pltpu.VMEM((1, 256), F32),
             pltpu.VMEM((256, 1024), BF16),
@@ -193,16 +220,28 @@
 def bottleneck_edge(strips, top, bot, expanded, middle, scale, shift, we, dw, wp):
     return pl.pallas_call(
         edge_kernel,
-        out_shape=[pieces(8, 8)] + [pieces(8, 4)] * 4,
-        scratch_shapes=[pltpu.VMEM((2, 8, 512 + 2 * PAD, 128), F32)],
+        out_shape=[pieces(24), pieces(8), pieces(8)],
+        scratch_shapes=[pltpu.VMEM((2, 8, SPAN + 2 * PAD, 128), F32)],
         compiler_params=vmem(24),
         name="bottleneck_edge",
     )(strips, top, bot, expanded, middle, scale, shift, we, dw, wp)
 
 
+def bottleneck_right(strips, top, bot, scale, shift, we, dw, wp):
+    return pl.pallas_call(
+        right_kernel,
+        out_shape=[pieces(24), pieces(8), pieces(8)],
+        scratch_shapes=[pltpu.VMEM((8, 8, SPAN + 2 * PAD, 128), F32)],
+        compiler_params=vmem(24),
+        name="bottleneck_right",
+    )(strips, top, bot, scale, shift, we, dw, wp)
+
+
 def normed_of(x, gain):
-    center = x - jnp.mean(x, axis=-1, keepdims=True)
-    spread = jnp.mean(center * center, axis=-1, keepdims=True)
+    ones = jnp.full((256, 256), 1.0 / 256.0, BF16)
+    center = x - jnp.dot(x.astype(BF16), ones, preferred_element_type=F32)
+    squares = (center * center).astype(BF16)
+    spread = jnp.dot(squares, ones, preferred_element_type=F32)
     return (center * lax.rsqrt(spread + EPSILON) * gain).astype(BF16)
 
 
@@ -286,14 +325,11 @@
             m_up = jnp.clip((local - 2 * v) * (v + 1) + tp - (3 - v), 0, 7)
             v = jnp.minimum(y + 1, 3)
             m_down = jnp.clip(local * (4 - v) + tp, 0, 7)
-            inside = jnp.logical_and(local >= 1, local <= 4)
-            at_mid = jnp.clip(local - 1, 0, 3) * 4 + tp
-            at_edge = jnp.where(local == 5, 4, 0) + tp
-            places.append((owner, inside, at_mid, at_edge, m_up, m_down))
+            places.append((owner, local * 4 + tp, m_up, m_down))
     return y, places
 
 
-def block_kernel(half, mid_ref, edge_ref, up_ref, down_ref, *refs):
+def block_kernel(half, own_ref, up_ref, down_ref, *refs):
     w = dict(zip(NAMES, refs))
     refs = refs[len(NAMES) :]
     if half == 1:
@@ -303,9 +339,8 @@
         (out_ref,) = refs
     y, places = block_places()
     units = []
-    js = slice(4 * half, 4 * half + 4)
-    for owner, inside, at_mid, at_edge, m_up, m_down in places:
-        mine = jnp.where(inside, mid_ref[at_mid, js].astype(F32), edge_ref[at_edge, js].astype(F32))
+    for owner, at, m_up, m_down in places:
+        mine = own_ref[at].astype(F32)
         above = up_ref[m_up].astype(F32)
         below = down_ref[m_down].astype(F32)
         units.append(jnp.where(owner == y, mine, jnp.where(owner < y, above, below)))
@@ -357,13 +392,13 @@
     lax.fori_loop(0, 3, slot, 0)
 
 
-def block_section(half, mid, edge, up, down, weights, *done):
+def block_section(half, own, up, down, weights, *done):
     return pl.pallas_call(
         functools.partial(block_kernel, half),
         out_shape=jax.ShapeDtypeStruct((8, 3, 4 if half == 0 else 8, 16, 256), BF16),
         compiler_params=vmem(24),
         name="block_section",
-    )(mid, edge, up, down, *weights, *done)
+    )(own, up, down, *weights, *done)
 
 
 def grid_section(x, weights):
@@ -389,11 +424,11 @@
     middle, expanded = bottleneck_middle(
         *[pltpu.with_memory_space_constraint(a, pltpu.HBM) for a in (stem_strips, *weights)]
     )
-    edge, up_l, down_l, up_r, down_r = bottleneck_edge(
-        stem_strips, top, bot, expanded, middle, *weights
-    )
-    up_l, up_r = [lax.ppermute(a, "cols", Y_UP) for a in (up_l, up_r)]
-    down_l, down_r = [lax.ppermute(a, "cols", Y_DOWN) for a in (down_l, down_r)]
+    own_l, up_l, down_l = bottleneck_edge(stem_strips, top, bot, expanded, middle, *weights)
+    own_l, up_l, down_l, top, bot = lax.optimization_barrier((own_l, up_l, down_l, top, bot))
+    up_l, down_l = lax.ppermute(up_l, "cols", Y_UP), lax.ppermute(down_l, "cols", Y_DOWN)
+    own_r, up_r, down_r = bottleneck_right(stem_strips, top, bot, *weights)
+    up_r, down_r = lax.ppermute(up_r, "cols", Y_UP), lax.ppermute(down_r, "cols", Y_DOWN)
     block_weights = (
         row(block_gain), block_inputs, block_output, block_bias,
         row(first_gain), first_up, first_down,
@@ -402,8 +437,8 @@
         row(grid_gain), grid_inputs, grid_output, grid_bias,
         row(second_gain), second_up, second_down,
     )
-    left = block_section(0, middle, edge, up_l, down_l, block_weights)
-    sent = block_section(1, middle, edge, up_r, down_r, block_weights, left)
+    left = block_section(0, own_l, up_l, down_l, block_weights)
+    sent = block_section(1, own_r, up_r, down_r, block_weights, left)
     arrived = lax.all_to_all(sent, "rows", 0, 0, axis_index_groups=CORE_ROWS, tiled=True)
     back = grid_section(arrived, grid_weights)
     landed = lax.all_to_all(back, both, 0, 0, axis_index_groups=CORE_ALL, tiled=True)

time: 128 us -> 124 us (0.969)
  blocking collectives: 59.1 us -> 52.6 us
  waiting for transfers between devices: 2.13 us -> 4.24 us
    all_to_all x1, blocking collectives: 32.6 us -> 28 us  [body(): lax.all_to_all(back, both, 0, 0, axis_index_groups=CORE_ALL, tiled=True)]
    ppermute x1, waiting for transfers between devices: 0.01 us -> 4.23 us  [body(): top = lax.ppermute(stem_strips[5:6], both, STRIP_DOWN)]
    ppermute x4, waiting for transfers between devices: 2.12 us -> 0.01 us  [the longest x1 0.01 us: body(): lax.ppermute(up_l, 'cols', Y_UP)]
    all_to_all x1, blocking collectives: 26.6 us -> 24.6 us  [body(): lax.all_to_all(sent, 'rows', 0, 0, axis_index_groups=CORE_ROWS, tiled=True)]
    pallas_call x2 -> x3, Pallas kernels: 17 us -> 17.9 us  [the longest x1 7.93 us: bottleneck_right(): pl.pallas_call(right_kernel, out_shape=[pieces(24), pieces(8), pieces(8)]...]
  transfers between devices with their start and end apart: 6 -> 6, of which waited for: 1 -> 1; matrix products, arithmetic and copies ran while one was open for 0% -> 0% of each run, Pallas kernels for 15% -> 18%
where the time goes in v5:
time: 124 us; the launch traced here: 123 us
  blocking collectives  52.6 us (42%)
  Pallas kernels  48.6 us (39%)
  starting transfers between devices  15.1 us (12%)
  waiting for transfers between devices  4.24 us (3%)
  local copies, waits for them, and re-layouts  2.43 us (2%)
    all_to_all x1, blocking collectives, body(): lax.all_to_all(back, both, 0, 0, axis_index_groups=CORE_ALL, tiled=True)  28 us
    all_to_all x1, blocking collectives, body(): lax.all_to_all(sent, 'rows', 0, 0, axis_index_groups=CORE_ROWS, tiled=True)  24.6 us
    pallas_call x1, Pallas kernels, grid_section(): pl.pallas_call(grid_kernel, out_shape=jax.ShapeDtypeStruct((64, 3, 16, 25...  16 us
    pallas_call x2, Pallas kernels, block_section(): pl.pallas_call(functools.partial(block_kernel, half), out_shape=jax.Shape...  14.7 us
    ppermute x1, starting transfers between devices, body(): bot = lax.ppermute(stem_strips[0:1], both, STRIP_UP)  8.28 us
    pallas_call x1, Pallas kernels, bottleneck_right(): pl.pallas_call(right_kernel, out_shape=[pieces(24), pieces(8), pieces(8)]...  7.93 us
    pallas_call x1, Pallas kernels, bottleneck_middle(): pl.pallas_call(middle_kernel, out_shape=[pieces(16), jax.ShapeDtypeStruct...  6.98 us
    ppermute x1, waiting for transfers between devices, body(): top = lax.ppermute(stem_strips[5:6], both, STRIP_DOWN)  4.23 us
  transfers between devices with their start and end apart: 6, of which 1 were waited for; matrix products, arithmetic and copies ran while one was open for 0% of the time, Pallas kernels for 18%

profile of v5, /device:TPU:0, one launch (start us, length us, event | category | flops | bytes accessed | tf_op | source)
XLA Modules:
  0.0 123.3 jit_solution(11037745040031832766)
XLA Ops:
  0.0 1.1 fusion
  1.1 0.0 copy-start
  1.1 0.0 copy-start.1
  1.1 0.0 copy-start.2
  1.1 0.0 copy-start.7
  1.1 0.0 copy-start.14
  1.1 0.0 copy-start.15
  1.1 8.3 %collective-permute-start.1 = (bf16[1,512,256]{2,1,0:T(8,128)(2,1)S(1)}, bf16[1,512,256]{2,1,0:T(8,128)(2,1)S(1)}, u32[]{:S(2)}, u32[]{:S(2)}) collective-permute-start(bf16[1,512,256]{2,1,0:T(8,128)(2,1)S(1)} %get-tuple-element.31), channel_id=1, source_target_pairs={{1,0},{2,1},{3,2},{4,3},{5,4},{6,5},{7,6},{8,7},{9,8},{10,9},{11,1... | collective-permute-start | bytes 786440 | tf_op jit(solution)/shard_map/ppermute | solution.py:422
  9.4 0.0 collective-permute-start
  9.4 7.0 %bottleneck_middle.1 = (bf16[16,4,16,256]{3,2,1,0:T(8,128)(2,1)S(1)}, f32[6,8,288,128]{3,2,1,0:T(8,128)S(1)}) custom-call(bf16[6,512,256]{2,1,0:T(8,128)(2,1)} %x_ref.3, f32[1,256]{1,0:T(1,128)} %bitcast.10, f32[1,256]{1,0:T(1,128)} %bitcast.13, bf16[256,1024]{1,0:T(8,128)(2,1)} %we_ref.3, f32[9,1024]{1,0:T(8,128)} %dw_ref.3, bf16[1024,256]{1,0:T(8,128)(2,1)} %wp_ref.3), custom_call_target="tpu_custom_call" | custom-call | tf_op jit(solution)/shard_map/bottleneck_middle/pallas_call | solution.py:202
  16.4 0.0 collective-permute-done.1.bot_ref
  16.4 4.2 %collective-permute-done.top_ref = bf16[1,512,256]{2,1,0:T(8,128)(2,1)S(1)} collective-permute-done((bf16[1,512,256]{2,1,0:T(8,128)(2,1)S(1)}, bf16[1,512,256]{2,1,0:T(8,128)(2,1)S(1)}, u32[]{:S(2)}, u32[]{:S(2)}) %collective-permute-start) | collective-permute-done | bytes 262176 | tf_op jit(solution)/shard_map/ppermute | solution.py:421
  20.7 3.0 %bottleneck_edge.1 = (bf16[24,4,16,256]{3,2,1,0:T(8,128)(2,1)S(1)}, bf16[8,4,16,256]{3,2,1,0:T(8,128)(2,1)S(1)}, bf16[8,4,16,256]{3,2,1,0:T(8,128)(2,1)S(1)}) custom-call(bf16[6,512,256]{2,1,0:T(8,128)(2,1)S(1)} %copy-done, bf16[1,512,256]{2,1,0:T(8,128)(2,1)S(1)} %collective-permute-done.top_ref, bf16[1,512,256]{2,1,0:T(8,128)(2,1)S(1)} %collective-permute-done.1.bot_ref, ...), custom_call_target="tpu_custom_call" | custom-call | tf_op jit(solution)/shard_map/bottleneck_edge/pallas_call | solution.py:221
  23.7 0.0 copy-start.3
  23.7 0.0 copy-start.4
  23.7 0.0 copy-start.5
  23.7 0.0 copy-start.6
  23.7 0.0 copy-start.10
  23.7 0.0 copy-start.16
  23.8 0.0 copy-start.17
  23.8 0.1 collective-permute-start.4
  23.9 3.2 %collective-permute-start.5 = (bf16[8,4,16,256]{3,2,1,0:T(8,128)(2,1)S(1)}, bf16[8,4,16,256]{3,2,1,0:T(8,128)(2,1)S(1)}, u32[]{:S(2)}, u32[]{:S(2)}) collective-permute-start(bf16[8,4,16,256]{3,2,1,0:T(8,128)(2,1)S(1)} %get-tuple-element.30), channel_id=1, source_target_pairs={{1,0},{2,1},{3,2},{0,3},{5,4},{6,5},{7,6},{4,7},{9,8},{10,9},{11,1... | collective-permute-start | bytes 786440 | tf_op jit(solution)/shard_map/ppermute | solution.py:429
  27.1 7.9 %bottleneck_right.1 = (bf16[24,4,16,256]{3,2,1,0:T(8,128)(2,1)S(1)}, bf16[8,4,16,256]{3,2,1,0:T(8,128)(2,1)S(1)}, bf16[8,4,16,256]{3,2,1,0:T(8,128)(2,1)S(1)}) custom-call(bf16[6,512,256]{2,1,0:T(8,128)(2,1)S(1)} %copy-done, bf16[1,512,256]{2,1,0:T(8,128)(2,1)S(1)} %collective-permute-done.top_ref, bf16[1,512,256]{2,1,0:T(8,128)(2,1)S(1)} %collective-permute-done.1.bot_ref, ...), custom_call_target="tpu_custom_call" | custom-call | tf_op jit(solution)/shard_map/bottleneck_right/pallas_call | solution.py:231
  35.0 0.3 collective-permute-start.2
  35.3 3.2 %collective-permute-start.3 = (bf16[8,4,16,256]{3,2,1,0:T(8,128)(2,1)S(1)}, bf16[8,4,16,256]{3,2,1,0:T(8,128)(2,1)S(1)}, u32[]{:S(2)}, u32[]{:S(2)}) collective-permute-start(bf16[8,4,16,256]{3,2,1,0:T(8,128)(2,1)S(1)} %get-tuple-element.27), channel_id=1, source_target_pairs={{1,0},{2,1},{3,2},{0,3},{5,4},{6,5},{7,6},{4,7},{9,8},{10,9},{11,1... | collective-permute-start | bytes 786440 | tf_op jit(solution)/shard_map/ppermute | solution.py:431
  38.5 0.0 collective-permute-done.4.up_ref
  38.5 0.0 collective-permute-done.5.down_ref
  38.5 0.0 copy-done.4
  38.5 0.0 copy-done.5
  38.5 0.0 copy-done.6
  38.5 0.0 copy-done.10
  38.6 0.0 copy-done.16
  38.6 0.0 copy-done.17
  38.6 7.2 %block_section.2.refs_7_ = bf16[8,3,4,16,256]{4,3,2,1,0:T(8,128)(2,1)S(1)} custom-call(bf16[24,4,16,256]{3,2,1,0:T(8,128)(2,1)S(1)} %get-tuple-element.28.own_ref, bf16[8,4,16,256]{3,2,1,0:T(8,128)(2,1)S(1)} %collective-permute-done.4.up_ref, bf16[8,4,16,256]{3,2,1,0:T(8,128)(2,1)S(1)} %collective-permute-done.5.down_ref, f32[1,256]{1,0:T(1,128)S(1)} %bitcast.16, ...), custom_call_target="tpu_custom_call" | custom-call | tf_op jit(solution)/shard_map/block_section/pallas_call | solution.py:396
  45.8 0.0 collective-permute-done.2.up_ref
  45.8 0.0 collective-permute-done.3.down_ref
  45.8 7.5 %block_section.3 = bf16[8,3,8,16,256]{4,3,2,1,0:T(8,128)(2,1)S(1)} custom-call(bf16[24,4,16,256]{3,2,1,0:T(8,128)(2,1)S(1)} %get-tuple-element.25.own_ref, bf16[8,4,16,256]{3,2,1,0:T(8,128)(2,1)S(1)} %collective-permute-done.2.up_ref, bf16[8,4,16,256]{3,2,1,0:T(8,128)(2,1)S(1)} %collective-permute-done.3.down_ref, f32[1,256]{1,0:T(1,128)S(1)} %bitcast.17, ...), custom_call_target="tpu_custom_call" | custom-call | tf_op jit(solution)/shard_map/block_section/pallas_call | solution.py:396
  53.4 0.0 copy-start.8
  53.4 0.0 copy-start.9
  53.4 0.0 copy-start.11
  53.4 0.0 copy-start.12
  53.4 0.0 copy-start.13
  53.4 0.0 copy-start.18
  53.4 0.0 copy-start.19
  53.4 24.6 %all_to_all.10.x_ref = bf16[8,3,8,16,256]{4,3,2,1,0:T(8,128)(2,1)S(1)} all-to-all(bf16[8,3,8,16,256]{4,3,2,1,0:T(8,128)(2,1)S(1)} %block_section.3), channel_id=1, replica_groups={{0,16,32,48,64,80,96,112},{8,24,40,56,72,88,104,120},{1,17,33,49,65,81,..., dimensions={0} | all-to-all | bytes 3145728 | tf_op jit(solution)/shard_map/all_to_all | solution.py:442
  78.1 16.0 %grid_section.1 = bf16[64,3,16,256]{3,2,1,0:T(8,128)(2,1)S(1)} custom-call(bf16[8,3,8,16,256]{4,3,2,1,0:T(8,128)(2,1)S(1)} %all_to_all.10.x_ref, f32[1,256]{1,0:T(1,128)S(1)} %bitcast.20, bf16[256,768]{1,0:T(8,128)(2,1)S(1)} %copy-done.11, bf16[256,256]{1,0:T(8,128)(2,1)S(1)} %copy-done.13, f32[8,64,64]{2,1,0:T(8,128)S(1)} %copy-done.12, ...), custom_call_target="tpu_custom_call" | custom-call | tf_op jit(solution)/shard_map/grid_section/pallas_call | solution.py:405
  94.1 28.0 %all_to_all.11 = bf16[64,3,16,256]{3,2,1,0:T(8,128)(2,1)S(1)} all-to-all(bf16[64,3,16,256]{3,2,1,0:T(8,128)(2,1)S(1)} %grid_section.1), channel_id=1, replica_groups={{0,1,2,3,4,5,6,7,16,17,18,19,20,21,22,23,32,33,34,35,36,37,38,39,48,49,..., dimensions={0} | all-to-all | bytes 3145728 | tf_op jit(solution)/shard_map/all_to_all | solution.py:444
  122.1 1.2 %copy.21 = bf16[2,3,8,4,16,256]{5,4,3,2,1,0:T(8,128)(2,1)} copy(bf16[2,3,8,4,16,256]{5,4,3,1,0,2:T(8,128)(2,1)S(1)} %bitcast.22) | data formatting | bytes 3145728 | tf_op jit(solution)/shard_map/transpose | solution.py:445
  (14 shorter events, 0.0 us)
Async XLA Ops:
  1.1 19.6 %copy-start = (bf16[6,512,256]{2,1,0:T(8,128)(2,1)S(1)}, bf16[6,512,256]{2,1,0:T(8,128)(2,1)}, u32[]{:S(2)}) copy-start(bf16[6,512,256]{2,1,0:T(8,128)(2,1)} %x_ref.3) | copy-start | bytes 4718596
  1.1 19.6 %copy-start.1 = (bf16[256,1024]{1,0:T(8,128)(2,1)S(1)}, bf16[256,1024]{1,0:T(8,128)(2,1)}, u32[]{:S(2)}) copy-start(bf16[256,1024]{1,0:T(8,128)(2,1)} %we_ref.3) | copy-start | bytes 1572868
  1.1 19.6 %copy-start.2 = (bf16[1024,256]{1,0:T(8,128)(2,1)S(1)}, bf16[1024,256]{1,0:T(8,128)(2,1)}, u32[]{:S(2)}) copy-start(bf16[1024,256]{1,0:T(8,128)(2,1)} %wp_ref.3) | copy-start | bytes 1572868
  1.1 19.6 %copy-start.7 = (f32[9,1024]{1,0:T(8,128)S(1)}, f32[9,1024]{1,0:T(8,128)}, u32[]{:S(2)}) copy-start(f32[9,1024]{1,0:T(8,128)} %dw_ref.3) | copy-start | bytes 110596
  1.1 19.6 %copy-start.14 = (f32[256]{0:T(256)S(1)}, f32[256]{0:T(256)}, u32[]{:S(2)}) copy-start(f32[256]{0:T(256)} %param.21) | copy-start | bytes 3076
  1.1 19.6 %copy-start.15 = (f32[256]{0:T(256)S(1)}, f32[256]{0:T(256)}, u32[]{:S(2)}) copy-start(f32[256]{0:T(256)} %param.22) | copy-start | bytes 3076
  1.1 15.3 %collective-permute-start.1 = (bf16[1,512,256]{2,1,0:T(8,128)(2,1)S(1)}, bf16[1,512,256]{2,1,0:T(8,128)(2,1)S(1)}, u32[]{:S(2)}, u32[]{:S(2)}) collective-permute-start(bf16[1,512,256]{2,1,0:T(8,128)(2,1)S(1)} %get-tuple-element.31), channel_id=1, source_target_pairs={{1,0},{2,1},{3,2},{4,3},{5,4},{6,5},{7,6},{8,7},{9,8},{10,9},{11,1... | collective-permute-start | bytes 786440 | tf_op jit(solution)/shard_map/ppermute | solution.py:422
  9.4 11.2 %collective-permute-start = (bf16[1,512,256]{2,1,0:T(8,128)(2,1)S(1)}, bf16[1,512,256]{2,1,0:T(8,128)(2,1)S(1)}, u32[]{:S(2)}, u32[]{:S(2)}) collective-permute-start(bf16[1,512,256]{2,1,0:T(8,128)(2,1)S(1)} %get-tuple-element.32), channel_id=1, source_target_pairs={{0,1},{1,2},{2,3},{3,4},{4,5},{5,6},{6,7},{7,8},{8,9},{9,10},{10,1... | collective-permute-start | bytes 786440 | tf_op jit(solution)/shard_map/ppermute | solution.py:421
  23.7 14.8 %copy-start.3 = (bf16[256,1024]{1,0:T(8,128)(2,1)S(1)}, bf16[256,1024]{1,0:T(8,128)(2,1)}, u32[]{:S(2)}) copy-start(bf16[256,1024]{1,0:T(8,128)(2,1)} %refs_5_.4) | copy-start | bytes 1572868
  23.7 14.8 %copy-start.4 = (bf16[1024,256]{1,0:T(8,128)(2,1)S(1)}, bf16[1024,256]{1,0:T(8,128)(2,1)}, u32[]{:S(2)}) copy-start(bf16[1024,256]{1,0:T(8,128)(2,1)} %refs_6_.4) | copy-start | bytes 1572868
  23.7 14.8 %copy-start.5 = (bf16[256,768]{1,0:T(8,128)(2,1)S(1)}, bf16[256,768]{1,0:T(8,128)(2,1)}, u32[]{:S(2)}) copy-start(bf16[256,768]{1,0:T(8,128)(2,1)} %refs_1_.4) | copy-start | bytes 1179652
  23.7 14.8 %copy-start.6 = (f32[8,64,64]{2,1,0:T(8,128)S(1)}, f32[8,64,64]{2,1,0:T(8,128)}, u32[]{:S(2)}) copy-start(f32[8,64,64]{2,1,0:T(8,128)} %refs_3_.4) | copy-start | bytes 393220
  23.7 14.8 %copy-start.10 = (bf16[256,256]{1,0:T(8,128)(2,1)S(1)}, bf16[256,256]{1,0:T(8,128)(2,1)}, u32[]{:S(2)}) copy-start(bf16[256,256]{1,0:T(8,128)(2,1)} %refs_2_.4) | copy-start | bytes 393220
  23.7 14.8 %copy-start.16 = (f32[256]{0:T(256)S(1)}, f32[256]{0:T(256)}, u32[]{:S(2)}) copy-start(f32[256]{0:T(256)} %param.26) | copy-start | bytes 3076
  23.8 14.8 %copy-start.17 = (f32[256]{0:T(256)S(1)}, f32[256]{0:T(256)}, u32[]{:S(2)}) copy-start(f32[256]{0:T(256)} %param.30) | copy-start | bytes 3076
  23.8 14.7 %collective-permute-start.4 = (bf16[8,4,16,256]{3,2,1,0:T(8,128)(2,1)S(1)}, bf16[8,4,16,256]{3,2,1,0:T(8,128)(2,1)S(1)}, u32[]{:S(2)}, u32[]{:S(2)}) collective-permute-start(bf16[8,4,16,256]{3,2,1,0:T(8,128)(2,1)S(1)} %get-tuple-element.29), channel_id=1, source_target_pairs={{0,1},{1,2},{2,3},{3,0},{4,5},{5,6},{6,7},{7,4},{8,9},{9,10},{10,1... | collective-permute-start | bytes 786440 | tf_op jit(solution)/shard_map/ppermute | solution.py:429
  23.9 14.7 %collective-permute-start.5 = (bf16[8,4,16,256]{3,2,1,0:T(8,128)(2,1)S(1)}, bf16[8,4,16,256]{3,2,1,0:T(8,128)(2,1)S(1)}, u32[]{:S(2)}, u32[]{:S(2)}) collective-permute-start(bf16[8,4,16,256]{3,2,1,0:T(8,128)(2,1)S(1)} %get-tuple-element.30), channel_id=1, source_target_pairs={{1,0},{2,1},{3,2},{0,3},{5,4},{6,5},{7,6},{4,7},{9,8},{10,9},{11,1... | collective-permute-start | bytes 786440 | tf_op jit(solution)/shard_map/ppermute | solution.py:429
  35.0 10.8 %collective-permute-start.2 = (bf16[8,4,16,256]{3,2,1,0:T(8,128)(2,1)S(1)}, bf16[8,4,16,256]{3,2,1,0:T(8,128)(2,1)S(1)}, u32[]{:S(2)}, u32[]{:S(2)}) collective-permute-start(bf16[8,4,16,256]{3,2,1,0:T(8,128)(2,1)S(1)} %get-tuple-element.26), channel_id=1, source_target_pairs={{0,1},{1,2},{2,3},{3,0},{4,5},{5,6},{6,7},{7,4},{8,9},{9,10},{10,1... | collective-permute-start | bytes 786440 | tf_op jit(solution)/shard_map/ppermute | solution.py:431
  35.3 10.5 %collective-permute-start.3 = (bf16[8,4,16,256]{3,2,1,0:T(8,128)(2,1)S(1)}, bf16[8,4,16,256]{3,2,1,0:T(8,128)(2,1)S(1)}, u32[]{:S(2)}, u32[]{:S(2)}) collective-permute-start(bf16[8,4,16,256]{3,2,1,0:T(8,128)(2,1)S(1)} %get-tuple-element.27), channel_id=1, source_target_pairs={{1,0},{2,1},{3,2},{0,3},{5,4},{6,5},{7,6},{4,7},{9,8},{10,9},{11,1... | collective-permute-start | bytes 786440 | tf_op jit(solution)/shard_map/ppermute | solution.py:431
  53.4 24.7 %copy-start.8 = (bf16[256,1024]{1,0:T(8,128)(2,1)S(1)}, bf16[256,1024]{1,0:T(8,128)(2,1)}, u32[]{:S(2)}) copy-start(bf16[256,1024]{1,0:T(8,128)(2,1)} %refs_5_.5) | copy-start | bytes 1572868
  53.4 24.7 %copy-start.9 = (bf16[1024,256]{1,0:T(8,128)(2,1)S(1)}, bf16[1024,256]{1,0:T(8,128)(2,1)}, u32[]{:S(2)}) copy-start(bf16[1024,256]{1,0:T(8,128)(2,1)} %refs_6_.5) | copy-start | bytes 1572868
  53.4 24.7 %copy-start.11 = (bf16[256,768]{1,0:T(8,128)(2,1)S(1)}, bf16[256,768]{1,0:T(8,128)(2,1)}, u32[]{:S(2)}) copy-start(bf16[256,768]{1,0:T(8,128)(2,1)} %refs_1_.5) | copy-start | bytes 1179652
  53.4 24.7 %copy-start.12 = (f32[8,64,64]{2,1,0:T(8,128)S(1)}, f32[8,64,64]{2,1,0:T(8,128)}, u32[]{:S(2)}) copy-start(f32[8,64,64]{2,1,0:T(8,128)} %refs_3_.5) | copy-start | bytes 393220
  53.4 24.7 %copy-start.13 = (bf16[256,256]{1,0:T(8,128)(2,1)S(1)}, bf16[256,256]{1,0:T(8,128)(2,1)}, u32[]{:S(2)}) copy-start(bf16[256,256]{1,0:T(8,128)(2,1)} %refs_2_.5) | copy-start | bytes 393220
  53.4 24.7 %copy-start.18 = (f32[256]{0:T(256)S(1)}, f32[256]{0:T(256)}, u32[]{:S(2)}) copy-start(f32[256]{0:T(256)} %param.33) | copy-start | bytes 3076
  53.4 24.7 %copy-start.19 = (f32[256]{0:T(256)S(1)}, f32[256]{0:T(256)}, u32[]{:S(2)}) copy-start(f32[256]{0:T(256)} %param.37) | copy-start | bytes 3076

commit v6 on v5

--- a/solution.py
+++ b/solution.py
@@ -16,10 +16,10 @@
 
 CORE_ROWS = [[core + 2 * i for i in range(8)] for core in range(2)]
 CORE_ALL = [[(core + 2 * i) * 8 + c for i in range(8) for c in range(8)] for core in range(2)]
-Y_UP = [(c, c // 4 * 4 + (c + 1) % 4) for c in range(8)]
-Y_DOWN = [(b, a) for a, b in Y_UP]
-STRIP_DOWN = [(d, (d + 1) % 128) for d in range(128)]
-STRIP_UP = [(b, a) for a, b in STRIP_DOWN]
+Y_OUTER = [(c, c ^ 1) for c in range(8)]
+Y_INNER = [(c, c // 4 * 4 + (0, 2, 1, 3)[c % 4]) for c in range(8)]
+STRIP_NEAR = [(d, d ^ 1) for d in range(128)]
+STRIP_FAR = [(d, ((d + 1) ^ 1) - 1 if 0 < d < 127 else 127 - d) for d in range(128)]
 
 
 def twice_gelu(x):
@@ -121,34 +121,46 @@
     lax.fori_loop(0, 2, depth, 0)
 
 
-def pick_pieces(own_ref, up_ref, down_ref):
+def pick_pieces(own_ref, outer_ref, inner_ref):
     v = own_y()
 
-    def pick(m, carry):
-        n_up = v + 1
-        row = jnp.minimum(2 * v + m // n_up, 5)
-        up_ref[m] = own_ref[row * 4 + jnp.clip(3 - v + lax.rem(m, n_up), 0, 3)]
-        n_down = 4 - v
-        row = jnp.minimum(m // n_down, 5)
-        down_ref[m] = own_ref[row * 4 + lax.rem(m, n_down)]
-        return carry
-
-    lax.fori_loop(0, 8, pick, 0)
-
-
-def expand_halo(half, top_ref, bot_ref, scale, shift, we_ref, e_ref, rows):
+    def pick(m, up):
+        wide = jnp.where(up, v + 1, 4 - v)
+        first = jnp.where(up, 2 * v, 0)
+        row = jnp.minimum(first + m // wide, 5)
+        tp = jnp.clip(jnp.where(up, 3 - v, 0) + lax.rem(m, wide), 0, 3)
+        return own_ref[row * 4 + tp]
+
+    def pick_outer(m, carry):
+        outer_ref[m] = pick(m, lax.rem(v, 2) == 0)
+        return carry
+
+    def pick_inner(m, carry):
+        inner_ref[m] = pick(m, v < 2)
+        return carry
+
+    lax.fori_loop(0, 6, pick_outer, 0)
+    lax.fori_loop(0, 8, pick_inner, 0)
+
+
+def expand_halo(half, near_ref, far_ref, scale, shift, we_ref, e_ref, rows):
     device = lax.axis_index("rows") * 8 + lax.axis_index("cols")
+    even = lax.rem(device, 2) == 0
     cols = slice(FIRST[half], FIRST[half] + SPAN)
-    for ref, row, present in ((top_ref, rows[0], device > 0), (bot_ref, rows[1], device < 127)):
-        expand_row(ref[0, cols], scale, shift, we_ref, e_ref, row, present.astype(F32))
+    above, below = rows
+    row = jnp.where(even, below, above)
+    expand_row(near_ref[0, cols], scale, shift, we_ref, e_ref, row, None)
+    inside = jnp.logical_and(device > 0, device < 127).astype(F32)
+    row = jnp.where(even, above, below)
+    expand_row(far_ref[0, cols], scale, shift, we_ref, e_ref, row, inside)
 
 
 def edge_kernel(
-    x_ref, top_ref, bot_ref, e_ref, mid_ref, scale_ref, shift_ref, we_ref, dw_ref, wp_ref,
-    own_ref, up_ref, down_ref, halo_ref,
+    x_ref, near_ref, far_ref, e_ref, mid_ref, scale_ref, shift_ref, we_ref, dw_ref, wp_ref,
+    own_ref, outer_ref, inner_ref, halo_ref,
 ):
     clear_edges(halo_ref)
-    expand_halo(0, top_ref, bot_ref, scale_ref[...], shift_ref[...], we_ref, halo_ref, (0, 1))
+    expand_halo(0, near_ref, far_ref, scale_ref[...], shift_ref[...], we_ref, halo_ref, (0, 1))
     taps = dw_ref[...] * 0.5
     sources = [(halo_ref, 0), (e_ref, 0), (e_ref, 1)]
     depth_row(0, sources, x_ref[0, 0:256], taps, wp_ref, own_ref, 0)
@@ -160,16 +172,16 @@
         return carry
 
     lax.fori_loop(0, 16, keep, 0)
-    pick_pieces(own_ref, up_ref, down_ref)
+    pick_pieces(own_ref, outer_ref, inner_ref)
 
 
 def right_kernel(
-    x_ref, top_ref, bot_ref, scale_ref, shift_ref, we_ref, dw_ref, wp_ref,
-    own_ref, up_ref, down_ref, e_ref,
+    x_ref, near_ref, far_ref, scale_ref, shift_ref, we_ref, dw_ref, wp_ref,
+    own_ref, outer_ref, inner_ref, e_ref,
 ):
     clear_edges(e_ref)
     scale, shift = scale_ref[...], shift_ref[...]
-    expand_halo(1, top_ref, bot_ref, scale, shift, we_ref, e_ref, (0, 7))
+    expand_halo(1, near_ref, far_ref, scale, shift, we_ref, e_ref, (0, 7))
     cols = slice(FIRST[1], FIRST[1] + SPAN)
 
     def expand(step, carry):
@@ -187,7 +199,7 @@
         return carry
 
     lax.fori_loop(0, 3, depth, 0)
-    pick_pieces(own_ref, up_ref, down_ref)
+    pick_pieces(own_ref, outer_ref, inner_ref)
 
 
 def vmem(limit):
@@ -217,24 +229,24 @@
     )(strips, scale, shift, we, dw, wp)
 
 
-def bottleneck_edge(strips, top, bot, expanded, middle, scale, shift, we, dw, wp):
+def bottleneck_edge(strips, near, far, expanded, middle, scale, shift, we, dw, wp):
     return pl.pallas_call(
         edge_kernel,
-        out_shape=[pieces(24), pieces(8), pieces(8)],
+        out_shape=[pieces(24), pieces(6), pieces(8)],
         scratch_shapes=[pltpu.VMEM((2, 8, SPAN + 2 * PAD, 128), F32)],
         compiler_params=vmem(24),
         name="bottleneck_edge",
-    )(strips, top, bot, expanded, middle, scale, shift, we, dw, wp)
-
-
-def bottleneck_right(strips, top, bot, scale, shift, we, dw, wp):
+    )(strips, near, far, expanded, middle, scale, shift, we, dw, wp)
+
+
+def bottleneck_right(strips, near, far, scale, shift, we, dw, wp):
     return pl.pallas_call(
         right_kernel,
-        out_shape=[pieces(24), pieces(8), pieces(8)],
+        out_shape=[pieces(24), pieces(6), pieces(8)],
         scratch_shapes=[pltpu.VMEM((8, 8, SPAN + 2 * PAD, 128), F32)],
         compiler_params=vmem(24),
         name="bottleneck_right",
-    )(strips, top, bot, scale, shift, we, dw, wp)
+    )(strips, near, far, scale, shift, we, dw, wp)
 
 
 def normed_of(x, gain):
@@ -322,14 +334,15 @@
             owner = row // 6
             local = row - 6 * owner
             v = jnp.maximum(y - 1, 0)
-            m_up = jnp.clip((local - 2 * v) * (v + 1) + tp - (3 - v), 0, 7)
+            m_up = (local - 2 * v) * (v + 1) + tp - (3 - v)
             v = jnp.minimum(y + 1, 3)
-            m_down = jnp.clip(local * (4 - v) + tp, 0, 7)
-            places.append((owner, local * 4 + tp, m_up, m_down))
+            m = jnp.where(owner < y, m_up, local * (4 - v) + tp)
+            outer = owner // 2 == y // 2
+            places.append((owner, local * 4 + tp, outer, jnp.clip(m, 0, 5), jnp.clip(m, 0, 7)))
     return y, places
 
 
-def block_kernel(half, own_ref, up_ref, down_ref, *refs):
+def block_kernel(half, own_ref, outer_ref, inner_ref, *refs):
     w = dict(zip(NAMES, refs))
     refs = refs[len(NAMES) :]
     if half == 1:
@@ -339,11 +352,11 @@
         (out_ref,) = refs
     y, places = block_places()
     units = []
-    for owner, at, m_up, m_down in places:
+    for owner, at, outer, m_outer, m_inner in places:
         mine = own_ref[at].astype(F32)
-        above = up_ref[m_up].astype(F32)
-        below = down_ref[m_down].astype(F32)
-        units.append(jnp.where(owner == y, mine, jnp.where(owner < y, above, below)))
+        one = outer_ref[m_outer].astype(F32)
+        two = inner_ref[m_inner].astype(F32)
+        units.append(jnp.where(owner == y, mine, jnp.where(outer, one, two)))
     windows = [(k, jj, t) for k in range(3) for jj in range(4) for t in range(2)]
     x = jnp.concatenate(
         [units[k * 8 + s][jj, t * 8 : (t + 1) * 8, :] for k, jj, t in windows for s in range(8)],
@@ -392,13 +405,13 @@
     lax.fori_loop(0, 3, slot, 0)
 
 
-def block_section(half, own, up, down, weights, *done):
+def block_section(half, own, outer, inner, weights, *done):
     return pl.pallas_call(
         functools.partial(block_kernel, half),
         out_shape=jax.ShapeDtypeStruct((8, 3, 4 if half == 0 else 8, 16, 256), BF16),
         compiler_params=vmem(24),
         name="block_section",
-    )(own, up, down, *weights, *done)
+    )(own, outer, inner, *weights, *done)
 
 
 def grid_section(x, weights):
@@ -418,17 +431,24 @@
 ):
     row = lambda a: a.reshape(1, -1)
     both = ("rows", "cols")
-    top = lax.ppermute(stem_strips[5:6], both, STRIP_DOWN)
-    bot = lax.ppermute(stem_strips[0:1], both, STRIP_UP)
+    even = lax.rem(lax.axis_index("cols"), 2) == 0
+    first, last = stem_strips[0:1], stem_strips[5:6]
+    near = lax.ppermute(jnp.where(even, last, first), both, STRIP_NEAR)
+    far = lax.ppermute(jnp.where(even, first, last), both, STRIP_FAR)
     weights = (row(norm_scale), row(norm_shift), expand_weight, depth_weight, project_weight)
     middle, expanded = bottleneck_middle(
         *[pltpu.with_memory_space_constraint(a, pltpu.HBM) for a in (stem_strips, *weights)]
     )
-    own_l, up_l, down_l = bottleneck_edge(stem_strips, top, bot, expanded, middle, *weights)
-    own_l, up_l, down_l, top, bot = lax.optimization_barrier((own_l, up_l, down_l, top, bot))
-    up_l, down_l = lax.ppermute(up_l, "cols", Y_UP), lax.ppermute(down_l, "cols", Y_DOWN)
-    own_r, up_r, down_r = bottleneck_right(stem_strips, top, bot, *weights)
-    up_r, down_r = lax.ppermute(up_r, "cols", Y_UP), lax.ppermute(down_r, "cols", Y_DOWN)
+    own_l, outer_l, inner_l = bottleneck_edge(stem_strips, near, far, expanded, middle, *weights)
+    own_l, outer_l, inner_l, near, far = lax.optimization_barrier((own_l, outer_l, inner_l, near, far))
+    outer_l = lax.ppermute(outer_l, "cols", Y_OUTER)
+    inner_l = lax.ppermute(inner_l, "cols", Y_INNER)
+    own_r, outer_r, inner_r = bottleneck_right(stem_strips, near, far, *weights)
+    outer_l, inner_l, outer_r, inner_r = lax.optimization_barrier(
+        (outer_l, inner_l, outer_r, inner_r)
+    )
+    outer_r = lax.ppermute(outer_r, "cols", Y_OUTER)
+    inner_r = lax.ppermute(inner_r, "cols", Y_INNER)
     block_weights = (
         row(block_gain), block_inputs, block_output, block_bias,
         row(first_gain), first_up, first_down,
@@ -437,8 +457,8 @@
         row(grid_gain), grid_inputs, grid_output, grid_bias,
         row(second_gain), second_up, second_down,
     )
-    left = block_section(0, own_l, up_l, down_l, block_weights)
-    sent = block_section(1, own_r, up_r, down_r, block_weights, left)
+    left = block_section(0, own_l, outer_l, inner_l, block_weights)
+    sent = block_section(1, own_r, outer_r, inner_r, block_weights, left)
     arrived = lax.all_to_all(sent, "rows", 0, 0, axis_index_groups=CORE_ROWS, tiled=True)
     back = grid_section(arrived, grid_weights)
     landed = lax.all_to_all(back, both, 0, 0, axis_index_groups=CORE_ALL, tiled=True)

time: 124 us -> 122 us (0.984)
  waiting for transfers between devices: 4.24 us -> 0.02 us
  starting transfers between devices: 15.1 us -> 16.6 us
    ppermute x6, waiting for transfers between devices: 4.24 us -> 0.02 us  [the longest x1 0.01 us: body(): far = lax.ppermute(jnp.where(even, first, last), both, STRIP_FAR)]
    ppermute x6, starting transfers between devices: 15.1 us -> 16.6 us  [the longest x1 8.28 us: body(): far = lax.ppermute(jnp.where(even, first, last), both, STRIP_FAR)]
  transfers between devices with their start and end apart: 6 -> 6, of which waited for: 1 -> 0; matrix products, arithmetic and copies ran while one was open for 0% -> 0% of each run, Pallas kernels for 18% -> 18%
where the time goes in v6:
time: 122 us; the launch traced here: 121 us
  blocking collectives  52.6 us (43%)
  Pallas kernels  49.3 us (40%)
  starting transfers between devices  16.6 us (14%)
  local copies, waits for them, and re-layouts  1.37 us (1%)
    all_to_all x1, blocking collectives, body(): lax.all_to_all(back, both, 0, 0, axis_index_groups=CORE_ALL, tiled=True)  27.5 us
    all_to_all x1, blocking collectives, body(): lax.all_to_all(sent, 'rows', 0, 0, axis_index_groups=CORE_ROWS, tiled=True)  25.1 us
    pallas_call x1, Pallas kernels, grid_section(): pl.pallas_call(grid_kernel, out_shape=jax.ShapeDtypeStruct((64, 3, 16, 25...  16 us
    pallas_call x2, Pallas kernels, block_section(): pl.pallas_call(functools.partial(block_kernel, half), out_shape=jax.Shape...  15 us
    ppermute x1, starting transfers between devices, body(): far = lax.ppermute(jnp.where(even, first, last), both, STRIP_FAR)  8.28 us
    pallas_call x1, Pallas kernels, bottleneck_right(): pl.pallas_call(right_kernel, out_shape=[pieces(24), pieces(6), pieces(8)]...  7.97 us
    pallas_call x1, Pallas kernels, bottleneck_middle(): pl.pallas_call(middle_kernel, out_shape=[pieces(16), jax.ShapeDtypeStruct...  6.98 us
    ppermute x1, starting transfers between devices, body(): outer_r = lax.ppermute(outer_r, 'cols', Y_OUTER)  3.53 us
  transfers between devices with their start and end apart: 6, of which 0 were waited for; matrix products, arithmetic and copies ran while one was open for 0% of the time, Pallas kernels for 18%

profile of v6, /device:TPU:0, one launch (start us, length us, event | category | flops | bytes accessed | tf_op | source)
XLA Modules:
  0.0 121.3 jit_solution(11004175912957947541)
XLA Ops:
  0.0 1.1 broadcast_select_fusion
  1.1 0.0 copy-start
  1.1 0.0 copy-start.1
  1.1 0.0 copy-start.2
  1.1 0.0 copy-start.7
  1.1 0.0 copy-start.14
  1.1 0.0 copy-start.15
  1.1 8.3 %collective-permute-start.1 = (bf16[1,512,256]{2,1,0:T(8,128)(2,1)S(1)}, bf16[1,512,256]{2,1,0:T(8,128)(2,1)S(1)}, u32[]{:S(2)}, u32[]{:S(2)}) collective-permute-start(bf16[1,512,256]{2,1,0:T(8,128)(2,1)S(1)} %get-tuple-element.39), channel_id=1, source_target_pairs={{0,127},{1,2},{2,1},{3,4},{4,3},{5,6},{6,5},{7,8},{8,7},{9,10},{10... | collective-permute-start | bytes 786440 | tf_op jit(solution)/shard_map/ppermute | solution.py:437
  9.4 0.0 collective-permute-start
  9.4 7.0 %bottleneck_middle.1 = (bf16[16,4,16,256]{3,2,1,0:T(8,128)(2,1)S(1)}, f32[6,8,288,128]{3,2,1,0:T(8,128)S(1)}) custom-call(bf16[6,512,256]{2,1,0:T(8,128)(2,1)} %x_ref.3, f32[1,256]{1,0:T(1,128)} %bitcast.10, f32[1,256]{1,0:T(1,128)} %bitcast.13, bf16[256,1024]{1,0:T(8,128)(2,1)} %we_ref.3, f32[9,1024]{1,0:T(8,128)} %dw_ref.3, bf16[1024,256]{1,0:T(8,128)(2,1)} %wp_ref.3), custom_call_target="tpu_custom_call" | custom-call | tf_op jit(solution)/shard_map/bottleneck_middle/pallas_call | solution.py:214
  16.4 0.0 collective-permute-done.1.far_ref
  16.4 0.0 collective-permute-done.near_ref
  16.4 0.0 copy-done
  16.4 0.0 copy-done.1
  16.5 0.0 copy-done.2
  16.5 0.0 copy-done.7
  16.5 0.0 copy-done.14
  16.5 3.4 %bottleneck_edge.1 = (bf16[24,4,16,256]{3,2,1,0:T(8,128)(2,1)S(1)}, bf16[6,4,16,256]{3,2,1,0:T(8,128)(2,1)S(1)}, bf16[8,4,16,256]{3,2,1,0:T(8,128)(2,1)S(1)}) custom-call(bf16[6,512,256]{2,1,0:T(8,128)(2,1)S(1)} %copy-done, bf16[1,512,256]{2,1,0:T(8,128)(2,1)S(1)} %collective-permute-done.near_ref, bf16[1,512,256]{2,1,0:T(8,128)(2,1)S(1)} %collective-permute-done.1.far_ref, ...), custom_call_target="tpu_custom_call" | custom-call | tf_op jit(solution)/shard_map/bottleneck_edge/pallas_call | solution.py:233
  19.9 0.0 copy-start.3
  19.9 0.0 copy-start.4
  19.9 0.0 copy-start.5
  19.9 0.0 copy-start.6
  19.9 0.0 copy-start.10
  19.9 0.0 copy-start.16
  19.9 0.0 copy-start.17
  20.0 0.8 collective-permute-start.3
  20.8 3.3 %collective-permute-start.2 = (bf16[6,4,16,256]{3,2,1,0:T(8,128)(2,1)S(1)}, bf16[6,4,16,256]{3,2,1,0:T(8,128)(2,1)S(1)}, u32[]{:S(2)}, u32[]{:S(2)}) collective-permute-start(bf16[6,4,16,256]{3,2,1,0:T(8,128)(2,1)S(1)} %get-tuple-element.30), channel_id=1, source_target_pairs={{0,1},{1,0},{2,3},{3,2},{4,5},{5,4},{6,7},{7,6},{8,9},{9,8},{10,11... | collective-permute-start | bytes 589832 | tf_op jit(solution)/shard_map/ppermute | solution.py:444
  24.1 8.0 %bottleneck_right.1 = (bf16[24,4,16,256]{3,2,1,0:T(8,128)(2,1)S(1)}, bf16[6,4,16,256]{3,2,1,0:T(8,128)(2,1)S(1)}, bf16[8,4,16,256]{3,2,1,0:T(8,128)(2,1)S(1)}) custom-call(bf16[6,512,256]{2,1,0:T(8,128)(2,1)S(1)} %copy-done, bf16[1,512,256]{2,1,0:T(8,128)(2,1)S(1)} %collective-permute-done.near_ref, bf16[1,512,256]{2,1,0:T(8,128)(2,1)S(1)} %collective-permute-done.1.far_ref, ...), custom_call_target="tpu_custom_call" | custom-call | tf_op jit(solution)/shard_map/bottleneck_right/pallas_call | solution.py:243
  32.1 0.0 collective-permute-done.2.outer_ref
  32.1 0.0 collective-permute-done.3.inner_ref
  32.1 0.7 collective-permute-start.5
  32.8 3.5 %collective-permute-start.4 = (bf16[6,4,16,256]{3,2,1,0:T(8,128)(2,1)S(1)}, bf16[6,4,16,256]{3,2,1,0:T(8,128)(2,1)S(1)}, u32[]{:S(2)}, u32[]{:S(2)}) collective-permute-start(bf16[6,4,16,256]{3,2,1,0:T(8,128)(2,1)S(1)} %get-tuple-element.34), channel_id=1, source_target_pairs={{0,1},{1,0},{2,3},{3,2},{4,5},{5,4},{6,7},{7,6},{8,9},{9,8},{10,11... | collective-permute-start | bytes 589832 | tf_op jit(solution)/shard_map/ppermute | solution.py:450
  36.3 7.3 %block_section.2.refs_7_ = bf16[8,3,4,16,256]{4,3,2,1,0:T(8,128)(2,1)S(1)} custom-call(bf16[24,4,16,256]{3,2,1,0:T(8,128)(2,1)S(1)} %get-tuple-element.36.own_ref, bf16[6,4,16,256]{3,2,1,0:T(8,128)(2,1)S(1)} %collective-permute-done.2.outer_ref, bf16[8,4,16,256]{3,2,1,0:T(8,128)(2,1)S(1)} %collective-permute-done.3.inner_ref, f32[1,256]{1,0:T(1,128)S(1)} %bitcast.16, ...), custom_call_target="tpu_custom_call" | custom-call | tf_op jit(solution)/shard_map/block_section/pallas_call | solution.py:409
  43.7 0.0 collective-permute-done.4.outer_ref
  43.7 0.0 collective-permute-done.5.inner_ref
  43.7 7.6 %block_section.3 = bf16[8,3,8,16,256]{4,3,2,1,0:T(8,128)(2,1)S(1)} custom-call(bf16[24,4,16,256]{3,2,1,0:T(8,128)(2,1)S(1)} %get-tuple-element.29.own_ref, bf16[6,4,16,256]{3,2,1,0:T(8,128)(2,1)S(1)} %collective-permute-done.4.outer_ref, bf16[8,4,16,256]{3,2,1,0:T(8,128)(2,1)S(1)} %collective-permute-done.5.inner_ref, f32[1,256]{1,0:T(1,128)S(1)} %bitcast.17, ...), custom_call_target="tpu_custom_call" | custom-call | tf_op jit(solution)/shard_map/block_section/pallas_call | solution.py:409
  51.3 0.0 copy-start.8
  51.4 0.0 copy-start.9
  51.4 0.0 copy-start.11
  51.4 0.0 copy-start.12
  51.4 0.0 copy-start.13
  51.4 0.0 copy-start.18
  51.4 0.0 copy-start.19
  51.4 25.1 %all_to_all.10.x_ref = bf16[8,3,8,16,256]{4,3,2,1,0:T(8,128)(2,1)S(1)} all-to-all(bf16[8,3,8,16,256]{4,3,2,1,0:T(8,128)(2,1)S(1)} %block_section.3), channel_id=1, replica_groups={{0,16,32,48,64,80,96,112},{8,24,40,56,72,88,104,120},{1,17,33,49,65,81,..., dimensions={0} | all-to-all | bytes 3145728 | tf_op jit(solution)/shard_map/all_to_all | solution.py:462
  76.6 0.0 copy-done.8
  76.6 16.0 %grid_section.1 = bf16[64,3,16,256]{3,2,1,0:T(8,128)(2,1)S(1)} custom-call(bf16[8,3,8,16,256]{4,3,2,1,0:T(8,128)(2,1)S(1)} %all_to_all.10.x_ref, f32[1,256]{1,0:T(1,128)S(1)} %bitcast.20, bf16[256,768]{1,0:T(8,128)(2,1)S(1)} %copy-done.11, bf16[256,256]{1,0:T(8,128)(2,1)S(1)} %copy-done.13, f32[8,64,64]{2,1,0:T(8,128)S(1)} %copy-done.12, ...), custom_call_target="tpu_custom_call" | custom-call | tf_op jit(solution)/shard_map/grid_section/pallas_call | solution.py:418
  92.6 27.5 %all_to_all.11 = bf16[64,3,16,256]{3,2,1,0:T(8,128)(2,1)S(1)} all-to-all(bf16[64,3,16,256]{3,2,1,0:T(8,128)(2,1)S(1)} %grid_section.1), channel_id=1, replica_groups={{0,1,2,3,4,5,6,7,16,17,18,19,20,21,22,23,32,33,34,35,36,37,38,39,48,49,..., dimensions={0} | all-to-all | bytes 3145728 | tf_op jit(solution)/shard_map/all_to_all | solution.py:464
  120.1 1.2 %copy.21 = bf16[2,3,8,4,16,256]{5,4,3,2,1,0:T(8,128)(2,1)} copy(bf16[2,3,8,4,16,256]{5,4,3,1,0,2:T(8,128)(2,1)S(1)} %bitcast.22) | data formatting | bytes 3145728 | tf_op jit(solution)/shard_map/transpose | solution.py:465
  (14 shorter events, 0.0 us)
Async XLA Ops:
  1.1 15.4 %copy-start = (bf16[6,512,256]{2,1,0:T(8,128)(2,1)S(1)}, bf16[6,512,256]{2,1,0:T(8,128)(2,1)}, u32[]{:S(2)}) copy-start(bf16[6,512,256]{2,1,0:T(8,128)(2,1)} %x_ref.3) | copy-start | bytes 4718596
  1.1 15.4 %copy-start.1 = (bf16[256,1024]{1,0:T(8,128)(2,1)S(1)}, bf16[256,1024]{1,0:T(8,128)(2,1)}, u32[]{:S(2)}) copy-start(bf16[256,1024]{1,0:T(8,128)(2,1)} %we_ref.3) | copy-start | bytes 1572868
  1.1 15.4 %copy-start.2 = (bf16[1024,256]{1,0:T(8,128)(2,1)S(1)}, bf16[1024,256]{1,0:T(8,128)(2,1)}, u32[]{:S(2)}) copy-start(bf16[1024,256]{1,0:T(8,128)(2,1)} %wp_ref.3) | copy-start | bytes 1572868
  1.1 15.4 %copy-start.7 = (f32[9,1024]{1,0:T(8,128)S(1)}, f32[9,1024]{1,0:T(8,128)}, u32[]{:S(2)}) copy-start(f32[9,1024]{1,0:T(8,128)} %dw_ref.3) | copy-start | bytes 110596
  1.1 15.4 %copy-start.14 = (f32[256]{0:T(256)S(1)}, f32[256]{0:T(256)}, u32[]{:S(2)}) copy-start(f32[256]{0:T(256)} %param.21) | copy-start | bytes 3076
  1.1 15.4 %copy-start.15 = (f32[256]{0:T(256)S(1)}, f32[256]{0:T(256)}, u32[]{:S(2)}) copy-start(f32[256]{0:T(256)} %param.22) | copy-start | bytes 3076
  1.1 15.3 %collective-permute-start.1 = (bf16[1,512,256]{2,1,0:T(8,128)(2,1)S(1)}, bf16[1,512,256]{2,1,0:T(8,128)(2,1)S(1)}, u32[]{:S(2)}, u32[]{:S(2)}) collective-permute-start(bf16[1,512,256]{2,1,0:T(8,128)(2,1)S(1)} %get-tuple-element.39), channel_id=1, source_target_pairs={{0,127},{1,2},{2,1},{3,4},{4,3},{5,6},{6,5},{7,8},{8,7},{9,10},{10... | collective-permute-start | bytes 786440 | tf_op jit(solution)/shard_map/ppermute | solution.py:437
  9.4 7.0 %collective-permute-start = (bf16[1,512,256]{2,1,0:T(8,128)(2,1)S(1)}, bf16[1,512,256]{2,1,0:T(8,128)(2,1)S(1)}, u32[]{:S(2)}, u32[]{:S(2)}) collective-permute-start(bf16[1,512,256]{2,1,0:T(8,128)(2,1)S(1)} %get-tuple-element.40), channel_id=1, source_target_pairs={{0,1},{1,0},{2,3},{3,2},{4,5},{5,4},{6,7},{7,6},{8,9},{9,8},{10,11... | collective-permute-start | bytes 786440 | tf_op jit(solution)/shard_map/ppermute | solution.py:436
  19.9 16.4 %copy-start.3 = (bf16[256,1024]{1,0:T(8,128)(2,1)S(1)}, bf16[256,1024]{1,0:T(8,128)(2,1)}, u32[]{:S(2)}) copy-start(bf16[256,1024]{1,0:T(8,128)(2,1)} %refs_5_.4) | copy-start | bytes 1572868
  19.9 16.4 %copy-start.4 = (bf16[1024,256]{1,0:T(8,128)(2,1)S(1)}, bf16[1024,256]{1,0:T(8,128)(2,1)}, u32[]{:S(2)}) copy-start(bf16[1024,256]{1,0:T(8,128)(2,1)} %refs_6_.4) | copy-start | bytes 1572868
  19.9 16.4 %copy-start.5 = (bf16[256,768]{1,0:T(8,128)(2,1)S(1)}, bf16[256,768]{1,0:T(8,128)(2,1)}, u32[]{:S(2)}) copy-start(bf16[256,768]{1,0:T(8,128)(2,1)} %refs_1_.4) | copy-start | bytes 1179652
  19.9 16.4 %copy-start.6 = (f32[8,64,64]{2,1,0:T(8,128)S(1)}, f32[8,64,64]{2,1,0:T(8,128)}, u32[]{:S(2)}) copy-start(f32[8,64,64]{2,1,0:T(8,128)} %refs_3_.4) | copy-start | bytes 393220
  19.9 16.4 %copy-start.10 = (bf16[256,256]{1,0:T(8,128)(2,1)S(1)}, bf16[256,256]{1,0:T(8,128)(2,1)}, u32[]{:S(2)}) copy-start(bf16[256,256]{1,0:T(8,128)(2,1)} %refs_2_.4) | copy-start | bytes 393220
  19.9 16.4 %copy-start.16 = (f32[256]{0:T(256)S(1)}, f32[256]{0:T(256)}, u32[]{:S(2)}) copy-start(f32[256]{0:T(256)} %param.26) | copy-start | bytes 3076
  19.9 16.4 %copy-start.17 = (f32[256]{0:T(256)S(1)}, f32[256]{0:T(256)}, u32[]{:S(2)}) copy-start(f32[256]{0:T(256)} %param.30) | copy-start | bytes 3076
  20.0 12.1 %collective-permute-start.3 = (bf16[8,4,16,256]{3,2,1,0:T(8,128)(2,1)S(1)}, bf16[8,4,16,256]{3,2,1,0:T(8,128)(2,1)S(1)}, u32[]{:S(2)}, u32[]{:S(2)}) collective-permute-start(bf16[8,4,16,256]{3,2,1,0:T(8,128)(2,1)S(1)} %get-tuple-element.31), channel_id=1, source_target_pairs={{0,0},{1,2},{2,1},{3,3},{4,4},{5,6},{6,5},{7,7},{8,8},{9,10},{10,9... | collective-permute-start | bytes 786440 | tf_op jit(solution)/shard_map/ppermute | solution.py:445
  20.8 11.3 %collective-permute-start.2 = (bf16[6,4,16,256]{3,2,1,0:T(8,128)(2,1)S(1)}, bf16[6,4,16,256]{3,2,1,0:T(8,128)(2,1)S(1)}, u32[]{:S(2)}, u32[]{:S(2)}) collective-permute-start(bf16[6,4,16,256]{3,2,1,0:T(8,128)(2,1)S(1)} %get-tuple-element.30), channel_id=1, source_target_pairs={{0,1},{1,0},{2,3},{3,2},{4,5},{5,4},{6,7},{7,6},{8,9},{9,8},{10,11... | collective-permute-start | bytes 589832 | tf_op jit(solution)/shard_map/ppermute | solution.py:444
  32.1 11.6 %collective-permute-start.5 = (bf16[8,4,16,256]{3,2,1,0:T(8,128)(2,1)S(1)}, bf16[8,4,16,256]{3,2,1,0:T(8,128)(2,1)S(1)}, u32[]{:S(2)}, u32[]{:S(2)}) collective-permute-start(bf16[8,4,16,256]{3,2,1,0:T(8,128)(2,1)S(1)} %get-tuple-element.35), channel_id=1, source_target_pairs={{0,0},{1,2},{2,1},{3,3},{4,4},{5,6},{6,5},{7,7},{8,8},{9,10},{10,9... | collective-permute-start | bytes 786440 | tf_op jit(solution)/shard_map/ppermute | solution.py:451
  32.8 10.9 %collective-permute-start.4 = (bf16[6,4,16,256]{3,2,1,0:T(8,128)(2,1)S(1)}, bf16[6,4,16,256]{3,2,1,0:T(8,128)(2,1)S(1)}, u32[]{:S(2)}, u32[]{:S(2)}) collective-permute-start(bf16[6,4,16,256]{3,2,1,0:T(8,128)(2,1)S(1)} %get-tuple-element.34), channel_id=1, source_target_pairs={{0,1},{1,0},{2,3},{3,2},{4,5},{5,4},{6,7},{7,6},{8,9},{9,8},{10,11... | collective-permute-start | bytes 589832 | tf_op jit(solution)/shard_map/ppermute | solution.py:450
  51.3 25.2 %copy-start.8 = (bf16[256,1024]{1,0:T(8,128)(2,1)S(1)}, bf16[256,1024]{1,0:T(8,128)(2,1)}, u32[]{:S(2)}) copy-start(bf16[256,1024]{1,0:T(8,128)(2,1)} %refs_5_.5) | copy-start | bytes 1572868
  51.4 25.2 %copy-start.9 = (bf16[1024,256]{1,0:T(8,128)(2,1)S(1)}, bf16[1024,256]{1,0:T(8,128)(2,1)}, u32[]{:S(2)}) copy-start(bf16[1024,256]{1,0:T(8,128)(2,1)} %refs_6_.5) | copy-start | bytes 1572868
  51.4 25.2 %copy-start.11 = (bf16[256,768]{1,0:T(8,128)(2,1)S(1)}, bf16[256,768]{1,0:T(8,128)(2,1)}, u32[]{:S(2)}) copy-start(bf16[256,768]{1,0:T(8,128)(2,1)} %refs_1_.5) | copy-start | bytes 1179652
  51.4 25.2 %copy-start.12 = (f32[8,64,64]{2,1,0:T(8,128)S(1)}, f32[8,64,64]{2,1,0:T(8,128)}, u32[]{:S(2)}) copy-start(f32[8,64,64]{2,1,0:T(8,128)} %refs_3_.5) | copy-start | bytes 393220
  51.4 25.2 %copy-start.13 = (bf16[256,256]{1,0:T(8,128)(2,1)S(1)}, bf16[256,256]{1,0:T(8,128)(2,1)}, u32[]{:S(2)}) copy-start(bf16[256,256]{1,0:T(8,128)(2,1)} %refs_2_.5) | copy-start | bytes 393220
  51.4 25.2 %copy-start.18 = (f32[256]{0:T(256)S(1)}, f32[256]{0:T(256)}, u32[]{:S(2)}) copy-start(f32[256]{0:T(256)} %param.33) | copy-start | bytes 3076
  51.4 25.2 %copy-start.19 = (f32[256]{0:T(256)S(1)}, f32[256]{0:T(256)}, u32[]{:S(2)}) copy-start(f32[256]{0:T(256)} %param.37) | copy-start | bytes 3076

commit v7 on v6

--- a/solution.py
+++ b/solution.py
@@ -314,7 +314,7 @@
     for c in range(4):
         cols = slice(c * 256, (c + 1) * 256)
         hidden = jnp.dot(normed, w["up"][:, cols], preferred_element_type=F32)
-        hidden = twice_gelu(hidden).astype(BF16)
+        hidden = twice_gelu_short(hidden)
         total = total + jnp.dot(hidden, w["down"][cols, :], preferred_element_type=F32)
     return x + 0.5 * total
 

time: 122 us -> 121 us (level)
  no operation moved by 1% of the time
where the time goes in v7:
time: 121 us; the launch traced here: 120 us
  blocking collectives  52.8 us (44%)
  Pallas kernels  48.2 us (40%)
  starting transfers between devices  16.6 us (14%)
  local copies, waits for them, and re-layouts  1.37 us (1%)
    all_to_all x1, blocking collectives, body(): lax.all_to_all(back, both, 0, 0, axis_index_groups=CORE_ALL, tiled=True)  27.7 us
    all_to_all x1, blocking collectives, body(): lax.all_to_all(sent, 'rows', 0, 0, axis_index_groups=CORE_ROWS, tiled=True)  25.1 us
    pallas_call x1, Pallas kernels, grid_section(): pl.pallas_call(grid_kernel, out_shape=jax.ShapeDtypeStruct((64, 3, 16, 25...  15.5 us
    pallas_call x2, Pallas kernels, block_section(): pl.pallas_call(functools.partial(block_kernel, half), out_shape=jax.Shape...  14.4 us
    ppermute x1, starting transfers between devices, body(): far = lax.ppermute(jnp.where(even, first, last), both, STRIP_FAR)  8.28 us
    pallas_call x1, Pallas kernels, bottleneck_right(): pl.pallas_call(right_kernel, out_shape=[pieces(24), pieces(6), pieces(8)]...  7.97 us
    pallas_call x1, Pallas kernels, bottleneck_middle(): pl.pallas_call(middle_kernel, out_shape=[pieces(16), jax.ShapeDtypeStruct...  6.98 us
    ppermute x1, starting transfers between devices, body(): outer_r = lax.ppermute(outer_r, 'cols', Y_OUTER)  3.53 us
  transfers between devices with their start and end apart: 6, of which 0 were waited for; matrix products, arithmetic and copies ran while one was open for 0% of the time, Pallas kernels for 18%

profile of v7, /device:TPU:0, one launch (start us, length us, event | category | flops | bytes accessed | tf_op | source)
XLA Modules:
  0.0 120.5 jit_solution(3813362441544845570)
XLA Ops:
  0.0 1.1 broadcast_select_fusion
  1.1 0.0 copy-start
  1.1 0.0 copy-start.1
  1.1 0.0 copy-start.2
  1.1 0.0 copy-start.7
  1.1 0.0 copy-start.14
  1.1 0.0 copy-start.15
  1.1 8.3 %collective-permute-start.1 = (bf16[1,512,256]{2,1,0:T(8,128)(2,1)S(1)}, bf16[1,512,256]{2,1,0:T(8,128)(2,1)S(1)}, u32[]{:S(2)}, u32[]{:S(2)}) collective-permute-start(bf16[1,512,256]{2,1,0:T(8,128)(2,1)S(1)} %get-tuple-element.39), channel_id=1, source_target_pairs={{0,127},{1,2},{2,1},{3,4},{4,3},{5,6},{6,5},{7,8},{8,7},{9,10},{10... | collective-permute-start | bytes 786440 | tf_op jit(solution)/shard_map/ppermute | solution.py:437
  9.4 0.0 collective-permute-start
  9.4 7.0 %bottleneck_middle.1 = (bf16[16,4,16,256]{3,2,1,0:T(8,128)(2,1)S(1)}, f32[6,8,288,128]{3,2,1,0:T(8,128)S(1)}) custom-call(bf16[6,512,256]{2,1,0:T(8,128)(2,1)} %x_ref.3, f32[1,256]{1,0:T(1,128)} %bitcast.10, f32[1,256]{1,0:T(1,128)} %bitcast.13, bf16[256,1024]{1,0:T(8,128)(2,1)} %we_ref.3, f32[9,1024]{1,0:T(8,128)} %dw_ref.3, bf16[1024,256]{1,0:T(8,128)(2,1)} %wp_ref.3), custom_call_target="tpu_custom_call" | custom-call | tf_op jit(solution)/shard_map/bottleneck_middle/pallas_call | solution.py:214
  16.4 0.0 collective-permute-done.1.far_ref
  16.4 0.0 collective-permute-done.near_ref
  16.4 0.0 copy-done
  16.4 0.0 copy-done.1
  16.5 3.4 %bottleneck_edge.1 = (bf16[24,4,16,256]{3,2,1,0:T(8,128)(2,1)S(1)}, bf16[6,4,16,256]{3,2,1,0:T(8,128)(2,1)S(1)}, bf16[8,4,16,256]{3,2,1,0:T(8,128)(2,1)S(1)}) custom-call(bf16[6,512,256]{2,1,0:T(8,128)(2,1)S(1)} %copy-done, bf16[1,512,256]{2,1,0:T(8,128)(2,1)S(1)} %collective-permute-done.near_ref, bf16[1,512,256]{2,1,0:T(8,128)(2,1)S(1)} %collective-permute-done.1.far_ref, ...), custom_call_target="tpu_custom_call" | custom-call | tf_op jit(solution)/shard_map/bottleneck_edge/pallas_call | solution.py:233
  19.9 0.0 copy-start.3
  19.9 0.0 copy-start.4
  19.9 0.0 copy-start.5
  19.9 0.0 copy-start.6
  19.9 0.0 copy-start.10
  19.9 0.0 copy-start.16
  19.9 0.0 copy-start.17
  20.0 0.8 collective-permute-start.3
  20.8 3.3 %collective-permute-start.2 = (bf16[6,4,16,256]{3,2,1,0:T(8,128)(2,1)S(1)}, bf16[6,4,16,256]{3,2,1,0:T(8,128)(2,1)S(1)}, u32[]{:S(2)}, u32[]{:S(2)}) collective-permute-start(bf16[6,4,16,256]{3,2,1,0:T(8,128)(2,1)S(1)} %get-tuple-element.30), channel_id=1, source_target_pairs={{0,1},{1,0},{2,3},{3,2},{4,5},{5,4},{6,7},{7,6},{8,9},{9,8},{10,11... | collective-permute-start | bytes 589832 | tf_op jit(solution)/shard_map/ppermute | solution.py:444
  24.1 8.0 %bottleneck_right.1 = (bf16[24,4,16,256]{3,2,1,0:T(8,128)(2,1)S(1)}, bf16[6,4,16,256]{3,2,1,0:T(8,128)(2,1)S(1)}, bf16[8,4,16,256]{3,2,1,0:T(8,128)(2,1)S(1)}) custom-call(bf16[6,512,256]{2,1,0:T(8,128)(2,1)S(1)} %copy-done, bf16[1,512,256]{2,1,0:T(8,128)(2,1)S(1)} %collective-permute-done.near_ref, bf16[1,512,256]{2,1,0:T(8,128)(2,1)S(1)} %collective-permute-done.1.far_ref, ...), custom_call_target="tpu_custom_call" | custom-call | tf_op jit(solution)/shard_map/bottleneck_right/pallas_call | solution.py:243
  32.1 0.0 collective-permute-done.2.outer_ref
  32.1 0.0 collective-permute-done.3.inner_ref
  32.1 0.7 collective-permute-start.5
  32.8 3.5 %collective-permute-start.4 = (bf16[6,4,16,256]{3,2,1,0:T(8,128)(2,1)S(1)}, bf16[6,4,16,256]{3,2,1,0:T(8,128)(2,1)S(1)}, u32[]{:S(2)}, u32[]{:S(2)}) collective-permute-start(bf16[6,4,16,256]{3,2,1,0:T(8,128)(2,1)S(1)} %get-tuple-element.34), channel_id=1, source_target_pairs={{0,1},{1,0},{2,3},{3,2},{4,5},{5,4},{6,7},{7,6},{8,9},{9,8},{10,11... | collective-permute-start | bytes 589832 | tf_op jit(solution)/shard_map/ppermute | solution.py:450
  36.3 7.1 %block_section.2.refs_7_ = bf16[8,3,4,16,256]{4,3,2,1,0:T(8,128)(2,1)S(1)} custom-call(bf16[24,4,16,256]{3,2,1,0:T(8,128)(2,1)S(1)} %get-tuple-element.36.own_ref, bf16[6,4,16,256]{3,2,1,0:T(8,128)(2,1)S(1)} %collective-permute-done.2.outer_ref, bf16[8,4,16,256]{3,2,1,0:T(8,128)(2,1)S(1)} %collective-permute-done.3.inner_ref, f32[1,256]{1,0:T(1,128)S(1)} %bitcast.16, ...), custom_call_target="tpu_custom_call" | custom-call | tf_op jit(solution)/shard_map/block_section/pallas_call | solution.py:409
  43.4 0.0 collective-permute-done.4.outer_ref
  43.4 0.0 collective-permute-done.5.inner_ref
  43.5 7.4 %block_section.3 = bf16[8,3,8,16,256]{4,3,2,1,0:T(8,128)(2,1)S(1)} custom-call(bf16[24,4,16,256]{3,2,1,0:T(8,128)(2,1)S(1)} %get-tuple-element.29.own_ref, bf16[6,4,16,256]{3,2,1,0:T(8,128)(2,1)S(1)} %collective-permute-done.4.outer_ref, bf16[8,4,16,256]{3,2,1,0:T(8,128)(2,1)S(1)} %collective-permute-done.5.inner_ref, f32[1,256]{1,0:T(1,128)S(1)} %bitcast.17, ...), custom_call_target="tpu_custom_call" | custom-call | tf_op jit(solution)/shard_map/block_section/pallas_call | solution.py:409
  50.8 0.0 copy-start.8
  50.8 0.0 copy-start.9
  50.8 0.0 copy-start.11
  50.9 0.0 copy-start.12
  50.9 0.0 copy-start.13
  50.9 0.0 copy-start.18
  50.9 0.0 copy-start.19
  50.9 25.1 %all_to_all.10.x_ref = bf16[8,3,8,16,256]{4,3,2,1,0:T(8,128)(2,1)S(1)} all-to-all(bf16[8,3,8,16,256]{4,3,2,1,0:T(8,128)(2,1)S(1)} %block_section.3), channel_id=1, replica_groups={{0,16,32,48,64,80,96,112},{8,24,40,56,72,88,104,120},{1,17,33,49,65,81,..., dimensions={0} | all-to-all | bytes 3145728 | tf_op jit(solution)/shard_map/all_to_all | solution.py:462
  76.0 0.0 copy-done.12
  76.1 0.0 copy-done.13
  76.1 0.0 copy-done.18
  76.1 0.0 copy-done.19
  76.1 15.5 %grid_section.1 = bf16[64,3,16,256]{3,2,1,0:T(8,128)(2,1)S(1)} custom-call(bf16[8,3,8,16,256]{4,3,2,1,0:T(8,128)(2,1)S(1)} %all_to_all.10.x_ref, f32[1,256]{1,0:T(1,128)S(1)} %bitcast.20, bf16[256,768]{1,0:T(8,128)(2,1)S(1)} %copy-done.11, bf16[256,256]{1,0:T(8,128)(2,1)S(1)} %copy-done.13, f32[8,64,64]{2,1,0:T(8,128)S(1)} %copy-done.12, ...), custom_call_target="tpu_custom_call" | custom-call | tf_op jit(solution)/shard_map/grid_section/pallas_call | solution.py:418
  91.6 27.7 %all_to_all.11 = bf16[64,3,16,256]{3,2,1,0:T(8,128)(2,1)S(1)} all-to-all(bf16[64,3,16,256]{3,2,1,0:T(8,128)(2,1)S(1)} %grid_section.1), channel_id=1, replica_groups={{0,1,2,3,4,5,6,7,16,17,18,19,20,21,22,23,32,33,34,35,36,37,38,39,48,49,..., dimensions={0} | all-to-all | bytes 3145728 | tf_op jit(solution)/shard_map/all_to_all | solution.py:464
  119.3 1.2 %copy.21 = bf16[2,3,8,4,16,256]{5,4,3,2,1,0:T(8,128)(2,1)} copy(bf16[2,3,8,4,16,256]{5,4,3,1,0,2:T(8,128)(2,1)S(1)} %bitcast.22) | data formatting | bytes 3145728 | tf_op jit(solution)/shard_map/transpose | solution.py:465
  (14 shorter events, 0.0 us)
Async XLA Ops:
  1.1 15.4 %copy-start = (bf16[6,512,256]{2,1,0:T(8,128)(2,1)S(1)}, bf16[6,512,256]{2,1,0:T(8,128)(2,1)}, u32[]{:S(2)}) copy-start(bf16[6,512,256]{2,1,0:T(8,128)(2,1)} %x_ref.3) | copy-start | bytes 4718596
  1.1 15.4 %copy-start.1 = (bf16[256,1024]{1,0:T(8,128)(2,1)S(1)}, bf16[256,1024]{1,0:T(8,128)(2,1)}, u32[]{:S(2)}) copy-start(bf16[256,1024]{1,0:T(8,128)(2,1)} %we_ref.3) | copy-start | bytes 1572868
  1.1 15.4 %copy-start.2 = (bf16[1024,256]{1,0:T(8,128)(2,1)S(1)}, bf16[1024,256]{1,0:T(8,128)(2,1)}, u32[]{:S(2)}) copy-start(bf16[1024,256]{1,0:T(8,128)(2,1)} %wp_ref.3) | copy-start | bytes 1572868
  1.1 15.4 %copy-start.7 = (f32[9,1024]{1,0:T(8,128)S(1)}, f32[9,1024]{1,0:T(8,128)}, u32[]{:S(2)}) copy-start(f32[9,1024]{1,0:T(8,128)} %dw_ref.3) | copy-start | bytes 110596
  1.1 15.4 %copy-start.14 = (f32[256]{0:T(256)S(1)}, f32[256]{0:T(256)}, u32[]{:S(2)}) copy-start(f32[256]{0:T(256)} %param.21) | copy-start | bytes 3076
  1.1 15.4 %copy-start.15 = (f32[256]{0:T(256)S(1)}, f32[256]{0:T(256)}, u32[]{:S(2)}) copy-start(f32[256]{0:T(256)} %param.22) | copy-start | bytes 3076
  1.1 15.3 %collective-permute-start.1 = (bf16[1,512,256]{2,1,0:T(8,128)(2,1)S(1)}, bf16[1,512,256]{2,1,0:T(8,128)(2,1)S(1)}, u32[]{:S(2)}, u32[]{:S(2)}) collective-permute-start(bf16[1,512,256]{2,1,0:T(8,128)(2,1)S(1)} %get-tuple-element.39), channel_id=1, source_target_pairs={{0,127},{1,2},{2,1},{3,4},{4,3},{5,6},{6,5},{7,8},{8,7},{9,10},{10... | collective-permute-start | bytes 786440 | tf_op jit(solution)/shard_map/ppermute | solution.py:437
  9.4 7.0 %collective-permute-start = (bf16[1,512,256]{2,1,0:T(8,128)(2,1)S(1)}, bf16[1,512,256]{2,1,0:T(8,128)(2,1)S(1)}, u32[]{:S(2)}, u32[]{:S(2)}) collective-permute-start(bf16[1,512,256]{2,1,0:T(8,128)(2,1)S(1)} %get-tuple-element.40), channel_id=1, source_target_pairs={{0,1},{1,0},{2,3},{3,2},{4,5},{5,4},{6,7},{7,6},{8,9},{9,8},{10,11... | collective-permute-start | bytes 786440 | tf_op jit(solution)/shard_map/ppermute | solution.py:436
  19.9 16.4 %copy-start.3 = (bf16[256,1024]{1,0:T(8,128)(2,1)S(1)}, bf16[256,1024]{1,0:T(8,128)(2,1)}, u32[]{:S(2)}) copy-start(bf16[256,1024]{1,0:T(8,128)(2,1)} %refs_5_.4) | copy-start | bytes 1572868
  19.9 16.4 %copy-start.4 = (bf16[1024,256]{1,0:T(8,128)(2,1)S(1)}, bf16[1024,256]{1,0:T(8,128)(2,1)}, u32[]{:S(2)}) copy-start(bf16[1024,256]{1,0:T(8,128)(2,1)} %refs_6_.4) | copy-start | bytes 1572868
  19.9 16.4 %copy-start.5 = (bf16[256,768]{1,0:T(8,128)(2,1)S(1)}, bf16[256,768]{1,0:T(8,128)(2,1)}, u32[]{:S(2)}) copy-start(bf16[256,768]{1,0:T(8,128)(2,1)} %refs_1_.4) | copy-start | bytes 1179652
  19.9 16.4 %copy-start.6 = (f32[8,64,64]{2,1,0:T(8,128)S(1)}, f32[8,64,64]{2,1,0:T(8,128)}, u32[]{:S(2)}) copy-start(f32[8,64,64]{2,1,0:T(8,128)} %refs_3_.4) | copy-start | bytes 393220
  19.9 16.4 %copy-start.10 = (bf16[256,256]{1,0:T(8,128)(2,1)S(1)}, bf16[256,256]{1,0:T(8,128)(2,1)}, u32[]{:S(2)}) copy-start(bf16[256,256]{1,0:T(8,128)(2,1)} %refs_2_.4) | copy-start | bytes 393220
  19.9 16.4 %copy-start.16 = (f32[256]{0:T(256)S(1)}, f32[256]{0:T(256)}, u32[]{:S(2)}) copy-start(f32[256]{0:T(256)} %param.26) | copy-start | bytes 3076
  19.9 16.4 %copy-start.17 = (f32[256]{0:T(256)S(1)}, f32[256]{0:T(256)}, u32[]{:S(2)}) copy-start(f32[256]{0:T(256)} %param.30) | copy-start | bytes 3076
  20.0 12.1 %collective-permute-start.3 = (bf16[8,4,16,256]{3,2,1,0:T(8,128)(2,1)S(1)}, bf16[8,4,16,256]{3,2,1,0:T(8,128)(2,1)S(1)}, u32[]{:S(2)}, u32[]{:S(2)}) collective-permute-start(bf16[8,4,16,256]{3,2,1,0:T(8,128)(2,1)S(1)} %get-tuple-element.31), channel_id=1, source_target_pairs={{0,0},{1,2},{2,1},{3,3},{4,4},{5,6},{6,5},{7,7},{8,8},{9,10},{10,9... | collective-permute-start | bytes 786440 | tf_op jit(solution)/shard_map/ppermute | solution.py:445
  20.8 11.3 %collective-permute-start.2 = (bf16[6,4,16,256]{3,2,1,0:T(8,128)(2,1)S(1)}, bf16[6,4,16,256]{3,2,1,0:T(8,128)(2,1)S(1)}, u32[]{:S(2)}, u32[]{:S(2)}) collective-permute-start(bf16[6,4,16,256]{3,2,1,0:T(8,128)(2,1)S(1)} %get-tuple-element.30), channel_id=1, source_target_pairs={{0,1},{1,0},{2,3},{3,2},{4,5},{5,4},{6,7},{7,6},{8,9},{9,8},{10,11... | collective-permute-start | bytes 589832 | tf_op jit(solution)/shard_map/ppermute | solution.py:444
  32.1 11.3 %collective-permute-start.5 = (bf16[8,4,16,256]{3,2,1,0:T(8,128)(2,1)S(1)}, bf16[8,4,16,256]{3,2,1,0:T(8,128)(2,1)S(1)}, u32[]{:S(2)}, u32[]{:S(2)}) collective-permute-start(bf16[8,4,16,256]{3,2,1,0:T(8,128)(2,1)S(1)} %get-tuple-element.35), channel_id=1, source_target_pairs={{0,0},{1,2},{2,1},{3,3},{4,4},{5,6},{6,5},{7,7},{8,8},{9,10},{10,9... | collective-permute-start | bytes 786440 | tf_op jit(solution)/shard_map/ppermute | solution.py:451
  32.8 10.7 %collective-permute-start.4 = (bf16[6,4,16,256]{3,2,1,0:T(8,128)(2,1)S(1)}, bf16[6,4,16,256]{3,2,1,0:T(8,128)(2,1)S(1)}, u32[]{:S(2)}, u32[]{:S(2)}) collective-permute-start(bf16[6,4,16,256]{3,2,1,0:T(8,128)(2,1)S(1)} %get-tuple-element.34), channel_id=1, source_target_pairs={{0,1},{1,0},{2,3},{3,2},{4,5},{5,4},{6,7},{7,6},{8,9},{9,8},{10,11... | collective-permute-start | bytes 589832 | tf_op jit(solution)/shard_map/ppermute | solution.py:450
  50.8 25.2 %copy-start.8 = (bf16[256,1024]{1,0:T(8,128)(2,1)S(1)}, bf16[256,1024]{1,0:T(8,128)(2,1)}, u32[]{:S(2)}) copy-start(bf16[256,1024]{1,0:T(8,128)(2,1)} %refs_5_.5) | copy-start | bytes 1572868
  50.8 25.2 %copy-start.9 = (bf16[1024,256]{1,0:T(8,128)(2,1)S(1)}, bf16[1024,256]{1,0:T(8,128)(2,1)}, u32[]{:S(2)}) copy-start(bf16[1024,256]{1,0:T(8,128)(2,1)} %refs_6_.5) | copy-start | bytes 1572868
  50.8 25.2 %copy-start.11 = (bf16[256,768]{1,0:T(8,128)(2,1)S(1)}, bf16[256,768]{1,0:T(8,128)(2,1)}, u32[]{:S(2)}) copy-start(bf16[256,768]{1,0:T(8,128)(2,1)} %refs_1_.5) | copy-start | bytes 1179652
  50.9 25.2 %copy-start.12 = (f32[8,64,64]{2,1,0:T(8,128)S(1)}, f32[8,64,64]{2,1,0:T(8,128)}, u32[]{:S(2)}) copy-start(f32[8,64,64]{2,1,0:T(8,128)} %refs_3_.5) | copy-start | bytes 393220
  50.9 25.2 %copy-start.13 = (bf16[256,256]{1,0:T(8,128)(2,1)S(1)}, bf16[256,256]{1,0:T(8,128)(2,1)}, u32[]{:S(2)}) copy-start(bf16[256,256]{1,0:T(8,128)(2,1)} %refs_2_.5) | copy-start | bytes 393220
  50.9 25.2 %copy-start.18 = (f32[256]{0:T(256)S(1)}, f32[256]{0:T(256)}, u32[]{:S(2)}) copy-start(f32[256]{0:T(256)} %param.33) | copy-start | bytes 3076
  50.9 25.2 %copy-start.19 = (f32[256]{0:T(256)S(1)}, f32[256]{0:T(256)}, u32[]{:S(2)}) copy-start(f32[256]{0:T(256)} %param.37) | copy-start | bytes 3076

commit v8 on v7

--- a/solution.py
+++ b/solution.py
@@ -58,7 +58,7 @@
     normed = (values.astype(F32) * scale + shift).astype(BF16)
     for nb in range(4):
         flat = jnp.dot(normed, we_ref[:, nb * 256 : (nb + 1) * 256], preferred_element_type=F32)
-        wide = twice_gelu(flat)
+        wide = twice_gelu_short(flat).astype(F32)
         if factor is not None:
             wide = wide * factor
         for part in range(2):

time: 121 us -> 119 us (0.983)
  Pallas kernels: 48.2 us -> 46.8 us
where the time goes in v8:
time: 119 us; the launch traced here: 118 us
  blocking collectives  52.1 us (44%)
  Pallas kernels  46.8 us (39%)
  starting transfers between devices  16.6 us (14%)
  local copies, waits for them, and re-layouts  1.37 us (1%)
    all_to_all x1, blocking collectives, body(): lax.all_to_all(back, both, 0, 0, axis_index_groups=CORE_ALL, tiled=True)  27 us
    all_to_all x1, blocking collectives, body(): lax.all_to_all(sent, 'rows', 0, 0, axis_index_groups=CORE_ROWS, tiled=True)  25.1 us
    pallas_call x1, Pallas kernels, grid_section(): pl.pallas_call(grid_kernel, out_shape=jax.ShapeDtypeStruct((64, 3, 16, 25...  15.5 us
    pallas_call x2, Pallas kernels, block_section(): pl.pallas_call(functools.partial(block_kernel, half), out_shape=jax.Shape...  14.4 us
    ppermute x1, starting transfers between devices, body(): far = lax.ppermute(jnp.where(even, first, last), both, STRIP_FAR)  8.28 us
    pallas_call x1, Pallas kernels, bottleneck_right(): pl.pallas_call(right_kernel, out_shape=[pieces(24), pieces(6), pieces(8)]...  7.43 us
    pallas_call x1, Pallas kernels, bottleneck_middle(): pl.pallas_call(middle_kernel, out_shape=[pieces(16), jax.ShapeDtypeStruct...  6.59 us
    ppermute x1, starting transfers between devices, body(): outer_r = lax.ppermute(outer_r, 'cols', Y_OUTER)  3.53 us
  transfers between devices with their start and end apart: 6, of which 0 were waited for; matrix products, arithmetic and copies ran while one was open for 0% of the time, Pallas kernels for 18%

profile of v8, /device:TPU:0, one launch (start us, length us, event | category | flops | bytes accessed | tf_op | source)
XLA Modules:
  0.0 118.4 jit_solution(8548704234566341031)
XLA Ops:
  0.0 1.1 broadcast_select_fusion
  1.1 0.0 copy-start
  1.1 0.0 copy-start.1
  1.1 0.0 copy-start.2
  1.1 0.0 copy-start.7
  1.1 0.0 copy-start.14
  1.1 0.0 copy-start.15
  1.1 8.3 %collective-permute-start.1 = (bf16[1,512,256]{2,1,0:T(8,128)(2,1)S(1)}, bf16[1,512,256]{2,1,0:T(8,128)(2,1)S(1)}, u32[]{:S(2)}, u32[]{:S(2)}) collective-permute-start(bf16[1,512,256]{2,1,0:T(8,128)(2,1)S(1)} %get-tuple-element.39), channel_id=1, source_target_pairs={{0,127},{1,2},{2,1},{3,4},{4,3},{5,6},{6,5},{7,8},{8,7},{9,10},{10... | collective-permute-start | bytes 786440 | tf_op jit(solution)/shard_map/ppermute | solution.py:437
  9.4 0.0 collective-permute-start
  9.4 6.6 %bottleneck_middle.1 = (bf16[16,4,16,256]{3,2,1,0:T(8,128)(2,1)S(1)}, f32[6,8,288,128]{3,2,1,0:T(8,128)S(1)}) custom-call(bf16[6,512,256]{2,1,0:T(8,128)(2,1)} %x_ref.3, f32[1,256]{1,0:T(1,128)} %bitcast.10, f32[1,256]{1,0:T(1,128)} %bitcast.13, bf16[256,1024]{1,0:T(8,128)(2,1)} %we_ref.3, f32[9,1024]{1,0:T(8,128)} %dw_ref.3, bf16[1024,256]{1,0:T(8,128)(2,1)} %wp_ref.3), custom_call_target="tpu_custom_call" | custom-call | tf_op jit(solution)/shard_map/bottleneck_middle/pallas_call | solution.py:214
  16.0 0.0 collective-permute-done.1.far_ref
  16.0 0.0 collective-permute-done.near_ref
  16.1 0.0 copy-done
  16.1 2.9 %bottleneck_edge.1 = (bf16[24,4,16,256]{3,2,1,0:T(8,128)(2,1)S(1)}, bf16[6,4,16,256]{3,2,1,0:T(8,128)(2,1)S(1)}, bf16[8,4,16,256]{3,2,1,0:T(8,128)(2,1)S(1)}) custom-call(bf16[6,512,256]{2,1,0:T(8,128)(2,1)S(1)} %copy-done, bf16[1,512,256]{2,1,0:T(8,128)(2,1)S(1)} %collective-permute-done.near_ref, bf16[1,512,256]{2,1,0:T(8,128)(2,1)S(1)} %collective-permute-done.1.far_ref, ...), custom_call_target="tpu_custom_call" | custom-call | tf_op jit(solution)/shard_map/bottleneck_edge/pallas_call | solution.py:233
  19.0 0.0 copy-start.3
  19.0 0.0 copy-start.4
  19.0 0.0 copy-start.5
  19.0 0.0 copy-start.6
  19.0 0.0 copy-start.10
  19.0 0.0 copy-start.16
  19.0 0.0 copy-start.17
  19.1 0.8 collective-permute-start.3
  19.9 3.3 %collective-permute-start.2 = (bf16[6,4,16,256]{3,2,1,0:T(8,128)(2,1)S(1)}, bf16[6,4,16,256]{3,2,1,0:T(8,128)(2,1)S(1)}, u32[]{:S(2)}, u32[]{:S(2)}) collective-permute-start(bf16[6,4,16,256]{3,2,1,0:T(8,128)(2,1)S(1)} %get-tuple-element.30), channel_id=1, source_target_pairs={{0,1},{1,0},{2,3},{3,2},{4,5},{5,4},{6,7},{7,6},{8,9},{9,8},{10,11... | collective-permute-start | bytes 589832 | tf_op jit(solution)/shard_map/ppermute | solution.py:444
  23.2 7.4 %bottleneck_right.1 = (bf16[24,4,16,256]{3,2,1,0:T(8,128)(2,1)S(1)}, bf16[6,4,16,256]{3,2,1,0:T(8,128)(2,1)S(1)}, bf16[8,4,16,256]{3,2,1,0:T(8,128)(2,1)S(1)}) custom-call(bf16[6,512,256]{2,1,0:T(8,128)(2,1)S(1)} %copy-done, bf16[1,512,256]{2,1,0:T(8,128)(2,1)S(1)} %collective-permute-done.near_ref, bf16[1,512,256]{2,1,0:T(8,128)(2,1)S(1)} %collective-permute-done.1.far_ref, ...), custom_call_target="tpu_custom_call" | custom-call | tf_op jit(solution)/shard_map/bottleneck_right/pallas_call | solution.py:243
  30.7 0.0 collective-permute-done.2.outer_ref
  30.7 0.0 collective-permute-done.3.inner_ref
  30.7 0.7 collective-permute-start.5
  31.4 3.5 %collective-permute-start.4 = (bf16[6,4,16,256]{3,2,1,0:T(8,128)(2,1)S(1)}, bf16[6,4,16,256]{3,2,1,0:T(8,128)(2,1)S(1)}, u32[]{:S(2)}, u32[]{:S(2)}) collective-permute-start(bf16[6,4,16,256]{3,2,1,0:T(8,128)(2,1)S(1)} %get-tuple-element.34), channel_id=1, source_target_pairs={{0,1},{1,0},{2,3},{3,2},{4,5},{5,4},{6,7},{7,6},{8,9},{9,8},{10,11... | collective-permute-start | bytes 589832 | tf_op jit(solution)/shard_map/ppermute | solution.py:450
  34.9 0.0 copy-done.3
  34.9 0.0 copy-done.10
  34.9 0.0 copy-done.16
  34.9 0.0 copy-done.17
  34.9 7.1 %block_section.2.refs_7_ = bf16[8,3,4,16,256]{4,3,2,1,0:T(8,128)(2,1)S(1)} custom-call(bf16[24,4,16,256]{3,2,1,0:T(8,128)(2,1)S(1)} %get-tuple-element.36.own_ref, bf16[6,4,16,256]{3,2,1,0:T(8,128)(2,1)S(1)} %collective-permute-done.2.outer_ref, bf16[8,4,16,256]{3,2,1,0:T(8,128)(2,1)S(1)} %collective-permute-done.3.inner_ref, f32[1,256]{1,0:T(1,128)S(1)} %bitcast.16, ...), custom_call_target="tpu_custom_call" | custom-call | tf_op jit(solution)/shard_map/block_section/pallas_call | solution.py:409
  42.0 0.0 collective-permute-done.4.outer_ref
  42.0 0.0 collective-permute-done.5.inner_ref
  42.0 7.4 %block_section.3 = bf16[8,3,8,16,256]{4,3,2,1,0:T(8,128)(2,1)S(1)} custom-call(bf16[24,4,16,256]{3,2,1,0:T(8,128)(2,1)S(1)} %get-tuple-element.29.own_ref, bf16[6,4,16,256]{3,2,1,0:T(8,128)(2,1)S(1)} %collective-permute-done.4.outer_ref, bf16[8,4,16,256]{3,2,1,0:T(8,128)(2,1)S(1)} %collective-permute-done.5.inner_ref, f32[1,256]{1,0:T(1,128)S(1)} %bitcast.17, ...), custom_call_target="tpu_custom_call" | custom-call | tf_op jit(solution)/shard_map/block_section/pallas_call | solution.py:409
  49.4 0.0 copy-start.8
  49.4 0.0 copy-start.9
  49.4 0.0 copy-start.11
  49.5 0.0 copy-start.12
  49.5 0.0 copy-start.13
  49.5 0.0 copy-start.18
  49.5 0.0 copy-start.19
  49.5 25.1 %all_to_all.10.x_ref = bf16[8,3,8,16,256]{4,3,2,1,0:T(8,128)(2,1)S(1)} all-to-all(bf16[8,3,8,16,256]{4,3,2,1,0:T(8,128)(2,1)S(1)} %block_section.3), channel_id=1, replica_groups={{0,16,32,48,64,80,96,112},{8,24,40,56,72,88,104,120},{1,17,33,49,65,81,..., dimensions={0} | all-to-all | bytes 3145728 | tf_op jit(solution)/shard_map/all_to_all | solution.py:462
  74.6 0.0 copy-done.9
  74.7 15.5 %grid_section.1 = bf16[64,3,16,256]{3,2,1,0:T(8,128)(2,1)S(1)} custom-call(bf16[8,3,8,16,256]{4,3,2,1,0:T(8,128)(2,1)S(1)} %all_to_all.10.x_ref, f32[1,256]{1,0:T(1,128)S(1)} %bitcast.20, bf16[256,768]{1,0:T(8,128)(2,1)S(1)} %copy-done.11, bf16[256,256]{1,0:T(8,128)(2,1)S(1)} %copy-done.13, f32[8,64,64]{2,1,0:T(8,128)S(1)} %copy-done.12, ...), custom_call_target="tpu_custom_call" | custom-call | tf_op jit(solution)/shard_map/grid_section/pallas_call | solution.py:418
  90.1 27.0 %all_to_all.11 = bf16[64,3,16,256]{3,2,1,0:T(8,128)(2,1)S(1)} all-to-all(bf16[64,3,16,256]{3,2,1,0:T(8,128)(2,1)S(1)} %grid_section.1), channel_id=1, replica_groups={{0,1,2,3,4,5,6,7,16,17,18,19,20,21,22,23,32,33,34,35,36,37,38,39,48,49,..., dimensions={0} | all-to-all | bytes 3145728 | tf_op jit(solution)/shard_map/all_to_all | solution.py:464
  117.2 1.2 %copy.21 = bf16[2,3,8,4,16,256]{5,4,3,2,1,0:T(8,128)(2,1)} copy(bf16[2,3,8,4,16,256]{5,4,3,1,0,2:T(8,128)(2,1)S(1)} %bitcast.22) | data formatting | bytes 3145728 | tf_op jit(solution)/shard_map/transpose | solution.py:465
  (14 shorter events, 0.0 us)
Async XLA Ops:
  1.1 15.0 %copy-start = (bf16[6,512,256]{2,1,0:T(8,128)(2,1)S(1)}, bf16[6,512,256]{2,1,0:T(8,128)(2,1)}, u32[]{:S(2)}) copy-start(bf16[6,512,256]{2,1,0:T(8,128)(2,1)} %x_ref.3) | copy-start | bytes 4718596
  1.1 15.0 %copy-start.1 = (bf16[256,1024]{1,0:T(8,128)(2,1)S(1)}, bf16[256,1024]{1,0:T(8,128)(2,1)}, u32[]{:S(2)}) copy-start(bf16[256,1024]{1,0:T(8,128)(2,1)} %we_ref.3) | copy-start | bytes 1572868
  1.1 15.0 %copy-start.2 = (bf16[1024,256]{1,0:T(8,128)(2,1)S(1)}, bf16[1024,256]{1,0:T(8,128)(2,1)}, u32[]{:S(2)}) copy-start(bf16[1024,256]{1,0:T(8,128)(2,1)} %wp_ref.3) | copy-start | bytes 1572868
  1.1 15.0 %copy-start.7 = (f32[9,1024]{1,0:T(8,128)S(1)}, f32[9,1024]{1,0:T(8,128)}, u32[]{:S(2)}) copy-start(f32[9,1024]{1,0:T(8,128)} %dw_ref.3) | copy-start | bytes 110596
  1.1 15.0 %copy-start.14 = (f32[256]{0:T(256)S(1)}, f32[256]{0:T(256)}, u32[]{:S(2)}) copy-start(f32[256]{0:T(256)} %param.21) | copy-start | bytes 3076
  1.1 15.0 %copy-start.15 = (f32[256]{0:T(256)S(1)}, f32[256]{0:T(256)}, u32[]{:S(2)}) copy-start(f32[256]{0:T(256)} %param.22) | copy-start | bytes 3076
  1.1 14.9 %collective-permute-start.1 = (bf16[1,512,256]{2,1,0:T(8,128)(2,1)S(1)}, bf16[1,512,256]{2,1,0:T(8,128)(2,1)S(1)}, u32[]{:S(2)}, u32[]{:S(2)}) collective-permute-start(bf16[1,512,256]{2,1,0:T(8,128)(2,1)S(1)} %get-tuple-element.39), channel_id=1, source_target_pairs={{0,127},{1,2},{2,1},{3,4},{4,3},{5,6},{6,5},{7,8},{8,7},{9,10},{10... | collective-permute-start | bytes 786440 | tf_op jit(solution)/shard_map/ppermute | solution.py:437
  9.4 6.6 %collective-permute-start = (bf16[1,512,256]{2,1,0:T(8,128)(2,1)S(1)}, bf16[1,512,256]{2,1,0:T(8,128)(2,1)S(1)}, u32[]{:S(2)}, u32[]{:S(2)}) collective-permute-start(bf16[1,512,256]{2,1,0:T(8,128)(2,1)S(1)} %get-tuple-element.40), channel_id=1, source_target_pairs={{0,1},{1,0},{2,3},{3,2},{4,5},{5,4},{6,7},{7,6},{8,9},{9,8},{10,11... | collective-permute-start | bytes 786440 | tf_op jit(solution)/shard_map/ppermute | solution.py:436
  19.0 15.9 %copy-start.3 = (bf16[256,1024]{1,0:T(8,128)(2,1)S(1)}, bf16[256,1024]{1,0:T(8,128)(2,1)}, u32[]{:S(2)}) copy-start(bf16[256,1024]{1,0:T(8,128)(2,1)} %refs_5_.4) | copy-start | bytes 1572868
  19.0 15.9 %copy-start.4 = (bf16[1024,256]{1,0:T(8,128)(2,1)S(1)}, bf16[1024,256]{1,0:T(8,128)(2,1)}, u32[]{:S(2)}) copy-start(bf16[1024,256]{1,0:T(8,128)(2,1)} %refs_6_.4) | copy-start | bytes 1572868
  19.0 15.9 %copy-start.5 = (bf16[256,768]{1,0:T(8,128)(2,1)S(1)}, bf16[256,768]{1,0:T(8,128)(2,1)}, u32[]{:S(2)}) copy-start(bf16[256,768]{1,0:T(8,128)(2,1)} %refs_1_.4) | copy-start | bytes 1179652
  19.0 15.9 %copy-start.6 = (f32[8,64,64]{2,1,0:T(8,128)S(1)}, f32[8,64,64]{2,1,0:T(8,128)}, u32[]{:S(2)}) copy-start(f32[8,64,64]{2,1,0:T(8,128)} %refs_3_.4) | copy-start | bytes 393220
  19.0 15.9 %copy-start.10 = (bf16[256,256]{1,0:T(8,128)(2,1)S(1)}, bf16[256,256]{1,0:T(8,128)(2,1)}, u32[]{:S(2)}) copy-start(bf16[256,256]{1,0:T(8,128)(2,1)} %refs_2_.4) | copy-start | bytes 393220
  19.0 15.9 %copy-start.16 = (f32[256]{0:T(256)S(1)}, f32[256]{0:T(256)}, u32[]{:S(2)}) copy-start(f32[256]{0:T(256)} %param.26) | copy-start | bytes 3076
  19.0 15.9 %copy-start.17 = (f32[256]{0:T(256)S(1)}, f32[256]{0:T(256)}, u32[]{:S(2)}) copy-start(f32[256]{0:T(256)} %param.30) | copy-start | bytes 3076
  19.1 11.6 %collective-permute-start.3 = (bf16[8,4,16,256]{3,2,1,0:T(8,128)(2,1)S(1)}, bf16[8,4,16,256]{3,2,1,0:T(8,128)(2,1)S(1)}, u32[]{:S(2)}, u32[]{:S(2)}) collective-permute-start(bf16[8,4,16,256]{3,2,1,0:T(8,128)(2,1)S(1)} %get-tuple-element.31), channel_id=1, source_target_pairs={{0,0},{1,2},{2,1},{3,3},{4,4},{5,6},{6,5},{7,7},{8,8},{9,10},{10,9... | collective-permute-start | bytes 786440 | tf_op jit(solution)/shard_map/ppermute | solution.py:445
  19.9 10.8 %collective-permute-start.2 = (bf16[6,4,16,256]{3,2,1,0:T(8,128)(2,1)S(1)}, bf16[6,4,16,256]{3,2,1,0:T(8,128)(2,1)S(1)}, u32[]{:S(2)}, u32[]{:S(2)}) collective-permute-start(bf16[6,4,16,256]{3,2,1,0:T(8,128)(2,1)S(1)} %get-tuple-element.30), channel_id=1, source_target_pairs={{0,1},{1,0},{2,3},{3,2},{4,5},{5,4},{6,7},{7,6},{8,9},{9,8},{10,11... | collective-permute-start | bytes 589832 | tf_op jit(solution)/shard_map/ppermute | solution.py:444
  30.7 11.4 %collective-permute-start.5 = (bf16[8,4,16,256]{3,2,1,0:T(8,128)(2,1)S(1)}, bf16[8,4,16,256]{3,2,1,0:T(8,128)(2,1)S(1)}, u32[]{:S(2)}, u32[]{:S(2)}) collective-permute-start(bf16[8,4,16,256]{3,2,1,0:T(8,128)(2,1)S(1)} %get-tuple-element.35), channel_id=1, source_target_pairs={{0,0},{1,2},{2,1},{3,3},{4,4},{5,6},{6,5},{7,7},{8,8},{9,10},{10,9... | collective-permute-start | bytes 786440 | tf_op jit(solution)/shard_map/ppermute | solution.py:451
  31.4 10.7 %collective-permute-start.4 = (bf16[6,4,16,256]{3,2,1,0:T(8,128)(2,1)S(1)}, bf16[6,4,16,256]{3,2,1,0:T(8,128)(2,1)S(1)}, u32[]{:S(2)}, u32[]{:S(2)}) collective-permute-start(bf16[6,4,16,256]{3,2,1,0:T(8,128)(2,1)S(1)} %get-tuple-element.34), channel_id=1, source_target_pairs={{0,1},{1,0},{2,3},{3,2},{4,5},{5,4},{6,7},{7,6},{8,9},{9,8},{10,11... | collective-permute-start | bytes 589832 | tf_op jit(solution)/shard_map/ppermute | solution.py:450
  49.4 25.2 %copy-start.8 = (bf16[256,1024]{1,0:T(8,128)(2,1)S(1)}, bf16[256,1024]{1,0:T(8,128)(2,1)}, u32[]{:S(2)}) copy-start(bf16[256,1024]{1,0:T(8,128)(2,1)} %refs_5_.5) | copy-start | bytes 1572868
  49.4 25.2 %copy-start.9 = (bf16[1024,256]{1,0:T(8,128)(2,1)S(1)}, bf16[1024,256]{1,0:T(8,128)(2,1)}, u32[]{:S(2)}) copy-start(bf16[1024,256]{1,0:T(8,128)(2,1)} %refs_6_.5) | copy-start | bytes 1572868
  49.4 25.2 %copy-start.11 = (bf16[256,768]{1,0:T(8,128)(2,1)S(1)}, bf16[256,768]{1,0:T(8,128)(2,1)}, u32[]{:S(2)}) copy-start(bf16[256,768]{1,0:T(8,128)(2,1)} %refs_1_.5) | copy-start | bytes 1179652
  49.5 25.2 %copy-start.12 = (f32[8,64,64]{2,1,0:T(8,128)S(1)}, f32[8,64,64]{2,1,0:T(8,128)}, u32[]{:S(2)}) copy-start(f32[8,64,64]{2,1,0:T(8,128)} %refs_3_.5) | copy-start | bytes 393220
  49.5 25.2 %copy-start.13 = (bf16[256,256]{1,0:T(8,128)(2,1)S(1)}, bf16[256,256]{1,0:T(8,128)(2,1)}, u32[]{:S(2)}) copy-start(bf16[256,256]{1,0:T(8,128)(2,1)} %refs_2_.5) | copy-start | bytes 393220
  49.5 25.2 %copy-start.18 = (f32[256]{0:T(256)S(1)}, f32[256]{0:T(256)}, u32[]{:S(2)}) copy-start(f32[256]{0:T(256)} %param.33) | copy-start | bytes 3076
  49.5 25.2 %copy-start.19 = (f32[256]{0:T(256)S(1)}, f32[256]{0:T(256)}, u32[]{:S(2)}) copy-start(f32[256]{0:T(256)} %param.37) | copy-start | bytes 3076
